TPU v7x, 32 devices: a whole 2x2x4 slice. The times are simulated.
32 devices in a mesh: groups: 2 (over x), leaf: 16 (over z, y, core).
Axes of the slice: x: 2, y: 2, z: 4, core: 2. Of those that a mesh axis runs over, the one named last changes fastest.
Arguments:
- queries: bfloat16 [8192, 2560], P(('groups', 'leaf')), parts along dimension 0, may hold values from -5 to 5
- keys: bfloat16 [8192, 512], P(('groups', 'leaf')), parts along dimension 0, may hold values from -5 to 5
- values: bfloat16 [8192, 512], P(('groups', 'leaf')), parts along dimension 0, may hold values from -6 to 6
- saved_out: bfloat16 [8192, 2560], P(('groups', 'leaf')), parts along dimension 0, may hold values from -3 to 3
- grad_out: bfloat16 [8192, 2560], P(('groups', 'leaf')), parts along dimension 0, may hold values from -60 to 60
- parents: int32 [32], P('groups'), parts along dimension 0, may hold values from -1 to 15, as said below
- assignment: int32 [32], P('groups'), parts along dimension 0, may hold values from 0 to 15, each once
- lengths: int32 [32], P('groups'), parts along dimension 0, may hold values from 64 to 256, as said below
Outputs:
- query_grad: bfloat16 [8192, 2560], P(('groups', 'leaf')), parts along dimension 0
- key_grad: bfloat16 [8192, 512], P(('groups', 'leaf')), parts along dimension 0
- value_grad: bfloat16 [8192, 512], P(('groups', 'leaf')), parts along dimension 0
There are 2 independent parts, one for each index of `groups`. A program takes and returns all parts, laid end to end along the dimension named above; each array names one. Nothing has to cross between parts.
Inputs may be any that keep to these rules, and one draw needn't show every extreme that they name: parents[s] is the segment that segment s continues, -1 for segment 0 alone; segments 0 to 1 are the root prompt, each continuing the one before; every chain of ancestors holds at most 5 segments, and some segment's holds exactly that many. lengths[s] counts the live tokens of segment s from its start; the root prompt's segments are full.
All inputs are finite; a program needn't handle non-finite values.
Results may differ from a plain program's by a relative error of at most 0.0052.
Values may be sent and summed in bfloat16 or wider, within the bound.
No kernel may reach another device: no remote copies, remote signals or barrier semaphores. Data moves between devices by JAX's collectives and lax.ppermute only.
A program may use at most 128 MiB of HBM per device.

v0:
```python
import math

import jax
import jax.numpy as jnp
from jax import lax
from jax.sharding import PartitionSpec as P

HQ = 20
HK = 4
DH = 128
ANCESTORS = 5


def pick(table, index):
    hits = index[..., None] == jnp.arange(table.shape[0], dtype=jnp.int32)
    return jnp.sum(jnp.where(hits, table, 0), axis=-1)


def pick_rows(table, index):
    hits = index[:, None] == jnp.arange(table.shape[0], dtype=jnp.int32)[None, :]
    return jnp.sum(jnp.where(hits[:, :, None], table[None, :, :], 0), axis=1)


def tree_tables(parents, assignment, lengths):
    count = parents.shape[0]
    iota = jnp.arange(count, dtype=jnp.int32)
    owner = jnp.sum(jnp.where(assignment[None, :] == iota[:, None], iota[None, :], 0), axis=1)
    links = [iota]
    for step in range(ANCESTORS):
        before = links[-1]
        above = pick(parents, jnp.maximum(before, 0))
        links.append(jnp.where(before >= 0, above, -1))
    stacked = jnp.stack(links)
    depth = jnp.sum((stacked[1:] >= 0).astype(jnp.int32), axis=0)
    steps_up = jnp.arange(ANCESTORS + 1, dtype=jnp.int32)
    slot_ids = jnp.arange(ANCESTORS, dtype=jnp.int32)
    hits = steps_up[:, None, None] == depth[None, None, :] - slot_ids[None, :, None]
    ancestor = jnp.sum(jnp.where(hits, stacked[:, None, :], 0), axis=0).T
    valid = (slot_ids[None, :] < depth[:, None]).astype(jnp.int32)
    ancestor = jnp.where(valid > 0, ancestor, 0)
    holder = pick(owner, ancestor)
    reach = pick(lengths, ancestor)
    return (
        owner,
        pick_rows(holder, assignment),
        pick_rows(valid, assignment),
        pick_rows(reach, assignment),
        pick(lengths, assignment),
        pick(depth, assignment),
    )


def build_mask(block_rows, usable, extent):
    position = jnp.arange(block_rows, dtype=jnp.int32)
    own_part = position[None, :] <= position[:, None]
    far_part = (usable[:, None] > 0) & (position[None, :] < extent[:, None])
    far_part = jnp.broadcast_to(far_part[None], (block_rows, ANCESTORS, block_rows))
    joined = jnp.concatenate([own_part[:, None, :], far_part], axis=1)
    return joined.reshape(block_rows, (ANCESTORS + 1) * block_rows)


def slot_grads(query, key_rows, value_rows, grad_rows, saved_rows, allowed):
    block_rows = query.shape[0]
    key_count = key_rows.shape[0]
    per_group = HQ // HK
    factor = 1.0 / math.sqrt(DH)
    query_heads = query.reshape(block_rows, HK, per_group, DH).transpose(1, 2, 0, 3)
    key_heads = key_rows.reshape(key_count, HK, DH).transpose(1, 0, 2)
    value_heads = value_rows.reshape(key_count, HK, DH).transpose(1, 0, 2)
    grad_heads = grad_rows.reshape(block_rows, HK, per_group, DH).transpose(1, 2, 0, 3)
    saved_heads = saved_rows.reshape(block_rows, HK, per_group, DH).transpose(1, 2, 0, 3)

    def one_group(pieces):
        query_part, key_part, value_part, grad_part, saved_part = pieces
        scores = (
            jnp.einsum("gid,kd->gik", query_part, key_part, preferred_element_type=jnp.float32)
            * factor
        )
        scores = jnp.where(allowed[None], scores, -1e30)
        highest = jnp.max(scores, axis=-1, keepdims=True)
        weights = jnp.exp(scores - highest)
        attention = weights / jnp.sum(weights, axis=-1, keepdims=True)
        attention_half = attention.astype(jnp.bfloat16)
        prob_grad = jnp.einsum(
            "gid,kd->gik", grad_part, value_part, preferred_element_type=jnp.float32
        )
        row_delta = jnp.sum(
            grad_part.astype(jnp.float32) * saved_part.astype(jnp.float32), axis=-1, keepdims=True
        )
        score_grad = (attention * (prob_grad - row_delta)).astype(jnp.bfloat16)
        query_terms = (
            jnp.einsum("gik,kd->gid", score_grad, key_part, preferred_element_type=jnp.float32)
            * factor
        )
        key_terms = (
            jnp.einsum("gik,gid->kd", score_grad, query_part, preferred_element_type=jnp.float32)
            * factor
        )
        value_terms = jnp.einsum(
            "gik,gid->kd", attention_half, grad_part, preferred_element_type=jnp.float32
        )
        return (query_terms, key_terms, value_terms)

    query_terms, key_terms, value_terms = lax.map(
        one_group, (query_heads, key_heads, value_heads, grad_heads, saved_heads)
    )
    query_terms = query_terms.transpose(2, 0, 1, 3).reshape(block_rows, HQ * DH)
    key_terms = key_terms.transpose(1, 0, 2).reshape(key_count, HK * DH)
    value_terms = value_terms.transpose(1, 0, 2).reshape(key_count, HK * DH)
    return (query_terms, key_terms, value_terms)


def fetch(key_parts, value_parts, table):
    picked_keys = key_parts[table]
    picked_values = value_parts[table]
    got_keys, got_values = (
        lax.all_to_all(picked_keys, "leaf", split_axis=0, concat_axis=2, tiled=True),
        lax.all_to_all(picked_values, "leaf", split_axis=0, concat_axis=2, tiled=True),
    )
    return (got_keys[0], got_values[0])


def give_back(key_terms, value_terms, table, valid_table):
    spans, block_rows, columns = key_terms.shape
    devices = table.shape[0]
    part_rows = block_rows // devices
    sent_keys = key_terms.reshape(spans, devices, part_rows, columns)
    sent_values = value_terms.reshape(spans, devices, part_rows, columns)
    got_keys, got_values = (
        lax.all_to_all(sent_keys, "leaf", split_axis=1, concat_axis=1, tiled=True),
        lax.all_to_all(sent_values, "leaf", split_axis=1, concat_axis=1, tiled=True),
    )
    targets = jnp.arange(devices, dtype=jnp.int32)
    routing = (
        (table[None, :, :] == targets[:, None, None]) & (valid_table[None, :, :] > 0)
    ).astype(jnp.float32)
    held_keys = jnp.einsum("tsa,asrw->trw", routing, got_keys, precision=lax.Precision.HIGHEST)
    held_values = jnp.einsum("tsa,asrw->trw", routing, got_values, precision=lax.Precision.HIGHEST)
    back_keys, back_values = (
        lax.all_to_all(held_keys, "leaf", split_axis=0, concat_axis=1, tiled=True),
        lax.all_to_all(held_values, "leaf", split_axis=0, concat_axis=1, tiled=True),
    )
    return (back_keys.reshape(block_rows, columns), back_values.reshape(block_rows, columns))


def local(queries, keys, values, saved_out, grad_out, parents, assignment, lengths):
    devices = lax.axis_size("leaf")
    device_index = lax.axis_index("leaf")
    block_rows = queries.shape[0]
    part_rows = block_rows // devices
    columns = keys.shape[1]
    owner, holder, valid, reach, own_length, own_depth = tree_tables(parents, assignment, lengths)
    mine = jnp.arange(devices, dtype=jnp.int32) == device_index
    my_valid = jnp.sum(jnp.where(mine[:, None], valid, 0), axis=0)
    my_reach = jnp.sum(jnp.where(mine[:, None], reach, 0), axis=0)
    my_length = jnp.sum(jnp.where(mine, own_length, 0))
    key_parts, value_parts = (
        lax.all_to_all(keys, "leaf", split_axis=0, concat_axis=0, tiled=True),
        lax.all_to_all(values, "leaf", split_axis=0, concat_axis=0, tiled=True),
    )
    key_parts = key_parts.reshape(devices, part_rows, columns)
    value_parts = value_parts.reshape(devices, part_rows, columns)
    ancestor_keys, ancestor_values = fetch(key_parts, value_parts, holder)
    position = jnp.arange(block_rows, dtype=jnp.int32)
    masked_grad = jnp.where((position < my_length)[:, None], grad_out, jnp.zeros_like(grad_out))
    key_rows = jnp.concatenate([keys[None], ancestor_keys], axis=0).reshape(-1, columns)
    value_rows = jnp.concatenate([values[None], ancestor_values], axis=0).reshape(-1, columns)
    allowed = build_mask(block_rows, my_valid, my_reach)
    query_terms, key_terms, value_terms = slot_grads(
        queries, key_rows, value_rows, masked_grad, saved_out, allowed
    )
    key_terms = key_terms.reshape(ANCESTORS + 1, block_rows, columns)
    value_terms = value_terms.reshape(ANCESTORS + 1, block_rows, columns)
    back_key, back_value = give_back(key_terms[1:], value_terms[1:], holder, valid)
    query_grad = query_terms.astype(jnp.bfloat16)
    key_grad = (key_terms[0] + back_key).astype(jnp.bfloat16)
    value_grad = (value_terms[0] + back_value).astype(jnp.bfloat16)
    return (query_grad, key_grad, value_grad)


def solution(mesh):
    in_specs = (
        P(("groups", "leaf"), None),
        P(("groups", "leaf"), None),
        P(("groups", "leaf"), None),
        P(("groups", "leaf"), None),
        P(("groups", "leaf"), None),
        P("groups"),
        P("groups"),
        P("groups"),
    )
    out_specs = (
        P(("groups", "leaf"), None),
        P(("groups", "leaf"), None),
        P(("groups", "leaf"), None),
    )
    return jax.shard_map(local, mesh=mesh, in_specs=in_specs, out_specs=out_specs, check_vma=False)
```

profile of v0, /device:TPU:0, one launch (start us, length us, event | category | flops | bytes accessed | tf_op | source)
XLA Modules:
  0.0 401.1 jit_solution(13174018958711605152)
XLA Ops:
  0.6 7.4 %all-to-all-start = ((bf16[16,16,512]{2,1,0:T(8,128)(2,1)}), bf16[16,16,512]{2,1,0:T(8,128)(2,1)S(1)}, u32[]{:S(2)}, u32[]{:S(2)}) async-start(bf16[16,16,512]{2,1,0:T(8,128)(2,1)} %bitcast.196), calls=%async_computation | async-start | bytes 524288 | tf_op jit(solution)/shard_map/all_to_all | solution.py:158
  25.6 6.1 %all-to-all-done.2 = bf16[16,16,512]{2,1,0:T(8,128)(2,1)S(1)} async-done(((bf16[16,16,512]{2,1,0:T(8,128)(2,1)}), bf16[16,16,512]{2,1,0:T(8,128)(2,1)S(1)}, u32[]{:S(2)}, u32[]{:S(2)}) %all-to-all-start.2) | async-done | bytes 262176 | tf_op jit(solution)/shard_map/all_to_all | solution.py:159
  37.2 25.5 %all-to-all-done.1 = bf16[16,5,16,512]{3,2,1,0:T(8,128)(2,1)S(1)} async-done(((bf16[16,5,16,512]{3,2,1,0:T(8,128)(2,1)}), bf16[16,5,16,512]{3,2,1,0:T(8,128)(2,1)S(1)}, u32[]{:S(2)}, u32[]{:S(2)}) %all-to-all-start.1) | async-done | bytes 1310752 | tf_op jit(solution)/shard_map/all_to_all | solution.py:117
  62.7 8.0 %all-to-all-start.3 = ((bf16[16,5,16,512]{3,2,1,0:T(8,128)(2,1)}), bf16[16,5,16,512]{3,2,1,0:T(8,128)(2,1)}, u32[]{:S(2)}, u32[]{:S(2)}) async-start(bf16[16,5,16,512]{3,2,1,0:T(8,128)(2,1)} %bitcast.33), calls=%async_computation.3 | async-start | bytes 2621440 | tf_op jit(solution)/shard_map/all_to_all | solution.py:118
  88.6 9.6 %all-to-all-done.3 = bf16[16,5,16,512]{3,2,1,0:T(8,128)(2,1)} async-done(((bf16[16,5,16,512]{3,2,1,0:T(8,128)(2,1)}), bf16[16,5,16,512]{3,2,1,0:T(8,128)(2,1)}, u32[]{:S(2)}, u32[]{:S(2)}) %all-to-all-start.3) | async-done | bytes 1310752 | tf_op jit(solution)/shard_map/all_to_all | solution.py:118
  107.2 110.5 %while.14 = (s32[]{:T(128)}, bf16[4,5,256,128]{2,3,1,0:T(8,128)(2,1)}, f32[4,1536,128]{2,1,0:T(8,128)}, f32[4,1536,128]{2,1,0:T(8,128)}, pred[256,6,256]{0,2,1:T...) while((s32[]{:T(128)}, ...), condition=%wide.region_21.22_spmd, body=%wide.region_17.21_spmd.sunk | while | flops 3046640640 | bytes 38828160 | solution.py:104
  109.5 7.3 %fusion.127 = (f32[5,256]{1,0:T(8,128)S(1)}, f32[5,256,1536]{2,1,0:T(8,128)}) fusion(pred[256,1536]{1,0:T(8,128)(4,1)S(1)} %copy.178, bf16[4,1536,128]{2,1,0:T(8,128)(2,1)} %get-tuple-element.261, s32[]{:T(128)S(6)} %copy.187, bf16[4,5,256,128]{2,3,1,0:T(8,128)(2,1)} %get-tuple-element.260), kind=kOutput, calls=%fused_computation.129.clone.1 | convolution fusion | flops 511182336 | bytes 8984576 | tf_op jit(solution)/shard_map/while/body/eval_jaxpr/sub | solution.py:81
  116.8 5.2 %multiply_convert_fusion.2 = bf16[5,256,1536]{2,1,0:T(8,128)(2,1)S(1)} fusion(f32[5,256]{1,0:T(8,128)S(1)} %fusion.126, f32[5,256,1536]{2,1,0:T(8,128)} %get-tuple-element.231, f32[5,256]{1,0:T(8,128)S(1)} %get-tuple-element.232, bf16[4,1536,128]{2,1,0:T(8,128)(2,1)} %get-tuple-element.263, s32[]{:T(128)S(6)} %copy.187, ...), kind=kOutput, calls=%fused_computation.3.clone.1 | convolution fusion | flops 511180800 | bytes 12528640 | tf_op jit(solution)/shard_map/while/body/eval_jaxpr/gid,kd->gik/dot_general | solution.py:84
  128.2 6.7 %fusion.130 = f32[4,1536,128]{2,1,0:T(8,128)} fusion(f32[4,1536,128]{2,1,0:T(8,128)} %get-tuple-element.247, s32[]{:T(128)S(6)} %copy.187, f32[5,256]{1,0:T(8,128)S(1)} %get-tuple-element.232, pred[256,1536]{1,0:T(8,128)(4,1)S(1)} %copy.178, bf16[4,1536,128]{2,1,0:T(8,128)(2,1)} %get-tuple-element.261, ...), kind=kOutput, calls=%fused_computation.18.clone.1 | convolution fusion | flops 1016466176 | bytes 2235392 | tf_op jit(solution)/shard_map/while/body/eval_jaxpr/gik,gid->kd/dot_general | solution.py:99
  137.1 7.3 %fusion.127 = (f32[5,256]{1,0:T(8,128)S(1)}, f32[5,256,1536]{2,1,0:T(8,128)}) fusion(pred[256,1536]{1,0:T(8,128)(4,1)S(1)} %copy.178, bf16[4,1536,128]{2,1,0:T(8,128)(2,1)} %get-tuple-element.261, s32[]{:T(128)S(6)} %copy.187, bf16[4,5,256,128]{2,3,1,0:T(8,128)(2,1)} %get-tuple-element.260), kind=kOutput, calls=%fused_computation.129.clone.1 | convolution fusion | flops 511182336 | bytes 8984576 | tf_op jit(solution)/shard_map/while/body/eval_jaxpr/sub | solution.py:81
  155.9 6.7 %fusion.130 = f32[4,1536,128]{2,1,0:T(8,128)} fusion(f32[4,1536,128]{2,1,0:T(8,128)} %get-tuple-element.247, s32[]{:T(128)S(6)} %copy.187, f32[5,256]{1,0:T(8,128)S(1)} %get-tuple-element.232, pred[256,1536]{1,0:T(8,128)(4,1)S(1)} %copy.178, bf16[4,1536,128]{2,1,0:T(8,128)(2,1)} %get-tuple-element.261, ...), kind=kOutput, calls=%fused_computation.18.clone.1 | convolution fusion | flops 1016466176 | bytes 2235392 | tf_op jit(solution)/shard_map/while/body/eval_jaxpr/gik,gid->kd/dot_general | solution.py:99
  164.8 7.3 %fusion.127 = (f32[5,256]{1,0:T(8,128)S(1)}, f32[5,256,1536]{2,1,0:T(8,128)}) fusion(pred[256,1536]{1,0:T(8,128)(4,1)S(1)} %copy.178, bf16[4,1536,128]{2,1,0:T(8,128)(2,1)} %get-tuple-element.261, s32[]{:T(128)S(6)} %copy.187, bf16[4,5,256,128]{2,3,1,0:T(8,128)(2,1)} %get-tuple-element.260), kind=kOutput, calls=%fused_computation.129.clone.1 | convolution fusion | flops 511182336 | bytes 8984576 | tf_op jit(solution)/shard_map/while/body/eval_jaxpr/sub | solution.py:81
  183.4 6.7 %fusion.130 = f32[4,1536,128]{2,1,0:T(8,128)} fusion(f32[4,1536,128]{2,1,0:T(8,128)} %get-tuple-element.247, s32[]{:T(128)S(6)} %copy.187, f32[5,256]{1,0:T(8,128)S(1)} %get-tuple-element.232, pred[256,1536]{1,0:T(8,128)(4,1)S(1)} %copy.178, bf16[4,1536,128]{2,1,0:T(8,128)(2,1)} %get-tuple-element.261, ...), kind=kOutput, calls=%fused_computation.18.clone.1 | convolution fusion | flops 1016466176 | bytes 2235392 | tf_op jit(solution)/shard_map/while/body/eval_jaxpr/gik,gid->kd/dot_general | solution.py:99
  192.4 7.3 %fusion.127 = (f32[5,256]{1,0:T(8,128)S(1)}, f32[5,256,1536]{2,1,0:T(8,128)}) fusion(pred[256,1536]{1,0:T(8,128)(4,1)S(1)} %copy.178, bf16[4,1536,128]{2,1,0:T(8,128)(2,1)} %get-tuple-element.261, s32[]{:T(128)S(6)} %copy.187, bf16[4,5,256,128]{2,3,1,0:T(8,128)(2,1)} %get-tuple-element.260), kind=kOutput, calls=%fused_computation.129.clone.1 | convolution fusion | flops 511182336 | bytes 8984576 | tf_op jit(solution)/shard_map/while/body/eval_jaxpr/sub | solution.py:81
  211.1 6.6 %fusion.130 = f32[4,1536,128]{2,1,0:T(8,128)} fusion(f32[4,1536,128]{2,1,0:T(8,128)} %get-tuple-element.247, s32[]{:T(128)S(6)} %copy.187, f32[5,256]{1,0:T(8,128)S(1)} %get-tuple-element.232, pred[256,1536]{1,0:T(8,128)(4,1)S(1)} %copy.178, bf16[4,1536,128]{2,1,0:T(8,128)(2,1)} %get-tuple-element.261, ...), kind=kOutput, calls=%fused_computation.18.clone.1 | convolution fusion | flops 1016466176 | bytes 2235392 | tf_op jit(solution)/shard_map/while/body/eval_jaxpr/gik,gid->kd/dot_general | solution.py:99
  219.6 5.4 %copy.146 = f32[1280,4,128]{2,1,0:T(4,128)S(1)} copy(f32[1280,4,128]{2,0,1:T(8,128)S(1)} %slice.29) | data formatting | bytes 5242880 | tf_op jit(solution)/shard_map/slice | solution.py:174
  230.9 8.0 %all-to-all-start.6 = ((f32[5,16,16,512]{3,2,0,1:T(8,128)}), f32[5,16,16,512]{3,2,0,1:T(8,128)S(1)}, u32[]{:S(2)}, u32[]{:S(2)}) async-start(f32[5,16,16,512]{3,2,0,1:T(8,128)} %copy.147), calls=%async_computation.6 | async-start | bytes 5242880 | tf_op jit(solution)/shard_map/all_to_all | solution.py:131
  240.9 6.5 %copy.141 = f32[1280,4,128]{2,1,0:T(4,128)} copy(f32[1280,4,128]{2,0,1:T(8,128)S(1)} %slice.27) | data formatting | bytes 5242880 | tf_op jit(solution)/shard_map/slice | solution.py:174
  255.2 34.0 %all-to-all-done.6 = f32[5,16,16,512]{3,2,0,1:T(8,128)S(1)} async-done(((f32[5,16,16,512]{3,2,0,1:T(8,128)}), f32[5,16,16,512]{3,2,0,1:T(8,128)S(1)}, u32[]{:S(2)}, u32[]{:S(2)}) %all-to-all-start.6) | async-done | bytes 2621472 | tf_op jit(solution)/shard_map/all_to_all | solution.py:131
  289.2 13.4 %all-to-all-start.4 = ((f32[5,16,16,512]{3,2,0,1:T(8,128)}), f32[5,16,16,512]{3,2,0,1:T(8,128)}, u32[]{:S(2)}, u32[]{:S(2)}) async-start(f32[5,16,16,512]{3,2,0,1:T(8,128)} %copy.142), calls=%async_computation.4 | async-start | bytes 5242880 | tf_op jit(solution)/shard_map/all_to_all | solution.py:130
  306.5 46.3 %all-to-all-done.4 = f32[5,16,16,512]{3,2,0,1:T(8,128)} async-done(((f32[5,16,16,512]{3,2,0,1:T(8,128)}), f32[5,16,16,512]{3,2,0,1:T(8,128)}, u32[]{:S(2)}, u32[]{:S(2)}) %all-to-all-start.4) | async-done | bytes 2621472 | tf_op jit(solution)/shard_map/all_to_all | solution.py:130
  352.9 13.3 %all-to-all-start.7 = ((f32[16,16,512]{2,1,0:T(8,128)}), f32[16,16,512]{2,1,0:T(8,128)S(1)}, u32[]{:S(2)}, u32[]{:S(2)}) async-start(f32[16,16,512]{2,1,0:T(8,128)} %copy.149), calls=%async_computation.7 | async-start | bytes 1048576 | tf_op jit(solution)/shard_map/all_to_all | solution.py:141
  371.9 8.8 %all-to-all-done.7 = f32[16,16,512]{2,1,0:T(8,128)S(1)} async-done(((f32[16,16,512]{2,1,0:T(8,128)}), f32[16,16,512]{2,1,0:T(8,128)S(1)}, u32[]{:S(2)}, u32[]{:S(2)}) %all-to-all-start.7) | async-done | bytes 524320 | tf_op jit(solution)/shard_map/all_to_all | solution.py:141
  388.2 11.1 %all-to-all-done.5 = f32[16,16,512]{2,1,0:T(8,128)S(1)} async-done(((f32[16,16,512]{2,1,0:T(8,128)}), f32[16,16,512]{2,1,0:T(8,128)S(1)}, u32[]{:S(2)}, u32[]{:S(2)}) %all-to-all-start.5) | async-done | bytes 524320 | tf_op jit(solution)/shard_map/all_to_all | solution.py:140
  (130 shorter events, 135.5 us)
Async XLA Ops:
  0.6 17.5 %all-to-all-start = ((bf16[16,16,512]{2,1,0:T(8,128)(2,1)}), bf16[16,16,512]{2,1,0:T(8,128)(2,1)S(1)}, u32[]{:S(2)}, u32[]{:S(2)}) async-start(bf16[16,16,512]{2,1,0:T(8,128)(2,1)} %bitcast.196), calls=%async_computation | async-start | bytes 524288 | tf_op jit(solution)/shard_map/all_to_all | solution.py:158
  18.1 13.5 %all-to-all-start.2 = ((bf16[16,16,512]{2,1,0:T(8,128)(2,1)}), bf16[16,16,512]{2,1,0:T(8,128)(2,1)S(1)}, u32[]{:S(2)}, u32[]{:S(2)}) async-start(bf16[16,16,512]{2,1,0:T(8,128)(2,1)} %bitcast.198), calls=%async_computation.2 | async-start | bytes 524288 | tf_op jit(solution)/shard_map/all_to_all | solution.py:159
  22.9 0.6 copy-start.6
  23.0 54.7 %copy-start.8 = (s32[16,5]{0,1:T(8,128)}, s32[16,5]{0,1:T(8,128)S(1)}, u32[]{:S(2)}) copy-start(s32[16,5]{0,1:T(8,128)S(1)} %get-tuple-element.129) | copy-start | bytes 964
  31.6 31.1 %all-to-all-start.1 = ((bf16[16,5,16,512]{3,2,1,0:T(8,128)(2,1)}), bf16[16,5,16,512]{3,2,1,0:T(8,128)(2,1)S(1)}, u32[]{:S(2)}, u32[]{:S(2)}) async-start(bf16[16,5,16,512]{3,2,1,0:T(8,128)(2,1)} %bitcast.24), calls=%async_computation.1 | async-start | bytes 2621440 | tf_op jit(solution)/shard_map/all_to_all | solution.py:117
  35.3 35.4 %copy-start.2 = (bf16[256,2560]{1,0:T(8,128)(2,1)S(1)}, bf16[256,2560]{1,0:T(8,128)(2,1)}, u32[]{:S(2)}) copy-start(bf16[256,2560]{1,0:T(8,128)(2,1)} %param.10) | copy-start | bytes 3932164
  62.7 8.1 %copy-start = (bf16[16,5,16,512]{3,2,1,0:T(8,128)(2,1)}, bf16[16,5,16,512]{3,2,1,0:T(8,128)(2,1)S(1)}, u32[]{:S(2)}) copy-start(bf16[16,5,16,512]{3,2,1,0:T(8,128)(2,1)S(1)} %all-to-all-done.1) | copy-start | bytes 3932164
  62.7 35.5 %all-to-all-start.3 = ((bf16[16,5,16,512]{3,2,1,0:T(8,128)(2,1)}), bf16[16,5,16,512]{3,2,1,0:T(8,128)(2,1)}, u32[]{:S(2)}, u32[]{:S(2)}) async-start(bf16[16,5,16,512]{3,2,1,0:T(8,128)(2,1)} %bitcast.33), calls=%async_computation.3 | async-start | bytes 2621440 | tf_op jit(solution)/shard_map/all_to_all | solution.py:118
  73.9 7.0 %copy-start.1 = (bf16[16,5,16,512]{3,2,1,0:T(8,128)(2,1)S(1)}, bf16[16,5,16,512]{3,2,1,0:T(8,128)(2,1)}, u32[]{:S(2)}) copy-start(bf16[16,5,16,512]{3,2,1,0:T(8,128)(2,1)} %copy-done) | copy-start | bytes 3932164
  78.3 2.7 copy-start.4
  85.8 13.9 %copy-start.5 = (bf16[256,512]{1,0:T(8,128)(2,1)S(1)}, bf16[256,512]{1,0:T(8,128)(2,1)}, u32[]{:S(2)}) copy-start(bf16[256,512]{1,0:T(8,128)(2,1)} %param.12) | copy-start | bytes 786436
  230.9 58.3 %all-to-all-start.6 = ((f32[5,16,16,512]{3,2,0,1:T(8,128)}), f32[5,16,16,512]{3,2,0,1:T(8,128)S(1)}, u32[]{:S(2)}, u32[]{:S(2)}) async-start(f32[5,16,16,512]{3,2,0,1:T(8,128)} %copy.147), calls=%async_computation.6 | async-start | bytes 5242880 | tf_op jit(solution)/shard_map/all_to_all | solution.py:131
  255.2 47.4 %copy-start.9 = (s32[16,5]{0,1:T(8,128)S(1)}, s32[16,5]{0,1:T(8,128)}, u32[]{:S(2)}) copy-start(s32[16,5]{0,1:T(8,128)} %copy-done.8) | copy-start | bytes 964
  255.2 47.4 %copy-start.7 = (s32[16,5]{0,1:T(8,128)S(1)}, s32[16,5]{0,1:T(8,128)}, u32[]{:S(2)}) copy-start(s32[16,5]{0,1:T(8,128)} %copy-done.6) | copy-start | bytes 964
  289.2 63.7 %all-to-all-start.4 = ((f32[5,16,16,512]{3,2,0,1:T(8,128)}), f32[5,16,16,512]{3,2,0,1:T(8,128)}, u32[]{:S(2)}, u32[]{:S(2)}) async-start(f32[5,16,16,512]{3,2,0,1:T(8,128)} %copy.142), calls=%async_computation.4 | async-start | bytes 5242880 | tf_op jit(solution)/shard_map/all_to_all | solution.py:130
  352.9 27.8 %all-to-all-start.7 = ((f32[16,16,512]{2,1,0:T(8,128)}), f32[16,16,512]{2,1,0:T(8,128)S(1)}, u32[]{:S(2)}, u32[]{:S(2)}) async-start(f32[16,16,512]{2,1,0:T(8,128)} %copy.149), calls=%async_computation.7 | async-start | bytes 1048576 | tf_op jit(solution)/shard_map/all_to_all | solution.py:141
  366.2 18.6 %copy-start.3 = (bf16[4,5,256,128]{2,3,1,0:T(8,128)(2,1)S(1)}, bf16[4,5,256,128]{2,3,1,0:T(8,128)(2,1)}, u32[]{:S(2)}) copy-start(bf16[4,5,256,128]{2,3,1,0:T(8,128)(2,1)} %get-tuple-element.57) | copy-start | bytes 3932164
  380.7 18.6 %all-to-all-start.5 = ((f32[16,16,512]{2,1,0:T(8,128)}), f32[16,16,512]{2,1,0:T(8,128)S(1)}, u32[]{:S(2)}, u32[]{:S(2)}) async-start(f32[16,16,512]{2,1,0:T(8,128)} %copy.144), calls=%async_computation.5 | async-start | bytes 1048576 | tf_op jit(solution)/shard_map/all_to_all | solution.py:140
where the time goes:
time: 403 us; the launch traced here: 401 us
  waiting for transfers between devices  145 us (36%)
  matrix products  105 us (26%)
  local copies, waits for them, and re-layouts  69.4 us (17%)
  starting transfers between devices  61.5 us (15%)
  other arithmetic  18.6 us (5%)
    all_to_all x1, waiting for transfers between devices, give_back(): lax.all_to_all(sent_keys, 'leaf', split_axis=1, concat_axis=1, tiled=True)  46.3 us
    all_to_all x1, waiting for transfers between devices, give_back(): lax.all_to_all(sent_values, 'leaf', split_axis=1, concat_axis=1, tiled=True)  34 us
    sub x4, matrix products, one_group(): weights = jnp.exp(scores - highest)  29.1 us
    dot_general x4, matrix products, one_group(): jnp.einsum('gik,gid->kd', attention_half, grad_part, preferred_element_ty...  26.7 us
    all_to_all x1, waiting for transfers between devices, fetch(): lax.all_to_all(picked_keys, 'leaf', split_axis=0, concat_axis=2, tiled=True)  25.5 us
    dot_general x4, matrix products, one_group(): jnp.einsum('gid,kd->gik', grad_part, value_part, preferred_element_type=j...  20.6 us
    all_to_all x1, starting transfers between devices, give_back(): lax.all_to_all(sent_keys, 'leaf', split_axis=1, concat_axis=1, tiled=True)  13.4 us
    all_to_all x1, starting transfers between devices, give_back(): lax.all_to_all(held_values, 'leaf', split_axis=0, concat_axis=1, tiled=True)  13.3 us
  transfers between devices with their start and end apart: 8, of which 8 were waited for; matrix products, arithmetic and copies ran while one was open for 14% of the time, Pallas kernels for 0%

commit v1 on v0

v1 whole, which is shorter than its diff:
```python
import functools
import math

import jax
import jax.numpy as jnp
from jax import lax
from jax.experimental import pallas as pl
from jax.experimental.pallas import tpu as pltpu
from jax.sharding import PartitionSpec as P

HQ = 20
HK = 4
DH = 128
PER = HQ // HK
ANCESTORS = 5
SLOTS = ANCESTORS + 1
SCALE = 1.0 / math.sqrt(DH)
EXP_SCALE = SCALE / math.log(2.0)
NT = (((1,), (1,)), ((), ()))
NN = (((1,), (0,)), ((), ()))


def dot(a, b, dims):
    return lax.dot_general(a, b, dims, preferred_element_type=jnp.float32)


def walk(me_ref, parents, assignment, lengths, owner, holder, reach):
    devices = parents.shape[0]
    me = me_ref[0]

    def invert(d, carry):
        owner[assignment[d]] = d
        return carry

    lax.fori_loop(0, devices, invert, 0)
    segment = assignment[me]
    holder[0] = me
    reach[0] = lengths[segment]
    depth = jnp.int32(0)
    up = parents[segment]
    for slot in range(1, SLOTS):
        usable = up >= 0
        at = jnp.maximum(up, 0)
        holder[slot] = owner[at]
        reach[slot] = lengths[at]
        depth = depth + usable.astype(jnp.int32)
        up = jnp.where(usable, parents[at], -1)
    holder[SLOTS] = depth


def kernel(me_ref, parents, assignment, lengths, q_ref, g_ref, o_ref, k_ref, v_ref,
           dq_ref, dk_ref, dv_ref,
           owner, holder, reach, s_ref, gm_ref, kt_ref, dqt_ref):
    rows = q_ref.shape[0]

    @pl.when(pl.program_id(0) == 0)
    def _():
        walk(me_ref, parents, assignment, lengths, owner, holder, reach)

    slots = holder[SLOTS] + 1
    dk_ref[...] = jnp.zeros_like(dk_ref)
    dv_ref[...] = jnp.zeros_like(dv_ref)
    row_at = lax.broadcasted_iota(jnp.int32, (rows, 1), 0)
    lane_at = lax.broadcasted_iota(jnp.int32, (1, rows), 1)
    key_at = lax.broadcasted_iota(jnp.int32, (rows, rows), 0)
    delta = []
    for h in range(PER):
        cols = slice(h * DH, (h + 1) * DH)
        masked = jnp.where(row_at < reach[0], g_ref[:, cols], jnp.zeros((), g_ref.dtype))
        gm_ref[:, cols] = masked
        terms = masked.astype(jnp.float32) * o_ref[:, cols].astype(jnp.float32)
        delta.append(jnp.sum(terms.T, axis=0, keepdims=True))

    def scores(slot, highest):
        held = holder[slot]
        k = k_ref[held]
        kt_ref[slot] = k.T
        limit = jnp.where(slot == 0, lane_at, reach[slot] - 1)
        allowed = key_at <= limit
        out = []
        for h in range(PER):
            s = dot(k, q_ref[:, h * DH:(h + 1) * DH], NT)
            s = jnp.where(allowed, s, -1e30)
            s_ref[slot, :, h * rows:(h + 1) * rows] = s
            out.append(jnp.maximum(highest[h], jnp.max(s, axis=0, keepdims=True)))
        return tuple(out)

    start = tuple(jnp.full((1, rows), -1e30, jnp.float32) for _ in range(PER))
    highest = lax.fori_loop(0, slots, scores, start)

    def weigh(slot, total):
        out = []
        for h in range(PER):
            at = (slot, slice(None), slice(h * rows, (h + 1) * rows))
            w = jnp.exp2((s_ref[at] - highest[h]) * EXP_SCALE)
            s_ref[at] = w
            out.append(total[h] + jnp.sum(w, axis=0, keepdims=True))
        return tuple(out)

    start = tuple(jnp.zeros((1, rows), jnp.float32) for _ in range(PER))
    total = lax.fori_loop(0, slots, weigh, start)
    inverse = [1.0 / t for t in total]
    dqt_ref[...] = jnp.zeros_like(dqt_ref)

    def grads(slot, carry):
        held = holder[slot]
        v = v_ref[held]
        kt = kt_ref[slot]
        dk = jnp.zeros((rows, DH), jnp.float32)
        dv = jnp.zeros((rows, DH), jnp.float32)
        for h in range(PER):
            cols = slice(h * DH, (h + 1) * DH)
            p = s_ref[slot, :, h * rows:(h + 1) * rows] * inverse[h]
            gm = gm_ref[:, cols]
            dp = dot(v, gm, NT)
            ds = (p * (dp - delta[h])).astype(jnp.bfloat16)
            dv = dv + dot(p.astype(jnp.bfloat16), gm, NN)
            dk = dk + dot(ds, q_ref[:, cols], NN)
            dqt_ref[h] += dot(kt, ds, NN)
        dk_ref[held] = (dk * SCALE).astype(dk_ref.dtype)
        dv_ref[held] = dv.astype(dv_ref.dtype)
        return carry

    lax.fori_loop(0, slots, grads, 0)
    for h in range(PER):
        dq_ref[:, h * DH:(h + 1) * DH] = (dqt_ref[h].T * SCALE).astype(dq_ref.dtype)


def attend(me, parents, assignment, lengths, queries, grad_out, saved_out, keys, values):
    rows = queries.shape[0]
    devices = keys.shape[0]
    smem = pl.BlockSpec(memory_space=pltpu.SMEM)
    wide = pl.BlockSpec((rows, PER * DH), lambda g: (0, g))
    held = pl.BlockSpec((devices, rows, DH), lambda g: (0, 0, g))
    return pl.pallas_call(
        kernel,
        grid=(HK,),
        in_specs=[smem] * 4 + [wide] * 3 + [held] * 2,
        out_specs=[wide, held, held],
        out_shape=[
            jax.ShapeDtypeStruct(queries.shape, jnp.bfloat16),
            jax.ShapeDtypeStruct(keys.shape, jnp.bfloat16),
            jax.ShapeDtypeStruct(values.shape, jnp.bfloat16),
        ],
        scratch_shapes=[
            pltpu.SMEM((devices,), jnp.int32),
            pltpu.SMEM((SLOTS + 1,), jnp.int32),
            pltpu.SMEM((SLOTS,), jnp.int32),
            pltpu.VMEM((SLOTS, rows, PER * rows), jnp.float32),
            pltpu.VMEM((rows, PER * DH), jnp.bfloat16),
            pltpu.VMEM((SLOTS, DH, rows), jnp.bfloat16),
            pltpu.VMEM((PER, DH, rows), jnp.float32),
        ],
        compiler_params=pltpu.CompilerParams(vmem_limit_bytes=56 * 1024 * 1024),
    )(me, parents, assignment, lengths, queries, grad_out, saved_out, keys, values)


def local(queries, keys, values, saved_out, grad_out, parents, assignment, lengths):
    rows, columns = keys.shape
    me = lax.axis_index("leaf").astype(jnp.int32).reshape(1)
    all_keys = lax.all_gather(keys, "leaf")
    all_values = lax.all_gather(values, "leaf")
    dq, dk, dv = attend(
        me, parents, assignment, lengths, queries, grad_out, saved_out, all_keys, all_values
    )
    key_grad = lax.psum_scatter(dk, "leaf", scatter_dimension=0)
    value_grad = lax.psum_scatter(dv, "leaf", scatter_dimension=0)
    return (dq, key_grad, value_grad)


def solution(mesh):
    tokens = P(("groups", "leaf"), None)
    tables = P("groups")
    return jax.shard_map(
        local,
        mesh=mesh,
        in_specs=(tokens,) * 5 + (tables,) * 3,
        out_specs=(tokens,) * 3,
        check_vma=False,
    )
```

time: 403 us -> 319 us (0.79)
  waiting for transfers between devices: 145 us -> 255 us
  matrix products: 105 us -> 0 us
  local copies, waits for them, and re-layouts: 69.4 us -> 0 us
  starting transfers between devices: 61.5 us -> 0.16 us
  Pallas kernels: 0 us -> 50.2 us
  other arithmetic: 18.6 us -> 0 us
  between operations: 1 us -> 13.8 us
    reduce_scatter x0 -> x2, waiting for transfers between devices: none -> 147 us  [the longest x1 76.5 us: local(): value_grad = lax.psum_scatter(dv, 'leaf', scatter_dimension=0)]
    all_to_all x8 -> x0, waiting for transfers between devices: 145 us -> none  [the longest x1 46.3 us: give_back(): lax.all_to_all(sent_keys, 'leaf', split_axis=1, concat_axis=1, tiled=True)]
    all_gather x0 -> x2, waiting for transfers between devices: none -> 106 us  [the longest x1 54.8 us: local(): all_keys = lax.all_gather(keys, 'leaf')]
    dot_general x18 -> x0, matrix products: 75.9 us -> none  [the longest x4 26.7 us: one_group(): jnp.einsum('gik,gid->kd', attention_half, grad_part, preferred_element_ty...]
    all_to_all x8 -> x0, starting transfers between devices: 61.5 us -> none  [the longest x1 13.4 us: give_back(): lax.all_to_all(sent_keys, 'leaf', split_axis=1, concat_axis=1, tiled=True)]
    pallas_call x0 -> x1, Pallas kernels: none -> 50.2 us  [attend(): pl.pallas_call(kernel, grid=(HK,), in_specs=[smem] * 4 + [wide] * 3 + [he...]
    sub x4 -> x0, matrix products: 29.1 us -> none  [one_group(): weights = jnp.exp(scores - highest)]
    slice x4 -> x0, local copies, waits for them, and re-layouts: 15.8 us -> none  [the longest x2 8.43 us: local(): key_terms[1:]]
  transfers between devices with their start and end apart: 8 -> 4, of which waited for: 8 -> 4; matrix products, arithmetic and copies ran while one was open for 14% -> 0% of each run, Pallas kernels for 0% -> 0%
where the time goes in v1:
time: 319 us
  waiting for transfers between devices  255 us (80%)
  Pallas kernels  50.2 us (16%)
  between operations  13.8 us (4%)
    reduce_scatter x1, waiting for transfers between devices, local(): value_grad = lax.psum_scatter(dv, 'leaf', scatter_dimension=0)  76.5 us
    reduce_scatter x1, waiting for transfers between devices, local(): key_grad = lax.psum_scatter(dk, 'leaf', scatter_dimension=0)  70.4 us
    all_gather x1, waiting for transfers between devices, local(): all_keys = lax.all_gather(keys, 'leaf')  54.8 us
    all_gather x1, waiting for transfers between devices, local(): all_values = lax.all_gather(values, 'leaf')  51.2 us
    pallas_call x1, Pallas kernels, attend(): pl.pallas_call(kernel, grid=(HK,), in_specs=[smem] * 4 + [wide] * 3 + [he...  50.2 us
  transfers between devices with their start and end apart: 4, of which 4 were waited for; matrix products, arithmetic and copies ran while one was open for 0% of the time, Pallas kernels for 0%

profile of v1, /device:TPU:0, one launch (start us, length us, event | category | flops | bytes accessed | tf_op | source)
XLA Modules:
  0.0 319.0 jit_solution(17544139531072191231)
XLA Ops:
  7.2 0.0 all-gather.5.cloned.1.call-start
  7.2 0.7 all-gather.5.cloned.1.call-update
  7.9 0.0 all-gather.7.cloned.1.call-start
  7.9 0.7 all-gather.7.cloned.1.call-update
  8.6 0.0 reduce-scatter.3.cloned.1.call-start
  8.7 54.8 %all-gather.5.cloned.1.call-done = bf16[4096,512]{1,0:T(8,128)(2,1)} async-done(((bf16[256,512]{1,0:T(8,128)(2,1)}), bf16[4096,512]{1,0:T(8,128)(2,1)}) %all-gather.5.cloned.1.call-update) | async-done | bytes 4194320 | tf_op jit(solution)/shard_map/all_gather | solution.py:161
  63.5 51.2 %all-gather.7.cloned.1.call-done = bf16[4096,512]{1,0:T(8,128)(2,1)} async-done(((bf16[256,512]{1,0:T(8,128)(2,1)}), bf16[4096,512]{1,0:T(8,128)(2,1)}) %all-gather.7.cloned.1.call-update) | async-done | bytes 4194320 | tf_op jit(solution)/shard_map/all_gather | solution.py:162
  114.7 50.2 %shard_map.103 = (bf16[256,2560]{1,0:T(8,128)(2,1)}, bf16[16,256,512]{2,1,0:T(8,128)(2,1)}, bf16[16,256,512]{2,1,0:T(8,128)(2,1)}) custom-call(s32[1]{0:T(128)} %bitcast.me_ref, s32[16]{0:T(128)} %parents.1, s32[16]{0:T(128)} %assignment.1, s32[16]{0:T(128)} %lengths.1, bf16[256,2560]{1,0:T(8,128)(2,1)} %q_ref.1, bf16[256,2560]{1,0:T(8,128)(2,1)} %g_ref.1, ...), custom_call_target="tpu_custom_call" | custom-call | tf_op jit(solution)/shard_map/pallas_call | solution.py:135
  164.9 0.0 reduce-scatter.3.cloned.1.call-update
  164.9 0.0 reduce-scatter.5.cloned.1.call-start
  165.0 0.5 reduce-scatter.5.cloned.1.call-update
  165.5 70.4 %reduce-scatter.3.cloned.1.call-done = bf16[1,256,512]{2,1,0:T(8,128)(2,1)} async-done(((bf16[16,256,512]{2,1,0:T(8,128)(2,1)}), bf16[1,256,512]{2,1,0:T(8,128)(2,1)}) %reduce-scatter.3.cloned.1.call-update) | async-done | bytes 262160 | tf_op jit(solution)/shard_map/reduce_scatter | solution.py:166
  235.9 76.5 %reduce-scatter.5.cloned.1.call-done = bf16[1,256,512]{2,1,0:T(8,128)(2,1)} async-done(((bf16[16,256,512]{2,1,0:T(8,128)(2,1)}), bf16[1,256,512]{2,1,0:T(8,128)(2,1)}) %reduce-scatter.5.cloned.1.call-update) | async-done | bytes 262160 | tf_op jit(solution)/shard_map/reduce_scatter | solution.py:167
Async XLA Ops:
  7.2 56.3 %all-gather.5.cloned.1.call-start = ((), (), s32[]{:S(2)}) async-start(), calls=%async_computation.4 | async-start | bytes 4456448 | tf_op jit(solution)/shard_map/all_gather | solution.py:161
  7.9 106.8 %all-gather.7.cloned.1.call-start = ((), (), s32[]{:S(2)}) async-start(), calls=%async_computation.5 | async-start | bytes 4456448 | tf_op jit(solution)/shard_map/all_gather | solution.py:162
  8.6 227.3 %reduce-scatter.3.cloned.1.call-start = ((), (), s32[]{:S(2)}) async-start(), calls=%async_computation.2 | async-start | bytes 4456448 | tf_op jit(solution)/shard_map/reduce_scatter | solution.py:166
  164.9 147.5 %reduce-scatter.5.cloned.1.call-start = ((), (), s32[]{:S(2)}) async-start(), calls=%async_computation.3 | async-start | bytes 4456448 | tf_op jit(solution)/shard_map/reduce_scatter | solution.py:167
Sparse Core Ops, SparseCore 0:
  10.2 53.2 all-gather.4
  65.6 49.0 all-gather.6
  165.1 70.8 reduce-scatter.2
  240.7 71.6 reduce-scatter.4

commit v2 on v1

v2 whole, which is shorter than its diff:
```python
import functools
import math

import jax
import jax.numpy as jnp
from jax import lax
from jax.experimental import pallas as pl
from jax.experimental.pallas import tpu as pltpu
from jax.sharding import PartitionSpec as P

HQ = 20
HK = 4
DH = 128
PER = HQ // HK
HALF = HK // 2
WIDE = PER * DH
ANCESTORS = 5
SLOTS = ANCESTORS + 1
SCALE = 1.0 / math.sqrt(DH)
EXP_SCALE = SCALE / math.log(2.0)
NT = (((1,), (1,)), ((), ()))
NN = (((1,), (0,)), ((), ()))


def dot(a, b, dims):
    return lax.dot_general(a, b, dims, preferred_element_type=jnp.float32)


def ring_order(chips):
    if chips == 8:
        return [0, 2, 4, 6, 7, 5, 3, 1]
    return list(range(chips))


def walk(device, me, places, parents, assignment, lengths, owner, block, reach, side):
    chips = places.shape[0]
    here = places[me // 2]

    def place(held):
        ahead = places[held // 2] - here
        ahead = jnp.where(ahead < 0, ahead + chips, ahead)
        return ahead * 2 + jnp.where(held % 2 == me % 2, 0, 1)

    segment = assignment[device]
    block[side, 0] = place(device)
    reach[side, 0] = lengths[segment]
    depth = jnp.int32(0)
    up = parents[segment]
    for slot in range(1, SLOTS):
        usable = up >= 0
        at = jnp.maximum(up, 0)
        block[side, slot] = place(owner[at])
        reach[side, slot] = lengths[at]
        depth = depth + usable.astype(jnp.int32)
        up = jnp.where(usable, parents[at], -1)
    block[side, SLOTS] = depth + 1


def kernel(chips, head, me_ref, places, parents, assignment, lengths, *refs):
    mine, refs = refs[:3], refs[3:]
    other, refs = refs[:3], refs[3:]
    k_in, refs = refs[:chips], refs[chips:]
    v_in, refs = refs[:chips], refs[chips:]
    dk_ref, dv_ref, dq_mine, dq_other = refs[:4]
    (owner, block, reach, q_ref, g_ref, o_ref, k_ref, v_ref, dk_sum, dv_sum,
     s_ref, kt_ref, dqt_ref, sems) = refs[4:]
    rows = dq_mine.shape[0]
    me = me_ref[0]

    copies = []
    for at, (ours, theirs, held) in enumerate(zip(mine, other, (q_ref, g_ref, o_ref))):
        column = pl.multiple_of((me % 2 * HALF + head) * WIDE, WIDE)
        copies.append(pltpu.make_async_copy(ours.at[:, pl.ds(column, WIDE)], held.at[0], sems.at[at]))
        copies.append(pltpu.make_async_copy(theirs.at[:, head * WIDE:(head + 1) * WIDE], held.at[1], sems.at[3 + at]))
    for at in range(chips):
        copies.append(pltpu.make_async_copy(k_in[at], k_ref.at[at], sems.at[6 + at]))
        copies.append(pltpu.make_async_copy(v_in[at], v_ref.at[at], sems.at[6 + chips + at]))
    for copy in copies:
        copy.start()

    def invert(d, carry):
        owner[assignment[d]] = d
        return carry

    lax.fori_loop(0, assignment.shape[0], invert, 0)
    walk(me, me, places, parents, assignment, lengths, owner, block, reach, 0)
    walk(me + 1 - me % 2 * 2, me, places, parents, assignment, lengths, owner, block, reach, 1)
    dk_sum[...] = jnp.zeros_like(dk_sum)
    dv_sum[...] = jnp.zeros_like(dv_sum)
    row_at = lax.broadcasted_iota(jnp.int32, (rows, 1), 0)
    lane_at = lax.broadcasted_iota(jnp.int32, (1, rows), 1)
    key_at = lax.broadcasted_iota(jnp.int32, (rows, rows), 0)
    for copy in copies:
        copy.wait()

    for side, dq_ref in enumerate((dq_mine, dq_other)):
        slots = block[side, SLOTS]
        delta = []
        for h in range(PER):
            cols = slice(h * DH, (h + 1) * DH)
            live = row_at < reach[side, 0]
            masked = jnp.where(live, g_ref[side, :, cols], jnp.zeros((), g_ref.dtype))
            g_ref[side, :, cols] = masked
            terms = masked.astype(jnp.float32) * o_ref[side, :, cols].astype(jnp.float32)
            delta.append(jnp.sum(terms.T, axis=0, keepdims=True))

        def key_rows(ref, slot):
            at = block[side, slot]
            first = pl.multiple_of(at % 2 * rows, rows)
            return ref.at[at // 2, pl.ds(first, rows), :]

        def scores(slot, highest):
            k = key_rows(k_ref, slot)[...]
            kt_ref[slot] = k.T
            limit = jnp.where(slot == 0, lane_at, reach[side, slot] - 1)
            allowed = key_at <= limit
            out = []
            for h in range(PER):
                s = dot(k, q_ref[side, :, h * DH:(h + 1) * DH], NT)
                s = jnp.where(allowed, s, -1e30)
                s_ref[slot, :, h * rows:(h + 1) * rows] = s
                out.append(jnp.maximum(highest[h], jnp.max(s, axis=0, keepdims=True)))
            return tuple(out)

        start = tuple(jnp.full((1, rows), -1e30, jnp.float32) for _ in range(PER))
        highest = lax.fori_loop(0, slots, scores, start)

        def weigh(slot, total):
            out = []
            for h in range(PER):
                at = (slot, slice(None), slice(h * rows, (h + 1) * rows))
                w = jnp.exp2((s_ref[at] - highest[h]) * EXP_SCALE)
                s_ref[at] = w
                out.append(total[h] + jnp.sum(w, axis=0, keepdims=True))
            return tuple(out)

        start = tuple(jnp.zeros((1, rows), jnp.float32) for _ in range(PER))
        total = lax.fori_loop(0, slots, weigh, start)
        inverse = [1.0 / t for t in total]
        dqt_ref[...] = jnp.zeros_like(dqt_ref)

        def grads(slot, carry):
            v = key_rows(v_ref, slot)[...]
            kt = kt_ref[slot]
            dk = jnp.zeros((rows, DH), jnp.float32)
            dv = jnp.zeros((rows, DH), jnp.float32)
            for h in range(PER):
                cols = slice(h * DH, (h + 1) * DH)
                p = s_ref[slot, :, h * rows:(h + 1) * rows] * inverse[h]
                gm = g_ref[side, :, cols]
                dp = dot(v, gm, NT)
                ds = (p * (dp - delta[h])).astype(jnp.bfloat16)
                dv = dv + dot(p.astype(jnp.bfloat16), gm, NN)
                dk = dk + dot(ds, q_ref[side, :, cols], NN)
                dqt_ref[h] += dot(kt, ds, NN)
            key_rows(dk_sum, slot)[...] += dk
            key_rows(dv_sum, slot)[...] += dv
            return carry

        lax.fori_loop(0, slots, grads, 0)
        for h in range(PER):
            dq_ref[:, h * DH:(h + 1) * DH] = (dqt_ref[h].T * SCALE).astype(dq_ref.dtype)
    dk_ref[...] = (dk_sum[...] * SCALE).astype(dk_ref.dtype)
    dv_ref[...] = dv_sum[...].astype(dv_ref.dtype)


def attend(head, tables, mine, other, keys, values):
    rows = mine[0].shape[0]
    chips = len(keys)
    devices = 2 * chips
    smem = pl.BlockSpec(memory_space=pltpu.SMEM)
    hbm = pl.BlockSpec(memory_space=pl.ANY)
    vmem = pl.BlockSpec(memory_space=pltpu.VMEM)
    dense = jax.ShapeDtypeStruct((chips, 2 * rows, DH), jnp.bfloat16)
    narrow = jax.ShapeDtypeStruct((rows, WIDE), jnp.bfloat16)
    work = 2 * 5 * 5 * PER * rows * rows * DH * 2
    return pl.pallas_call(
        functools.partial(kernel, chips, head),
        in_specs=[smem] * 5 + [hbm] * (6 + 2 * chips),
        out_specs=[vmem] * 4,
        out_shape=[dense, dense, narrow, narrow],
        scratch_shapes=[
            pltpu.SMEM((devices,), jnp.int32),
            pltpu.SMEM((2, SLOTS + 1), jnp.int32),
            pltpu.SMEM((2, SLOTS), jnp.int32),
            pltpu.VMEM((2, rows, WIDE), jnp.bfloat16),
            pltpu.VMEM((2, rows, WIDE), jnp.bfloat16),
            pltpu.VMEM((2, rows, WIDE), jnp.bfloat16),
            pltpu.VMEM((chips, 2 * rows, DH), jnp.bfloat16),
            pltpu.VMEM((chips, 2 * rows, DH), jnp.bfloat16),
            pltpu.VMEM((chips, 2 * rows, DH), jnp.float32),
            pltpu.VMEM((chips, 2 * rows, DH), jnp.float32),
            pltpu.VMEM((SLOTS, rows, PER * rows), jnp.float32),
            pltpu.VMEM((SLOTS, DH, rows), jnp.bfloat16),
            pltpu.VMEM((PER, DH, rows), jnp.float32),
            pltpu.SemaphoreType.DMA((6 + 2 * chips,)),
        ],
        compiler_params=pltpu.CompilerParams(vmem_limit_bytes=56 * 1024 * 1024),
        cost_estimate=pl.CostEstimate(flops=work, bytes_accessed=8 << 20, transcendentals=0),
    )(*tables, *mine, *other, *keys, *values)


def spread(block, right, left, steps_right, steps_left):
    chips = 1 + steps_right + steps_left
    got = [block] + [None] * (chips - 1)
    up = down = block
    for step in range(1, max(steps_right, steps_left) + 1):
        if step <= steps_right:
            up = lax.ppermute(up, "leaf", right)
            got[chips - step] = up
        if step <= steps_left:
            down = lax.ppermute(down, "leaf", left)
            got[step] = down
    return got


def add(a, b):
    return (a.astype(jnp.float32) + b.astype(jnp.float32)).astype(jnp.bfloat16)


def collect(terms, right, left, steps_right, steps_left):
    chips = terms.shape[0]
    up = terms[steps_right]
    down = terms[chips - steps_left]
    for step in range(max(steps_right, steps_left), 0, -1):
        if step <= steps_right:
            up = lax.ppermute(up, "leaf", right)
            if step > 1:
                up = add(up, terms[step - 1])
        if step <= steps_left:
            down = lax.ppermute(down, "leaf", left)
            if step > 1:
                down = add(down, terms[chips - step + 1])
    total = terms[0].astype(jnp.float32) + up.astype(jnp.float32) + down.astype(jnp.float32)
    return total.astype(jnp.bfloat16)


def local(queries, keys, values, saved_out, grad_out, parents, assignment, lengths):
    rows = keys.shape[0]
    chips = lax.axis_size("leaf") // 2
    order = ring_order(chips)
    ahead = [(order[i], order[(i + 1) % chips]) for i in range(chips)]
    right = [(2 * a + c, 2 * b + c) for a, b in ahead for c in range(2)]
    left = [(b, a) for a, b in right]
    swap = [(2 * a + c, 2 * a + 1 - c) for a in range(chips) for c in range(2)]
    places = jnp.asarray([order.index(chip) for chip in range(chips)], jnp.int32)
    index = lax.axis_index("leaf").astype(jnp.int32)
    core = index % 2
    tables = (index.reshape(1), places, parents, assignment, lengths)
    far, near = chips // 2, chips - 1 - chips // 2

    def part(array, which, width):
        return lax.dynamic_slice(array, (0, which * width), (rows, width))

    def chip_block(array, head):
        kept = part(array, core * HALF + head, DH)
        sent = part(array, (1 - core) * HALF + head, DH)
        return jnp.concatenate([kept, lax.ppermute(sent, "leaf", swap)], axis=0)

    gathered = []
    for head in range(HALF):
        gathered.append((
            spread(chip_block(keys, head), right, left, far, near),
            spread(chip_block(values, head), right, left, near, far),
        ))
    mine = (queries, grad_out, saved_out)
    other = tuple(
        lax.ppermute(part(array, 1 - core, HALF * WIDE), "leaf", swap) for array in mine
    )
    key_sums, value_sums, ours, theirs = [], [], [], []
    for head in range(HALF):
        dk, dv, dq_mine, dq_other = attend(head, tables, mine, other, *gathered[head])
        key_sums.append(collect(dk, right, left, far, near))
        value_sums.append(collect(dv, right, left, near, far))
        ours.append(dq_mine)
        theirs.append(lax.ppermute(dq_other, "leaf", swap))

    def whole(kept, got):
        low = jnp.concatenate([jnp.where(core == 0, a, b) for a, b in zip(kept, got)], axis=1)
        high = jnp.concatenate([jnp.where(core == 0, b, a) for a, b in zip(kept, got)], axis=1)
        return jnp.concatenate([low, high], axis=1)

    def owned(sums):
        kept = [total[:rows] for total in sums]
        got = [lax.ppermute(total[rows:], "leaf", swap) for total in sums]
        return whole(kept, got)

    return (whole(ours, theirs), owned(key_sums), owned(value_sums))


def solution(mesh):
    tokens = P(("groups", "leaf"), None)
    tables = P("groups")
    return jax.shard_map(
        local,
        mesh=mesh,
        in_specs=(tokens,) * 5 + (tables,) * 3,
        out_specs=(tokens,) * 3,
        check_vma=False,
    )
```

time: 319 us -> 178 us (0.56)
  waiting for transfers between devices: 255 us -> 51 us
  starting transfers between devices: 0.16 us -> 73.1 us
  Pallas kernels: 50.2 us -> 36.9 us
  between operations: 13.8 us -> 1.52 us
  local copies, waits for them, and re-layouts: 0 us -> 8.42 us
  other arithmetic: 0 us -> 4.71 us
    reduce_scatter x2 -> x0, waiting for transfers between devices: 147 us -> none  [the longest x1 76.5 us: local(): value_grad = lax.psum_scatter(dv, 'leaf', scatter_dimension=0)]
    all_gather x2 -> x0, waiting for transfers between devices: 106 us -> none  [the longest x1 54.8 us: local(): all_keys = lax.all_gather(keys, 'leaf')]
    ppermute x0 -> x69, starting transfers between devices: none -> 73.1 us  [the longest x14 31.1 us: collect(): up = lax.ppermute(up, 'leaf', right)]
    ppermute x0 -> x69, waiting for transfers between devices: none -> 51 us  [the longest x14 20.5 us: spread(): up = lax.ppermute(up, 'leaf', right)]
    pallas_call x1 -> x2, Pallas kernels: 50.2 us -> 36.9 us  [attend(): pl.pallas_call(functools.partial(kernel, chips, head), in_specs=[smem] *...]
  transfers between devices with their start and end apart: 4 -> 69, of which waited for: 4 -> 26; matrix products, arithmetic and copies ran while one was open for 0% -> 5% of each run, Pallas kernels for 0% -> 21%
where the time goes in v2:
time: 178 us; the launch traced here: 176 us
  starting transfers between devices  73.1 us (41%)
  waiting for transfers between devices  51 us (29%)
  Pallas kernels  36.9 us (21%)
  local copies, waits for them, and re-layouts  8.42 us (5%)
  other arithmetic  4.71 us (3%)
    pallas_call x2, Pallas kernels, attend(): pl.pallas_call(functools.partial(kernel, chips, head), in_specs=[smem] *...  36.9 us
    ppermute x14, starting transfers between devices, collect(): up = lax.ppermute(up, 'leaf', right)  31.1 us
    ppermute x14, waiting for transfers between devices, spread(): up = lax.ppermute(up, 'leaf', right)  20.5 us
    ppermute x14, starting transfers between devices, spread(): down = lax.ppermute(down, 'leaf', left)  17.7 us
    ppermute x14, waiting for transfers between devices, collect(): down = lax.ppermute(down, 'leaf', left)  16.8 us
    ppermute x14, starting transfers between devices, collect(): down = lax.ppermute(down, 'leaf', left)  11.6 us
    ppermute x14, starting transfers between devices, spread(): up = lax.ppermute(up, 'leaf', right)  10.2 us
    ppermute x14, waiting for transfers between devices, spread(): down = lax.ppermute(down, 'leaf', left)  8.55 us
  transfers between devices with their start and end apart: 69, of which 26 were waited for; matrix products, arithmetic and copies ran while one was open for 5% of the time, Pallas kernels for 21%

profile of v2, /device:TPU:0, one launch (start us, length us, event | category | flops | bytes accessed | tf_op | source)
XLA Modules:
  0.0 175.6 jit_solution(3560059921670014269)
XLA Ops:
  3.9 3.0 %collective-permute-start.12 = (bf16[512,128]{1,0:T(8,128)(2,1)S(1)}, bf16[512,128]{1,0:T(8,128)(2,1)S(1)}, u32[]{:S(2)}, u32[]{:S(2)}) collective-permute-start(bf16[512,128]{1,0:T(8,128)(2,1)S(1)} %pad_maximum_fusion.4.refs_14_), channel_id=1, source_target_pairs={{4,0},{5,1},{8,4},{9,5},{12,8},{13,9},{14,12},{15,13},{10,14},{11,... | collective-permute-start | bytes 393224 | tf_op jit(solution)/shard_map/ppermute | solution.py:212
  11.2 4.9 %collective-permute-done.7.refs_13_ = bf16[512,128]{1,0:T(8,128)(2,1)S(1)} collective-permute-done((bf16[512,128]{1,0:T(8,128)(2,1)S(1)}, bf16[512,128]{1,0:T(8,128)(2,1)S(1)}, u32[]{:S(2)}, u32[]{:S(2)}) %collective-permute-start.7) | collective-permute-done | bytes 131104 | tf_op jit(solution)/shard_map/ppermute | solution.py:209
  22.6 2.7 %collective-permute-done.21.refs_7_ = bf16[512,128]{1,0:T(8,128)(2,1)S(1)} collective-permute-done((bf16[512,128]{1,0:T(8,128)(2,1)S(1)}, bf16[512,128]{1,0:T(8,128)(2,1)S(1)}, u32[]{:S(2)}, u32[]{:S(2)}) %collective-permute-start.21) | collective-permute-done | bytes 131104 | tf_op jit(solution)/shard_map/ppermute | solution.py:212
  37.3 3.0 %collective-permute-done.9.refs_11_ = bf16[512,128]{1,0:T(8,128)(2,1)} collective-permute-done((bf16[512,128]{1,0:T(8,128)(2,1)S(1)}, bf16[512,128]{1,0:T(8,128)(2,1)}, u32[]{:S(2)}, u32[]{:S(2)}) %collective-permute-start.9) | collective-permute-done | bytes 131104 | tf_op jit(solution)/shard_map/ppermute | solution.py:209
  42.4 3.8 %collective-permute-done.18.refs_19_ = bf16[512,128]{1,0:T(8,128)(2,1)S(1)} collective-permute-done((bf16[512,128]{1,0:T(8,128)(2,1)S(1)}, bf16[512,128]{1,0:T(8,128)(2,1)S(1)}, u32[]{:S(2)}, u32[]{:S(2)}) %collective-permute-start.18) | collective-permute-done | bytes 131104 | tf_op jit(solution)/shard_map/ppermute | solution.py:209
  48.3 4.3 %collective-permute-done.26.refs_11_ = bf16[512,128]{1,0:T(8,128)(2,1)} collective-permute-done((bf16[512,128]{1,0:T(8,128)(2,1)S(1)}, bf16[512,128]{1,0:T(8,128)(2,1)}, u32[]{:S(2)}, u32[]{:S(2)}) %collective-permute-start.26) | collective-permute-done | bytes 131104 | tf_op jit(solution)/shard_map/ppermute | solution.py:209
  55.3 3.2 %collective-permute-done.10.refs_10_ = bf16[512,128]{1,0:T(8,128)(2,1)} collective-permute-done((bf16[512,128]{1,0:T(8,128)(2,1)}, bf16[512,128]{1,0:T(8,128)(2,1)}, u32[]{:S(2)}, u32[]{:S(2)}) %collective-permute-start.10) | collective-permute-done | bytes 131104 | tf_op jit(solution)/shard_map/ppermute | solution.py:209
  58.5 2.1 %collective-permute-start.23 = (bf16[512,128]{1,0:T(8,128)(2,1)}, bf16[512,128]{1,0:T(8,128)(2,1)S(1)}, u32[]{:S(2)}, u32[]{:S(2)}) collective-permute-start(bf16[512,128]{1,0:T(8,128)(2,1)} %collective-permute-done.22.refs_8_), channel_id=1, source_target_pairs={{4,0},{5,1},{8,4},{9,5},{12,8},{13,9},{14,12},{15,13},{10,14},{11,... | collective-permute-start | bytes 393224 | tf_op jit(solution)/shard_map/ppermute | solution.py:212
  63.7 18.3 %shard_map.112 = (bf16[8,512,128]{2,1,0:T(8,128)(2,1)}, bf16[8,512,128]{2,1,0:T(8,128)(2,1)}, bf16[256,640]{1,0:T(8,128)(2,1)}, bf16[256,640]{1,0:T(8,128)(2,1)}) custom-call(s32[1]{0:T(128)} %bitcast.me_ref, s32[8]{0:T(128)} %constant.32.clone.places, s32[16]{0:T(128)} %parents.3, s32[16]{0:T(128)} %assignment.3, s32[16]{0:T(128)} %lengths.3, ...), custom_call_target="tpu_custom_call" | custom-call | flops 4194304000 | bytes 8388608 | tf_op jit(solution)/shard_map/pallas_call | solution.py:177
  83.0 4.9 %collective-permute-start.56 = (bf16[512,128]{1,0:T(8,128)(2,1)S(1)}, bf16[512,128]{1,0:T(8,128)(2,1)S(1)}, u32[]{:S(2)}, u32[]{:S(2)}) collective-permute-start(bf16[512,128]{1,0:T(8,128)(2,1)S(1)} %get-tuple-element.24), channel_id=1, source_target_pairs={{4,0},{5,1},{8,4},{9,5},{12,8},{13,9},{14,12},{15,13},{10,14},{11,... | collective-permute-start | bytes 393224 | tf_op jit(solution)/shard_map/ppermute | solution.py:231
  89.4 18.5 %shard_map.113 = (bf16[8,512,128]{2,1,0:T(8,128)(2,1)}, bf16[8,512,128]{2,1,0:T(8,128)(2,1)}, bf16[256,640]{1,0:T(8,128)(2,1)}, bf16[256,640]{1,0:T(8,128)(2,1)}) custom-call(s32[1]{0:T(128)} %bitcast.me_ref, s32[8]{0:T(128)} %constant.32.clone.places, s32[16]{0:T(128)} %parents.3, s32[16]{0:T(128)} %assignment.3, s32[16]{0:T(128)} %lengths.3, ...), custom_call_target="tpu_custom_call" | custom-call | flops 4194304000 | bytes 8388608 | tf_op jit(solution)/shard_map/pallas_call | solution.py:177
  109.1 5.7 %collective-permute-start.64 = (bf16[512,128]{1,0:T(8,128)(2,1)S(1)}, bf16[512,128]{1,0:T(8,128)(2,1)S(1)}, u32[]{:S(2)}, u32[]{:S(2)}) collective-permute-start(bf16[512,128]{1,0:T(8,128)(2,1)S(1)} %get-tuple-element.30), channel_id=1, source_target_pairs={{4,0},{5,1},{8,4},{9,5},{12,8},{13,9},{14,12},{15,13},{10,14},{11,... | collective-permute-start | bytes 393224 | tf_op jit(solution)/shard_map/ppermute | solution.py:231
  114.8 8.4 %collective-permute-start.37 = (bf16[512,128]{1,0:T(8,128)(2,1)S(1)}, bf16[512,128]{1,0:T(8,128)(2,1)S(1)}, u32[]{:S(2)}, u32[]{:S(2)}) collective-permute-start(bf16[512,128]{1,0:T(8,128)(2,1)S(1)} %get-tuple-element.35), channel_id=1, source_target_pairs={{0,4},{1,5},{4,8},{5,9},{8,12},{9,13},{12,14},{13,15},{14,10},{15,... | collective-permute-start | bytes 393224 | tf_op jit(solution)/shard_map/ppermute | solution.py:227
  124.3 2.1 %collective-permute-start.45 = (bf16[512,128]{1,0:T(8,128)(2,1)S(1)}, bf16[512,128]{1,0:T(8,128)(2,1)S(1)}, u32[]{:S(2)}, u32[]{:S(2)}) collective-permute-start(bf16[512,128]{1,0:T(8,128)(2,1)S(1)} %get-tuple-element.41), channel_id=1, source_target_pairs={{0,4},{1,5},{4,8},{5,9},{8,12},{9,13},{12,14},{13,15},{14,10},{15,... | collective-permute-start | bytes 393224 | tf_op jit(solution)/shard_map/ppermute | solution.py:227
  129.5 6.2 %collective-permute-done.57 = bf16[512,128]{1,0:T(8,128)(2,1)S(1)} collective-permute-done((bf16[512,128]{1,0:T(8,128)(2,1)S(1)}, bf16[512,128]{1,0:T(8,128)(2,1)S(1)}, u32[]{:S(2)}, u32[]{:S(2)}) %collective-permute-start.57) | collective-permute-done | bytes 131104 | tf_op jit(solution)/shard_map/ppermute | solution.py:231
  135.9 4.8 %collective-permute-done.65 = bf16[512,128]{1,0:T(8,128)(2,1)S(1)} collective-permute-done((bf16[512,128]{1,0:T(8,128)(2,1)S(1)}, bf16[512,128]{1,0:T(8,128)(2,1)S(1)}, u32[]{:S(2)}, u32[]{:S(2)}) %collective-permute-start.65) | collective-permute-done | bytes 131104 | tf_op jit(solution)/shard_map/ppermute | solution.py:231
  140.7 2.0 %collective-permute-start.38 = (bf16[512,128]{1,0:T(8,128)(2,1)S(1)}, bf16[512,128]{1,0:T(8,128)(2,1)S(1)}, u32[]{:S(2)}, u32[]{:S(2)}) collective-permute-start(bf16[512,128]{1,0:T(8,128)(2,1)S(1)} %fusion.25), channel_id=1, source_target_pairs={{0,4},{1,5},{4,8},{5,9},{8,12},{9,13},{12,14},{13,15},{14,10},{15,... | collective-permute-start | bytes 393224 | tf_op jit(solution)/shard_map/ppermute | solution.py:227
  144.8 2.0 %collective-permute-done.38 = bf16[512,128]{1,0:T(8,128)(2,1)S(1)} collective-permute-done((bf16[512,128]{1,0:T(8,128)(2,1)S(1)}, bf16[512,128]{1,0:T(8,128)(2,1)S(1)}, u32[]{:S(2)}, u32[]{:S(2)}) %collective-permute-start.38) | collective-permute-done | bytes 131104 | tf_op jit(solution)/shard_map/ppermute | solution.py:227
  146.8 2.0 %collective-permute-start.54 = (bf16[512,128]{1,0:T(8,128)(2,1)S(1)}, bf16[512,128]{1,0:T(8,128)(2,1)S(1)}, u32[]{:S(2)}, u32[]{:S(2)}) collective-permute-start(bf16[512,128]{1,0:T(8,128)(2,1)S(1)} %get-tuple-element.21), channel_id=1, source_target_pairs={{0,4},{1,5},{4,8},{5,9},{8,12},{9,13},{12,14},{13,15},{14,10},{15,... | collective-permute-start | bytes 393224 | tf_op jit(solution)/shard_map/ppermute | solution.py:227
  149.6 2.0 %collective-permute-start.62 = (bf16[512,128]{1,0:T(8,128)(2,1)S(1)}, bf16[512,128]{1,0:T(8,128)(2,1)S(1)}, u32[]{:S(2)}, u32[]{:S(2)}) collective-permute-start(bf16[512,128]{1,0:T(8,128)(2,1)S(1)} %get-tuple-element.27), channel_id=1, source_target_pairs={{0,4},{1,5},{4,8},{5,9},{8,12},{9,13},{12,14},{13,15},{14,10},{15,... | collective-permute-start | bytes 393224 | tf_op jit(solution)/shard_map/ppermute | solution.py:227
  151.8 2.2 %collective-permute-start.39 = (bf16[512,128]{1,0:T(8,128)(2,1)S(1)}, bf16[512,128]{1,0:T(8,128)(2,1)S(1)}, u32[]{:S(2)}, u32[]{:S(2)}) collective-permute-start(bf16[512,128]{1,0:T(8,128)(2,1)S(1)} %get-tuple-element.33), channel_id=1, source_target_pairs={{0,4},{1,5},{4,8},{5,9},{8,12},{9,13},{12,14},{13,15},{14,10},{15,... | collective-permute-start | bytes 393224 | tf_op jit(solution)/shard_map/ppermute | solution.py:227
  155.4 2.0 %collective-permute-start.47 = (bf16[512,128]{1,0:T(8,128)(2,1)S(1)}, bf16[512,128]{1,0:T(8,128)(2,1)S(1)}, u32[]{:S(2)}, u32[]{:S(2)}) collective-permute-start(bf16[512,128]{1,0:T(8,128)(2,1)S(1)} %get-tuple-element.39), channel_id=1, source_target_pairs={{0,4},{1,5},{4,8},{5,9},{8,12},{9,13},{12,14},{13,15},{14,10},{15,... | collective-permute-start | bytes 393224 | tf_op jit(solution)/shard_map/ppermute | solution.py:227
  161.2 2.4 %collective-permute-start.63 = (bf16[512,128]{1,0:T(8,128)(2,1)S(1)}, bf16[512,128]{1,0:T(8,128)(2,1)S(1)}, u32[]{:S(2)}, u32[]{:S(2)}) collective-permute-start(bf16[512,128]{1,0:T(8,128)(2,1)S(1)} %get-tuple-element.25), channel_id=1, source_target_pairs={{0,4},{1,5},{4,8},{5,9},{8,12},{9,13},{12,14},{13,15},{14,10},{15,... | collective-permute-start | bytes 393224 | tf_op jit(solution)/shard_map/ppermute | solution.py:227
  164.0 2.2 %collective-permute-start.40 = (bf16[512,128]{1,0:T(8,128)(2,1)S(1)}, bf16[512,128]{1,0:T(8,128)(2,1)S(1)}, u32[]{:S(2)}, u32[]{:S(2)}) collective-permute-start(bf16[512,128]{1,0:T(8,128)(2,1)S(1)} %get-tuple-element.31), channel_id=1, source_target_pairs={{0,4},{1,5},{4,8},{5,9},{8,12},{9,13},{12,14},{13,15},{14,10},{15,... | collective-permute-start | bytes 393224 | tf_op jit(solution)/shard_map/ppermute | solution.py:227
  (234 shorter events, 61.3 us)
Async XLA Ops:
  3.9 13.8 %collective-permute-start.12 = (bf16[512,128]{1,0:T(8,128)(2,1)S(1)}, bf16[512,128]{1,0:T(8,128)(2,1)S(1)}, u32[]{:S(2)}, u32[]{:S(2)}) collective-permute-start(bf16[512,128]{1,0:T(8,128)(2,1)S(1)} %pad_maximum_fusion.4.refs_14_), channel_id=1, source_target_pairs={{4,0},{5,1},{8,4},{9,5},{12,8},{13,9},{14,12},{15,13},{10,14},{11,... | collective-permute-start | bytes 393224 | tf_op jit(solution)/shard_map/ppermute | solution.py:212
  6.9 12.5 %collective-permute-start.16 = (bf16[512,128]{1,0:T(8,128)(2,1)S(1)}, bf16[512,128]{1,0:T(8,128)(2,1)S(1)}, u32[]{:S(2)}, u32[]{:S(2)}) collective-permute-start(bf16[512,128]{1,0:T(8,128)(2,1)S(1)} %pad_maximum_fusion.4.refs_14_), channel_id=1, source_target_pairs={{0,4},{1,5},{4,8},{5,9},{8,12},{9,13},{12,14},{13,15},{14,10},{15,... | collective-permute-start | bytes 393224 | tf_op jit(solution)/shard_map/ppermute | solution.py:209
  7.1 9.0 %collective-permute-start.7 = (bf16[512,128]{1,0:T(8,128)(2,1)S(1)}, bf16[512,128]{1,0:T(8,128)(2,1)S(1)}, u32[]{:S(2)}, u32[]{:S(2)}) collective-permute-start(bf16[512,128]{1,0:T(8,128)(2,1)S(1)} %pad_maximum_fusion.3.refs_6_), channel_id=1, source_target_pairs={{0,4},{1,5},{4,8},{5,9},{8,12},{9,13},{12,14},{13,15},{14,10},{15,... | collective-permute-start | bytes 393224 | tf_op jit(solution)/shard_map/ppermute | solution.py:209
  9.1 10.8 %collective-permute-start.4 = (bf16[512,128]{1,0:T(8,128)(2,1)S(1)}, bf16[512,128]{1,0:T(8,128)(2,1)S(1)}, u32[]{:S(2)}, u32[]{:S(2)}) collective-permute-start(bf16[512,128]{1,0:T(8,128)(2,1)S(1)} %pad_maximum_fusion.3.refs_6_), channel_id=1, source_target_pairs={{4,0},{5,1},{8,4},{9,5},{12,8},{13,9},{14,12},{15,13},{10,14},{11,... | collective-permute-start | bytes 393224 | tf_op jit(solution)/shard_map/ppermute | solution.py:212
  9.2 11.1 %collective-permute-start.24 = (bf16[512,128]{1,0:T(8,128)(2,1)S(1)}, bf16[512,128]{1,0:T(8,128)(2,1)S(1)}, u32[]{:S(2)}, u32[]{:S(2)}) collective-permute-start(bf16[512,128]{1,0:T(8,128)(2,1)S(1)} %pad_maximum_fusion.5.refs_6_), channel_id=1, source_target_pairs={{0,4},{1,5},{4,8},{5,9},{8,12},{9,13},{12,14},{13,15},{14,10},{15,... | collective-permute-start | bytes 393224 | tf_op jit(solution)/shard_map/ppermute | solution.py:209
  19.9 8.8 %collective-permute-start.8 = (bf16[512,128]{1,0:T(8,128)(2,1)S(1)}, bf16[512,128]{1,0:T(8,128)(2,1)S(1)}, u32[]{:S(2)}, u32[]{:S(2)}) collective-permute-start(bf16[512,128]{1,0:T(8,128)(2,1)S(1)} %collective-permute-done.7.refs_13_), channel_id=1, source_target_pairs={{0,4},{1,5},{4,8},{5,9},{8,12},{9,13},{12,14},{13,15},{14,10},{15,... | collective-permute-start | bytes 393224 | tf_op jit(solution)/shard_map/ppermute | solution.py:209
  20.3 9.9 %collective-permute-start.13 = (bf16[512,128]{1,0:T(8,128)(2,1)S(1)}, bf16[512,128]{1,0:T(8,128)(2,1)S(1)}, u32[]{:S(2)}, u32[]{:S(2)}) collective-permute-start(bf16[512,128]{1,0:T(8,128)(2,1)S(1)} %collective-permute-done.12.refs_15_), channel_id=1, source_target_pairs={{4,0},{5,1},{8,4},{9,5},{12,8},{13,9},{14,12},{15,13},{10,14},{11,... | collective-permute-start | bytes 393224 | tf_op jit(solution)/shard_map/ppermute | solution.py:212
  32.4 28.9 %collective-permute-start = (bf16[256,1280]{1,0:T(8,128)(2,1)S(1)}, bf16[256,1280]{1,0:T(8,128)(2,1)S(1)}, u32[]{:S(2)}, u32[]{:S(2)}) collective-permute-start(bf16[256,1280]{1,0:T(8,128)(2,1)S(1)} %constant_dynamic-slice_fusion.10), channel_id=1, source_target_pairs={{0,1},{1,0},{2,3},{3,2},{4,5},{5,4},{6,7},{7,6},{8,9},{9,8},{10,11... | collective-permute-start | bytes 1966088 | tf_op jit(solution)/shard_map/ppermute | solution.py:268
  32.5 30.3 %collective-permute-start.1 = (bf16[256,1280]{1,0:T(8,128)(2,1)S(1)}, bf16[256,1280]{1,0:T(8,128)(2,1)S(1)}, u32[]{:S(2)}, u32[]{:S(2)}) collective-permute-start(bf16[256,1280]{1,0:T(8,128)(2,1)S(1)} %constant_dynamic-slice_fusion.9), channel_id=1, source_target_pairs={{0,1},{1,0},{2,3},{3,2},{4,5},{5,4},{6,7},{7,6},{8,9},{9,8},{10,11... | collective-permute-start | bytes 1966088 | tf_op jit(solution)/shard_map/ppermute | solution.py:268
  33.6 29.7 %collective-permute-start.2 = (bf16[256,1280]{1,0:T(8,128)(2,1)S(1)}, bf16[256,1280]{1,0:T(8,128)(2,1)}, u32[]{:S(2)}, u32[]{:S(2)}) collective-permute-start(bf16[256,1280]{1,0:T(8,128)(2,1)S(1)} %constant_dynamic-slice_fusion.8), channel_id=1, source_target_pairs={{0,1},{1,0},{2,3},{3,2},{4,5},{5,4},{6,7},{7,6},{8,9},{9,8},{10,11... | collective-permute-start | bytes 1966088 | tf_op jit(solution)/shard_map/ppermute | solution.py:268
  58.5 29.5 %collective-permute-start.23 = (bf16[512,128]{1,0:T(8,128)(2,1)}, bf16[512,128]{1,0:T(8,128)(2,1)S(1)}, u32[]{:S(2)}, u32[]{:S(2)}) collective-permute-start(bf16[512,128]{1,0:T(8,128)(2,1)} %collective-permute-done.22.refs_8_), channel_id=1, source_target_pairs={{4,0},{5,1},{8,4},{9,5},{12,8},{13,9},{14,12},{15,13},{10,14},{11,... | collective-permute-start | bytes 393224 | tf_op jit(solution)/shard_map/ppermute | solution.py:212
  60.8 27.2 %collective-permute-start.35 = (bf16[512,128]{1,0:T(8,128)(2,1)}, bf16[512,128]{1,0:T(8,128)(2,1)S(1)}, u32[]{:S(2)}, u32[]{:S(2)}) collective-permute-start(bf16[512,128]{1,0:T(8,128)(2,1)} %collective-permute-done.34.refs_20_), channel_id=1, source_target_pairs={{0,4},{1,5},{4,8},{5,9},{8,12},{9,13},{12,14},{13,15},{14,10},{15,... | collective-permute-start | bytes 393224 | tf_op jit(solution)/shard_map/ppermute | solution.py:209
  61.3 26.7 %collective-permute-start.27 = (bf16[512,128]{1,0:T(8,128)(2,1)}, bf16[512,128]{1,0:T(8,128)(2,1)S(1)}, u32[]{:S(2)}, u32[]{:S(2)}) collective-permute-start(bf16[512,128]{1,0:T(8,128)(2,1)} %collective-permute-done.26.refs_11_), channel_id=1, source_target_pairs={{0,4},{1,5},{4,8},{5,9},{8,12},{9,13},{12,14},{13,15},{14,10},{15,... | collective-permute-start | bytes 393224 | tf_op jit(solution)/shard_map/ppermute | solution.py:209
  62.8 25.2 %collective-permute-start.32 = (bf16[512,128]{1,0:T(8,128)(2,1)}, bf16[512,128]{1,0:T(8,128)(2,1)S(1)}, u32[]{:S(2)}, u32[]{:S(2)}) collective-permute-start(bf16[512,128]{1,0:T(8,128)(2,1)} %copy-done.31), channel_id=1, source_target_pairs={{4,0},{5,1},{8,4},{9,5},{12,8},{13,9},{14,12},{15,13},{10,14},{11,... | collective-permute-start | bytes 393224 | tf_op jit(solution)/shard_map/ppermute | solution.py:212
  83.0 41.1 %collective-permute-start.56 = (bf16[512,128]{1,0:T(8,128)(2,1)S(1)}, bf16[512,128]{1,0:T(8,128)(2,1)S(1)}, u32[]{:S(2)}, u32[]{:S(2)}) collective-permute-start(bf16[512,128]{1,0:T(8,128)(2,1)S(1)} %get-tuple-element.24), channel_id=1, source_target_pairs={{4,0},{5,1},{8,4},{9,5},{12,8},{13,9},{14,12},{15,13},{10,14},{11,... | collective-permute-start | bytes 393224 | tf_op jit(solution)/shard_map/ppermute | solution.py:231
  88.0 41.4 %collective-permute-start.53 = (bf16[512,128]{1,0:T(8,128)(2,1)S(1)}, bf16[512,128]{1,0:T(8,128)(2,1)S(1)}, u32[]{:S(2)}, u32[]{:S(2)}) collective-permute-start(bf16[512,128]{1,0:T(8,128)(2,1)S(1)} %get-tuple-element.23), channel_id=1, source_target_pairs={{0,4},{1,5},{4,8},{5,9},{8,12},{9,13},{12,14},{13,15},{14,10},{15,... | collective-permute-start | bytes 393224 | tf_op jit(solution)/shard_map/ppermute | solution.py:227
  109.1 15.3 %collective-permute-start.64 = (bf16[512,128]{1,0:T(8,128)(2,1)S(1)}, bf16[512,128]{1,0:T(8,128)(2,1)S(1)}, u32[]{:S(2)}, u32[]{:S(2)}) collective-permute-start(bf16[512,128]{1,0:T(8,128)(2,1)S(1)} %get-tuple-element.30), channel_id=1, source_target_pairs={{4,0},{5,1},{8,4},{9,5},{12,8},{13,9},{14,12},{15,13},{10,14},{11,... | collective-permute-start | bytes 393224 | tf_op jit(solution)/shard_map/ppermute | solution.py:231
  114.7 21.0 %collective-permute-start.61 = (bf16[512,128]{1,0:T(8,128)(2,1)S(1)}, bf16[512,128]{1,0:T(8,128)(2,1)S(1)}, u32[]{:S(2)}, u32[]{:S(2)}) collective-permute-start(bf16[512,128]{1,0:T(8,128)(2,1)S(1)} %get-tuple-element.29), channel_id=1, source_target_pairs={{0,4},{1,5},{4,8},{5,9},{8,12},{9,13},{12,14},{13,15},{14,10},{15,... | collective-permute-start | bytes 393224 | tf_op jit(solution)/shard_map/ppermute | solution.py:227
  114.8 12.6 %collective-permute-start.37 = (bf16[512,128]{1,0:T(8,128)(2,1)S(1)}, bf16[512,128]{1,0:T(8,128)(2,1)S(1)}, u32[]{:S(2)}, u32[]{:S(2)}) collective-permute-start(bf16[512,128]{1,0:T(8,128)(2,1)S(1)} %get-tuple-element.35), channel_id=1, source_target_pairs={{0,4},{1,5},{4,8},{5,9},{8,12},{9,13},{12,14},{13,15},{14,10},{15,... | collective-permute-start | bytes 393224 | tf_op jit(solution)/shard_map/ppermute | solution.py:227
  124.2 18.6 %collective-permute-start.41 = (bf16[512,128]{1,0:T(8,128)(2,1)S(1)}, bf16[512,128]{1,0:T(8,128)(2,1)S(1)}, u32[]{:S(2)}, u32[]{:S(2)}) collective-permute-start(bf16[512,128]{1,0:T(8,128)(2,1)S(1)} %get-tuple-element.36), channel_id=1, source_target_pairs={{4,0},{5,1},{8,4},{9,5},{12,8},{13,9},{14,12},{15,13},{10,14},{11,... | collective-permute-start | bytes 393224 | tf_op jit(solution)/shard_map/ppermute | solution.py:231
  127.4 21.5 %collective-permute-start.49 = (bf16[512,128]{1,0:T(8,128)(2,1)S(1)}, bf16[512,128]{1,0:T(8,128)(2,1)S(1)}, u32[]{:S(2)}, u32[]{:S(2)}) collective-permute-start(bf16[512,128]{1,0:T(8,128)(2,1)S(1)} %get-tuple-element.42), channel_id=1, source_target_pairs={{4,0},{5,1},{8,4},{9,5},{12,8},{13,9},{14,12},{15,13},{10,14},{11,... | collective-permute-start | bytes 393224 | tf_op jit(solution)/shard_map/ppermute | solution.py:231
  129.4 22.3 %collective-permute-start.19 = (bf16[256,640]{1,0:T(8,128)(2,1)S(1)}, bf16[256,640]{1,0:T(8,128)(2,1)S(1)}, u32[]{:S(2)}, u32[]{:S(2)}) collective-permute-start(bf16[256,640]{1,0:T(8,128)(2,1)S(1)} %copy-done.15), channel_id=1, source_target_pairs={{0,1},{1,0},{2,3},{3,2},{4,5},{5,4},{6,7},{7,6},{8,9},{9,8},{10,11... | collective-permute-start | bytes 983048 | tf_op jit(solution)/shard_map/ppermute | solution.py:276
  135.8 16.0 %collective-permute-start.36 = (bf16[256,640]{1,0:T(8,128)(2,1)S(1)}, bf16[256,640]{1,0:T(8,128)(2,1)S(1)}, u32[]{:S(2)}, u32[]{:S(2)}) collective-permute-start(bf16[256,640]{1,0:T(8,128)(2,1)S(1)} %copy-done.16), channel_id=1, source_target_pairs={{0,1},{1,0},{2,3},{3,2},{4,5},{5,4},{6,7},{7,6},{8,9},{9,8},{10,11... | collective-permute-start | bytes 983048 | tf_op jit(solution)/shard_map/ppermute | solution.py:276
  146.8 8.6 %collective-permute-start.54 = (bf16[512,128]{1,0:T(8,128)(2,1)S(1)}, bf16[512,128]{1,0:T(8,128)(2,1)S(1)}, u32[]{:S(2)}, u32[]{:S(2)}) collective-permute-start(bf16[512,128]{1,0:T(8,128)(2,1)S(1)} %get-tuple-element.21), channel_id=1, source_target_pairs={{0,4},{1,5},{4,8},{5,9},{8,12},{9,13},{12,14},{13,15},{14,10},{15,... | collective-permute-start | bytes 393224 | tf_op jit(solution)/shard_map/ppermute | solution.py:227
  (83 other events, 801.4 us)

commit v3 on v2

v3 whole, which is shorter than its diff:
```python
import functools
import math

import jax
import jax.numpy as jnp
from jax import lax
from jax.experimental import pallas as pl
from jax.experimental.pallas import tpu as pltpu
from jax.sharding import PartitionSpec as P

HQ = 20
HK = 4
DH = 128
PER = HQ // HK
HALF = HK // 2
WIDE = PER * DH
ANCESTORS = 5
SLOTS = ANCESTORS + 1
SCALE = 1.0 / math.sqrt(DH)
EXP_SCALE = SCALE / math.log(2.0)
NN = (((1,), (0,)), ((), ()))


def dot(a, b):
    return lax.dot_general(a, b, NN, preferred_element_type=jnp.float32)


def ring_order(chips):
    if chips == 8:
        return [0, 2, 4, 6, 7, 5, 3, 1]
    return list(range(chips))


def walk(device, me, places, parents, assignment, lengths, owner, block, reach, side):
    chips = places.shape[0]
    here = places[me // 2]

    def place(held):
        ahead = places[held // 2] - here
        ahead = jnp.where(ahead < 0, ahead + chips, ahead)
        return ahead * 2 + jnp.where(held % 2 == me % 2, 0, 1)

    segment = assignment[device]
    block[side, 0] = place(device)
    reach[side, 0] = lengths[segment]
    depth = jnp.int32(0)
    up = parents[segment]
    for slot in range(1, SLOTS):
        usable = up >= 0
        at = jnp.maximum(up, 0)
        block[side, slot] = place(owner[at])
        reach[side, slot] = lengths[at]
        depth = depth + usable.astype(jnp.int32)
        up = jnp.where(usable, parents[at], -1)
    block[side, SLOTS] = depth + 1


def kernel(chips, head, me_ref, places, parents, assignment, lengths, *refs):
    mine, refs = refs[:3], refs[3:]
    other_ref, refs = refs[0], refs[1:]
    kv_in, refs = refs[:chips + 1], refs[chips + 1:]
    sum_ref, up_ref, down_ref, dq_mine, dq_other = refs[:5]
    (owner, block, reach, q_ref, g_ref, o_ref, qt_ref, gt_ref, kv_ref, total_ref,
     s_ref, kt_ref, dqt_ref, sems) = refs[5:]
    rows = dq_mine.shape[0]
    far = chips // 2
    me = me_ref[0]

    copies = []
    for at, held in enumerate((q_ref, g_ref, o_ref)):
        for h in range(PER):
            column = pl.multiple_of(((me % 2 * HALF + head) * PER + h) * DH, DH)
            copies.append((mine[at].at[:, pl.ds(column, DH)], held.at[0, h]))
            column = ((at * HALF + head) * PER + h) * DH
            copies.append((other_ref.at[:, column:column + DH], held.at[1, h]))
    blocks = [at for at in range(chips) if at != far]
    for at, held in zip(blocks, kv_in):
        copies.append((held, kv_ref.at[at]))
    copies.append((kv_in[chips - 1], kv_ref.at[far, :rows]))
    copies.append((kv_in[chips], kv_ref.at[far, rows:]))
    copies = [pltpu.make_async_copy(a, b, sems.at[i]) for i, (a, b) in enumerate(copies)]
    for copy in copies:
        copy.start()

    def invert(d, carry):
        owner[assignment[d]] = d
        return carry

    lax.fori_loop(0, assignment.shape[0], invert, 0)
    walk(me, me, places, parents, assignment, lengths, owner, block, reach, 0)
    walk(me + 1 - me % 2 * 2, me, places, parents, assignment, lengths, owner, block, reach, 1)

    def clear(at, carry):
        total_ref[at] = jnp.zeros(total_ref.shape[1:], total_ref.dtype)
        return carry

    lax.fori_loop(0, chips, clear, 0)
    row_at = lax.broadcasted_iota(jnp.int32, (rows, 1), 0)
    lane_at = lax.broadcasted_iota(jnp.int32, (1, PER * rows), 1) % rows
    key_at = lax.broadcasted_iota(jnp.int32, (rows, 1), 0)
    for copy in copies:
        copy.wait()

    for side, dq_ref in enumerate((dq_mine, dq_other)):
        slots = block[side, SLOTS]
        delta = []
        for h in range(PER):
            masked = jnp.where(row_at < reach[side, 0], g_ref[side, h], jnp.zeros((), g_ref.dtype))
            g_ref[side, h] = masked
            gt_ref[:, h * rows:(h + 1) * rows] = masked.T
            qt_ref[:, h * rows:(h + 1) * rows] = q_ref[side, h].T
            terms = masked.astype(jnp.float32) * o_ref[side, h].astype(jnp.float32)
            delta.append(jnp.sum(terms.T, axis=0, keepdims=True))
        delta = jnp.concatenate(delta, axis=1)

        def key_rows(ref, slot):
            at = block[side, slot]
            first = pl.multiple_of(at % 2 * rows, rows)
            return ref.at[at // 2, pl.ds(first, rows)]

        def fold(x, op):
            return op(x.reshape(rows // 8, 8, PER * rows), axis=0)

        def scores(slot, highest):
            k = key_rows(kv_ref, slot)[:, :DH]
            kt_ref[slot] = k.T
            limit = jnp.where(slot == 0, lane_at, reach[side, slot] - 1)
            s = jnp.where(key_at <= limit, dot(k, qt_ref[...]), -1e30)
            s_ref[slot] = s
            return jnp.maximum(highest, fold(s, jnp.max))

        highest = jnp.full((8, PER * rows), -1e30, jnp.float32)
        highest = lax.fori_loop(0, slots, scores, highest)
        highest = jnp.max(highest, axis=0, keepdims=True)

        def weigh(slot, total):
            w = jnp.exp2((s_ref[slot] - highest) * EXP_SCALE)
            s_ref[slot] = w
            return total + fold(w, jnp.sum)

        total = jnp.zeros((8, PER * rows), jnp.float32)
        total = lax.fori_loop(0, slots, weigh, total)
        inverse = 1.0 / jnp.sum(total, axis=0, keepdims=True)
        dqt_ref[...] = jnp.zeros_like(dqt_ref)

        def grads(slot, carry):
            v = key_rows(kv_ref, slot)[:, DH:]
            p = s_ref[slot] * inverse
            ds = (p * (dot(v, gt_ref[...]) - delta)).astype(jnp.bfloat16)
            into = key_rows(total_ref, slot)
            into[:, DH:] += dot(p.astype(jnp.bfloat16), g_ref[side].reshape(PER * rows, DH))
            into[:, :DH] += dot(ds, q_ref[side].reshape(PER * rows, DH))
            dqt_ref[...] += dot(kt_ref[slot], ds)
            return carry

        lax.fori_loop(0, slots, grads, 0)
        for h in range(PER):
            dq = dqt_ref[:, h * rows:(h + 1) * rows].T * SCALE
            dq_ref[:, h * DH:(h + 1) * DH] = dq.astype(dq_ref.dtype)

    def finish(at, carry):
        sum_ref[at, :, :DH] = (total_ref[at, :, :DH] * SCALE).astype(sum_ref.dtype)
        sum_ref[at, :, DH:] = total_ref[at, :, DH:].astype(sum_ref.dtype)
        return carry

    lax.fori_loop(0, chips, finish, 0)
    up_ref[...] = sum_ref[far, :rows]
    down_ref[...] = sum_ref[far, rows:]


def attend(head, tables, mine, other, blocks):
    rows = other.shape[0]
    chips = len(blocks) - 1
    devices = 2 * chips
    smem = pl.BlockSpec(memory_space=pltpu.SMEM)
    hbm = pl.BlockSpec(memory_space=pl.ANY)
    vmem = pl.BlockSpec(memory_space=pltpu.VMEM)
    bf16, f32 = jnp.bfloat16, jnp.float32
    work = 2 * 5 * 5 * PER * rows * rows * DH * 2
    return pl.pallas_call(
        functools.partial(kernel, chips, head),
        in_specs=[smem] * 5 + [hbm] * (4 + chips + 1),
        out_specs=[vmem] * 5,
        out_shape=[
            jax.ShapeDtypeStruct((chips, 2 * rows, 2 * DH), bf16),
            jax.ShapeDtypeStruct((rows, 2 * DH), bf16),
            jax.ShapeDtypeStruct((rows, 2 * DH), bf16),
            jax.ShapeDtypeStruct((rows, WIDE), bf16),
            jax.ShapeDtypeStruct((rows, WIDE), bf16),
        ],
        scratch_shapes=[
            pltpu.SMEM((devices,), jnp.int32),
            pltpu.SMEM((2, SLOTS + 1), jnp.int32),
            pltpu.SMEM((2, SLOTS), jnp.int32),
            pltpu.VMEM((2, PER, rows, DH), bf16),
            pltpu.VMEM((2, PER, rows, DH), bf16),
            pltpu.VMEM((2, PER, rows, DH), bf16),
            pltpu.VMEM((DH, PER * rows), bf16),
            pltpu.VMEM((DH, PER * rows), bf16),
            pltpu.VMEM((chips, 2 * rows, 2 * DH), bf16),
            pltpu.VMEM((chips, 2 * rows, 2 * DH), f32),
            pltpu.VMEM((SLOTS, rows, PER * rows), f32),
            pltpu.VMEM((SLOTS, DH, rows), bf16),
            pltpu.VMEM((DH, PER * rows), f32),
            pltpu.SemaphoreType.DMA((6 * PER + chips + 1,)),
        ],
        compiler_params=pltpu.CompilerParams(vmem_limit_bytes=56 * 1024 * 1024),
        cost_estimate=pl.CostEstimate(flops=work, bytes_accessed=8 << 20, transcendentals=0),
    )(*tables, *mine, other, *blocks)


def spread(block, right, left, chips):
    far, rows = chips // 2, block.shape[0] // 2
    got = {0: block}
    up = down = block
    for step in range(1, far):
        up = got[chips - step] = lax.ppermute(up, "leaf", right)
        down = got[step] = lax.ppermute(down, "leaf", left)
    up = lax.ppermute(up[:rows], "leaf", right)
    down = lax.ppermute(down[rows:], "leaf", left)
    return [got[at] for at in range(chips) if at != far] + [up, down]


def wide(x):
    return x.astype(jnp.float32)


def collect(terms, up, down, right, left):
    chips, rows = terms.shape[0], up.shape[0]
    up = lax.ppermute(up, "leaf", right)
    down = lax.ppermute(down, "leaf", left)
    up = jnp.pad(wide(up), ((0, rows), (0, 0)))
    down = jnp.pad(wide(down), ((rows, 0), (0, 0)))
    for step in range(chips // 2 - 1, 0, -1):
        up = wide(lax.ppermute((up + wide(terms[step])).astype(terms.dtype), "leaf", right))
        down = wide(lax.ppermute((down + wide(terms[chips - step])).astype(terms.dtype), "leaf", left))
    return (wide(terms[0]) + up + down).astype(terms.dtype)


def local(queries, keys, values, saved_out, grad_out, parents, assignment, lengths):
    rows = keys.shape[0]
    chips = lax.axis_size("leaf") // 2
    order = ring_order(chips)
    ahead = [(order[i], order[(i + 1) % chips]) for i in range(chips)]
    right = [(2 * a + c, 2 * b + c) for a, b in ahead for c in range(2)]
    left = [(b, a) for a, b in right]
    swap = [(2 * a + c, 2 * a + 1 - c) for a in range(chips) for c in range(2)]
    places = jnp.asarray([order.index(chip) for chip in range(chips)], jnp.int32)
    index = lax.axis_index("leaf").astype(jnp.int32)
    core = index % 2
    tables = (index.reshape(1), places, parents, assignment, lengths)

    def part(array, which, width):
        return lax.dynamic_slice(array, (0, which * width), (rows, width))

    def heads_of(which):
        pieces = [part(array, which * HALF + head, DH) for head in range(HALF) for array in (keys, values)]
        return jnp.concatenate(pieces, axis=1)

    kept = heads_of(core)
    got = lax.ppermute(heads_of(1 - core), "leaf", swap)
    gathered = []
    for head in range(HALF):
        cols = slice(head * 2 * DH, (head + 1) * 2 * DH)
        block = jnp.concatenate([kept[:, cols], got[:, cols]], axis=0)
        gathered.append(spread(block, right, left, chips))
    mine = (queries, grad_out, saved_out)
    other = jnp.concatenate([part(array, 1 - core, HALF * WIDE) for array in mine], axis=1)
    other = lax.ppermute(other, "leaf", swap)
    sums, ours, theirs = [], [], []
    for head in range(HALF):
        terms, up, down, dq_mine, dq_other = attend(head, tables, mine, other, gathered[head])
        sums.append(collect(terms, up, down, right, left))
        ours.append(dq_mine)
        theirs.append(lax.ppermute(dq_other, "leaf", swap))

    def whole(kept, got):
        low = [jnp.where(core == 0, a, b) for a, b in zip(kept, got)]
        high = [jnp.where(core == 0, b, a) for a, b in zip(kept, got)]
        return jnp.concatenate(low + high, axis=1)

    sums = jnp.concatenate(sums, axis=1)
    kept, got = sums[:rows], lax.ppermute(sums[rows:], "leaf", swap)

    def owned(first):
        columns = [slice((2 * head + first) * DH, (2 * head + first + 1) * DH) for head in range(HALF)]
        return whole([kept[:, c] for c in columns], [got[:, c] for c in columns])

    return (whole(ours, theirs), owned(0), owned(1))


def solution(mesh):
    tokens = P(("groups", "leaf"), None)
    tables = P("groups")
    return jax.shard_map(
        local,
        mesh=mesh,
        in_specs=(tokens,) * 5 + (tables,) * 3,
        out_specs=(tokens,) * 3,
        check_vma=False,
    )
```

time: 178 us -> 140 us (0.79); the launches traced: 176 us -> 141 us
  starting transfers between devices: 73.1 us -> 40.1 us
  other arithmetic: 4.71 us -> 9.14 us
  local copies, waits for them, and re-layouts: 8.42 us -> 4.95 us
  waiting for transfers between devices: 51 us -> 48.9 us
    ppermute x14 -> x2, starting transfers between devices: 31.1 us -> 8.91 us  [collect(): up = lax.ppermute(up, 'leaf', right)]
    ppermute x39 -> x31, waiting for transfers between devices: 29.5 us -> 44.7 us  [the longest x6 22.1 us: spread(): up = got[chips - step] = lax.ppermute(up, 'leaf', right)]
    ppermute x14 -> x2, waiting for transfers between devices: 16.8 us -> 2.07 us  [collect(): down = lax.ppermute(down, 'leaf', left)]
    ppermute x14 -> x2, starting transfers between devices: 11.6 us -> 0.01 us  [collect(): down = lax.ppermute(down, 'leaf', left)]
    convert_element_type x16 -> x8, other arithmetic: 1.85 us -> 6.11 us  [the longest x6 4.97 us: collect(): (up + wide(terms[step])).astype(terms.dtype)]
    squeeze x4 -> x0, local copies, waits for them, and re-layouts: 3.12 us -> none  [collect(): up = terms[steps_right]]
    ppermute x14 -> x2, waiting for transfers between devices: 4.69 us -> 2.1 us  [collect(): up = lax.ppermute(up, 'leaf', right)]
    ppermute x39 -> x31, starting transfers between devices: 30.3 us -> 30.7 us  [the longest x6 13.5 us: spread(): up = got[chips - step] = lax.ppermute(up, 'leaf', right)]
  transfers between devices with their start and end apart: 69 -> 37, of which waited for: 26 -> 21; matrix products, arithmetic and copies ran while one was open for 5% -> 5% of each run, Pallas kernels for 21% -> 26%
where the time goes in v3:
time: 140 us; the launch traced here: 141 us
  waiting for transfers between devices  48.9 us (35%)
  starting transfers between devices  40.1 us (29%)
  Pallas kernels  37 us (26%)
  other arithmetic  9.14 us (7%)
  local copies, waits for them, and re-layouts  4.95 us (4%)
    pallas_call x2, Pallas kernels, attend(): pl.pallas_call(functools.partial(kernel, chips, head), in_specs=[smem] *...  37 us
    ppermute x6, waiting for transfers between devices, spread(): up = got[chips - step] = lax.ppermute(up, 'leaf', right)  22.1 us
    ppermute x6, starting transfers between devices, spread(): up = got[chips - step] = lax.ppermute(up, 'leaf', right)  13.5 us
    ppermute x2, starting transfers between devices, collect(): up = lax.ppermute(up, 'leaf', right)  8.91 us
    ppermute x6, waiting for transfers between devices, collect(): lax.ppermute((down + wide(terms[chips - step])).astype(terms.dtype), 'lea...  8.74 us
    ppermute x6, waiting for transfers between devices, collect(): lax.ppermute((up + wide(terms[step])).astype(terms.dtype), 'leaf', right)  8.13 us
    ppermute x6, starting transfers between devices, collect(): lax.ppermute((down + wide(terms[chips - step])).astype(terms.dtype), 'lea...  6.08 us
    ppermute x6, starting transfers between devices, collect(): lax.ppermute((up + wide(terms[step])).astype(terms.dtype), 'leaf', right)  5.47 us
  transfers between devices with their start and end apart: 37, of which 21 were waited for; matrix products, arithmetic and copies ran while one was open for 5% of the time, Pallas kernels for 26%

profile of v3, /device:TPU:0, one launch (start us, length us, event | category | flops | bytes accessed | tf_op | source)
XLA Modules:
  0.0 141.1 jit_solution(15292834739366497383)
XLA Ops:
  4.9 3.0 %collective-permute-done.1 = bf16[256,512]{1,0:T(8,128)(2,1)S(1)} collective-permute-done((bf16[256,512]{1,0:T(8,128)(2,1)S(1)}, bf16[256,512]{1,0:T(8,128)(2,1)S(1)}, u32[]{:S(2)}, u32[]{:S(2)}) %collective-permute-start.1) | collective-permute-done | bytes 262176 | tf_op jit(solution)/shard_map/ppermute | solution.py:261
  7.9 3.0 %collective-permute-start.5 = (bf16[512,256]{1,0:T(8,128)(2,1)S(1)}, bf16[512,256]{1,0:T(8,128)(2,1)S(1)}, u32[]{:S(2)}, u32[]{:S(2)}) collective-permute-start(bf16[512,256]{1,0:T(8,128)(2,1)S(1)} %pad_maximum_fusion.4.refs_4_), channel_id=1, source_target_pairs={{0,4},{1,5},{4,8},{5,9},{8,12},{9,13},{12,14},{13,15},{14,10},{15,... | collective-permute-start | bytes 786440 | tf_op jit(solution)/shard_map/ppermute | solution.py:217
  10.9 2.1 %collective-permute-start.14 = (bf16[512,256]{1,0:T(8,128)(2,1)S(1)}, bf16[512,256]{1,0:T(8,128)(2,1)S(1)}, u32[]{:S(2)}, u32[]{:S(2)}) collective-permute-start(bf16[512,256]{1,0:T(8,128)(2,1)S(1)} %pad_maximum_fusion.5.refs_4_), channel_id=1, source_target_pairs={{0,4},{1,5},{4,8},{5,9},{8,12},{9,13},{12,14},{13,15},{14,10},{15,... | collective-permute-start | bytes 786440 | tf_op jit(solution)/shard_map/ppermute | solution.py:217
  13.0 4.9 %collective-permute-done.5.refs_10_ = bf16[512,256]{1,0:T(8,128)(2,1)S(1)} collective-permute-done((bf16[512,256]{1,0:T(8,128)(2,1)S(1)}, bf16[512,256]{1,0:T(8,128)(2,1)S(1)}, u32[]{:S(2)}, u32[]{:S(2)}) %collective-permute-start.5) | collective-permute-done | bytes 262176 | tf_op jit(solution)/shard_map/ppermute | solution.py:217
  17.9 2.1 %collective-permute-start.6 = (bf16[512,256]{1,0:T(8,128)(2,1)S(1)}, bf16[512,256]{1,0:T(8,128)(2,1)S(1)}, u32[]{:S(2)}, u32[]{:S(2)}) collective-permute-start(bf16[512,256]{1,0:T(8,128)(2,1)S(1)} %collective-permute-done.5.refs_10_), channel_id=1, source_target_pairs={{0,4},{1,5},{4,8},{5,9},{8,12},{9,13},{12,14},{13,15},{14,10},{15,... | collective-permute-start | bytes 786440 | tf_op jit(solution)/shard_map/ppermute | solution.py:217
  20.1 3.5 %collective-permute-done.14.refs_10_ = bf16[512,256]{1,0:T(8,128)(2,1)S(1)} collective-permute-done((bf16[512,256]{1,0:T(8,128)(2,1)S(1)}, bf16[512,256]{1,0:T(8,128)(2,1)S(1)}, u32[]{:S(2)}, u32[]{:S(2)}) %collective-permute-start.14) | collective-permute-done | bytes 262176 | tf_op jit(solution)/shard_map/ppermute | solution.py:217
  23.5 2.1 %collective-permute-start.15 = (bf16[512,256]{1,0:T(8,128)(2,1)S(1)}, bf16[512,256]{1,0:T(8,128)(2,1)S(1)}, u32[]{:S(2)}, u32[]{:S(2)}) collective-permute-start(bf16[512,256]{1,0:T(8,128)(2,1)S(1)} %collective-permute-done.14.refs_10_), channel_id=1, source_target_pairs={{0,4},{1,5},{4,8},{5,9},{8,12},{9,13},{12,14},{13,15},{14,10},{15,... | collective-permute-start | bytes 786440 | tf_op jit(solution)/shard_map/ppermute | solution.py:217
  25.7 3.5 %collective-permute-done.6.refs_9_ = bf16[512,256]{1,0:T(8,128)(2,1)S(1)} collective-permute-done((bf16[512,256]{1,0:T(8,128)(2,1)S(1)}, bf16[512,256]{1,0:T(8,128)(2,1)S(1)}, u32[]{:S(2)}, u32[]{:S(2)}) %collective-permute-start.6) | collective-permute-done | bytes 262176 | tf_op jit(solution)/shard_map/ppermute | solution.py:217
  29.2 2.1 %collective-permute-start.7 = (bf16[512,256]{1,0:T(8,128)(2,1)S(1)}, bf16[512,256]{1,0:T(8,128)(2,1)S(1)}, u32[]{:S(2)}, u32[]{:S(2)}) collective-permute-start(bf16[512,256]{1,0:T(8,128)(2,1)S(1)} %collective-permute-done.6.refs_9_), channel_id=1, source_target_pairs={{0,4},{1,5},{4,8},{5,9},{8,12},{9,13},{12,14},{13,15},{14,10},{15,... | collective-permute-start | bytes 786440 | tf_op jit(solution)/shard_map/ppermute | solution.py:217
  31.3 3.5 %collective-permute-done.15.refs_9_ = bf16[512,256]{1,0:T(8,128)(2,1)S(1)} collective-permute-done((bf16[512,256]{1,0:T(8,128)(2,1)S(1)}, bf16[512,256]{1,0:T(8,128)(2,1)S(1)}, u32[]{:S(2)}, u32[]{:S(2)}) %collective-permute-start.15) | collective-permute-done | bytes 262176 | tf_op jit(solution)/shard_map/ppermute | solution.py:217
  34.8 2.1 %collective-permute-start.16 = (bf16[512,256]{1,0:T(8,128)(2,1)S(1)}, bf16[512,256]{1,0:T(8,128)(2,1)S(1)}, u32[]{:S(2)}, u32[]{:S(2)}) collective-permute-start(bf16[512,256]{1,0:T(8,128)(2,1)S(1)} %collective-permute-done.15.refs_9_), channel_id=1, source_target_pairs={{0,4},{1,5},{4,8},{5,9},{8,12},{9,13},{12,14},{13,15},{14,10},{15,... | collective-permute-start | bytes 786440 | tf_op jit(solution)/shard_map/ppermute | solution.py:217
  36.9 3.5 %collective-permute-done.7.refs_8_ = bf16[512,256]{1,0:T(8,128)(2,1)S(1)} collective-permute-done((bf16[512,256]{1,0:T(8,128)(2,1)S(1)}, bf16[512,256]{1,0:T(8,128)(2,1)S(1)}, u32[]{:S(2)}, u32[]{:S(2)}) %collective-permute-start.7) | collective-permute-done | bytes 262176 | tf_op jit(solution)/shard_map/ppermute | solution.py:217
  40.4 2.2 %collective-permute-start.8 = (bf16[256,256]{1,0:T(8,128)(2,1)S(1)}, bf16[256,256]{1,0:T(8,128)(2,1)S(1)}, u32[]{:S(2)}, u32[]{:S(2)}) collective-permute-start(bf16[256,256]{1,0:T(8,128)(2,1)S(1)} %slice.130), channel_id=1, source_target_pairs={{0,4},{1,5},{4,8},{5,9},{8,12},{9,13},{12,14},{13,15},{14,10},{15,... | collective-permute-start | bytes 393224 | tf_op jit(solution)/shard_map/ppermute | solution.py:219
  42.7 3.3 %collective-permute-done.16.refs_8_ = bf16[512,256]{1,0:T(8,128)(2,1)S(1)} collective-permute-done((bf16[512,256]{1,0:T(8,128)(2,1)S(1)}, bf16[512,256]{1,0:T(8,128)(2,1)S(1)}, u32[]{:S(2)}, u32[]{:S(2)}) %collective-permute-start.16) | collective-permute-done | bytes 262176 | tf_op jit(solution)/shard_map/ppermute | solution.py:217
  46.0 2.2 %collective-permute-start.17 = (bf16[256,256]{1,0:T(8,128)(2,1)S(1)}, bf16[256,256]{1,0:T(8,128)(2,1)S(1)}, u32[]{:S(2)}, u32[]{:S(2)}) collective-permute-start(bf16[256,256]{1,0:T(8,128)(2,1)S(1)} %slice.133), channel_id=1, source_target_pairs={{0,4},{1,5},{4,8},{5,9},{8,12},{9,13},{12,14},{13,15},{14,10},{15,... | collective-permute-start | bytes 393224 | tf_op jit(solution)/shard_map/ppermute | solution.py:219
  51.2 18.5 %shard_map.112 = (bf16[8,512,256]{2,1,0:T(8,128)(2,1)}, bf16[256,256]{1,0:T(8,128)(2,1)}, bf16[256,256]{1,0:T(8,128)(2,1)}, bf16[256,640]{1,0:T(8,128)(2,1)}, bf16[256,640]{1,0:T(8,128)(2,1)}) custom-call(s32[1]{0:T(128)} %bitcast.me_ref, s32[8]{0:T(128)} %constant.35.clone.places, s32[16]{0:T(128)} %parents.3, s32[16]{0:T(128)} %assignment.3, s32[16]{0:T(128)} %lengths.3, ...), custom_call_target="tpu_custom_call" | custom-call | flops 4194304000 | bytes 8388608 | tf_op jit(solution)/shard_map/pallas_call | solution.py:180
  69.8 4.2 %collective-permute-start.20 = (bf16[256,256]{1,0:T(8,128)(2,1)}, bf16[256,256]{1,0:T(8,128)(2,1)S(1)}, u32[]{:S(2)}, u32[]{:S(2)}) collective-permute-start(bf16[256,256]{1,0:T(8,128)(2,1)} %get-tuple-element.18), channel_id=1, source_target_pairs={{0,4},{1,5},{4,8},{5,9},{8,12},{9,13},{12,14},{13,15},{14,10},{15,... | collective-permute-start | bytes 393224 | tf_op jit(solution)/shard_map/ppermute | solution.py:230
  75.3 18.5 %shard_map.113 = (bf16[8,512,256]{2,1,0:T(8,128)(2,1)}, bf16[256,256]{1,0:T(8,128)(2,1)}, bf16[256,256]{1,0:T(8,128)(2,1)}, bf16[256,640]{1,0:T(8,128)(2,1)}, bf16[256,640]{1,0:T(8,128)(2,1)}) custom-call(s32[1]{0:T(128)} %bitcast.me_ref, s32[8]{0:T(128)} %constant.35.clone.places, s32[16]{0:T(128)} %parents.3, s32[16]{0:T(128)} %assignment.3, s32[16]{0:T(128)} %lengths.3, ...), custom_call_target="tpu_custom_call" | custom-call | flops 4194304000 | bytes 8388608 | tf_op jit(solution)/shard_map/pallas_call | solution.py:180
  93.8 4.7 %collective-permute-start.28 = (bf16[256,256]{1,0:T(8,128)(2,1)}, bf16[256,256]{1,0:T(8,128)(2,1)S(1)}, u32[]{:S(2)}, u32[]{:S(2)}) collective-permute-start(bf16[256,256]{1,0:T(8,128)(2,1)} %get-tuple-element.21), channel_id=1, source_target_pairs={{0,4},{1,5},{4,8},{5,9},{8,12},{9,13},{12,14},{13,15},{14,10},{15,... | collective-permute-start | bytes 393224 | tf_op jit(solution)/shard_map/ppermute | solution.py:230
  98.6 2.1 %collective-permute-start.21 = (bf16[512,256]{1,0:T(8,128)(2,1)S(1)}, bf16[512,256]{1,0:T(8,128)(2,1)}, u32[]{:S(2)}, u32[]{:S(2)}) collective-permute-start(bf16[512,256]{1,0:T(8,128)(2,1)S(1)} %get-tuple-element.27), channel_id=1, source_target_pairs={{0,4},{1,5},{4,8},{5,9},{8,12},{9,13},{12,14},{13,15},{14,10},{15,... | collective-permute-start | bytes 786440 | tf_op jit(solution)/shard_map/ppermute | solution.py:235
  100.7 2.1 %collective-permute-done.28 = bf16[256,256]{1,0:T(8,128)(2,1)S(1)} collective-permute-done((bf16[256,256]{1,0:T(8,128)(2,1)}, bf16[256,256]{1,0:T(8,128)(2,1)S(1)}, u32[]{:S(2)}, u32[]{:S(2)}) %collective-permute-start.28) | collective-permute-done | bytes 131104 | tf_op jit(solution)/shard_map/ppermute | solution.py:230
  102.8 2.1 %collective-permute-done.32 = bf16[256,256]{1,0:T(8,128)(2,1)S(1)} collective-permute-done((bf16[256,256]{1,0:T(8,128)(2,1)}, bf16[256,256]{1,0:T(8,128)(2,1)S(1)}, u32[]{:S(2)}, u32[]{:S(2)}) %collective-permute-start.32) | collective-permute-done | bytes 131104 | tf_op jit(solution)/shard_map/ppermute | solution.py:231
  116.8 3.4 %collective-permute-done.22 = bf16[512,256]{1,0:T(8,128)(2,1)S(1)} collective-permute-done((bf16[512,256]{1,0:T(8,128)(2,1)S(1)}, bf16[512,256]{1,0:T(8,128)(2,1)S(1)}, u32[]{:S(2)}, u32[]{:S(2)}) %collective-permute-start.22) | collective-permute-done | bytes 262176 | tf_op jit(solution)/shard_map/ppermute | solution.py:235
  130.7 2.3 %collective-permute-done.27 = bf16[512,256]{1,0:T(8,128)(2,1)S(1)} collective-permute-done((bf16[512,256]{1,0:T(8,128)(2,1)S(1)}, bf16[512,256]{1,0:T(8,128)(2,1)S(1)}, u32[]{:S(2)}, u32[]{:S(2)}) %collective-permute-start.27) | collective-permute-done | bytes 262176 | tf_op jit(solution)/shard_map/ppermute | solution.py:236
  (125 shorter events, 39.3 us)
Async XLA Ops:
  3.3 47.2 %collective-permute-start = (bf16[256,3840]{1,0:T(8,128)(2,1)S(1)}, bf16[256,3840]{1,0:T(8,128)(2,1)}, u32[]{:S(2)}, u32[]{:S(2)}) collective-permute-start(bf16[256,3840]{1,0:T(8,128)(2,1)S(1)} %pad_maximum_fusion), channel_id=1, source_target_pairs={{0,1},{1,0},{2,3},{3,2},{4,5},{5,4},{6,7},{7,6},{8,9},{9,8},{10,11... | collective-permute-start | bytes 5898248 | tf_op jit(solution)/shard_map/ppermute | solution.py:269
  7.9 10.0 %collective-permute-start.5 = (bf16[512,256]{1,0:T(8,128)(2,1)S(1)}, bf16[512,256]{1,0:T(8,128)(2,1)S(1)}, u32[]{:S(2)}, u32[]{:S(2)}) collective-permute-start(bf16[512,256]{1,0:T(8,128)(2,1)S(1)} %pad_maximum_fusion.4.refs_4_), channel_id=1, source_target_pairs={{0,4},{1,5},{4,8},{5,9},{8,12},{9,13},{12,14},{13,15},{14,10},{15,... | collective-permute-start | bytes 786440 | tf_op jit(solution)/shard_map/ppermute | solution.py:217
  10.9 9.2 %collective-permute-start.2 = (bf16[512,256]{1,0:T(8,128)(2,1)S(1)}, bf16[512,256]{1,0:T(8,128)(2,1)S(1)}, u32[]{:S(2)}, u32[]{:S(2)}) collective-permute-start(bf16[512,256]{1,0:T(8,128)(2,1)S(1)} %pad_maximum_fusion.4.refs_4_), channel_id=1, source_target_pairs={{4,0},{5,1},{8,4},{9,5},{12,8},{13,9},{14,12},{15,13},{10,14},{11,... | collective-permute-start | bytes 786440 | tf_op jit(solution)/shard_map/ppermute | solution.py:218
  10.9 12.6 %collective-permute-start.14 = (bf16[512,256]{1,0:T(8,128)(2,1)S(1)}, bf16[512,256]{1,0:T(8,128)(2,1)S(1)}, u32[]{:S(2)}, u32[]{:S(2)}) collective-permute-start(bf16[512,256]{1,0:T(8,128)(2,1)S(1)} %pad_maximum_fusion.5.refs_4_), channel_id=1, source_target_pairs={{0,4},{1,5},{4,8},{5,9},{8,12},{9,13},{12,14},{13,15},{14,10},{15,... | collective-permute-start | bytes 786440 | tf_op jit(solution)/shard_map/ppermute | solution.py:217
  13.0 12.7 %collective-permute-start.11 = (bf16[512,256]{1,0:T(8,128)(2,1)S(1)}, bf16[512,256]{1,0:T(8,128)(2,1)S(1)}, u32[]{:S(2)}, u32[]{:S(2)}) collective-permute-start(bf16[512,256]{1,0:T(8,128)(2,1)S(1)} %pad_maximum_fusion.5.refs_4_), channel_id=1, source_target_pairs={{4,0},{5,1},{8,4},{9,5},{12,8},{13,9},{14,12},{15,13},{10,14},{11,... | collective-permute-start | bytes 786440 | tf_op jit(solution)/shard_map/ppermute | solution.py:218
  17.9 11.2 %collective-permute-start.6 = (bf16[512,256]{1,0:T(8,128)(2,1)S(1)}, bf16[512,256]{1,0:T(8,128)(2,1)S(1)}, u32[]{:S(2)}, u32[]{:S(2)}) collective-permute-start(bf16[512,256]{1,0:T(8,128)(2,1)S(1)} %collective-permute-done.5.refs_10_), channel_id=1, source_target_pairs={{0,4},{1,5},{4,8},{5,9},{8,12},{9,13},{12,14},{13,15},{14,10},{15,... | collective-permute-start | bytes 786440 | tf_op jit(solution)/shard_map/ppermute | solution.py:217
  20.1 11.2 %collective-permute-start.3 = (bf16[512,256]{1,0:T(8,128)(2,1)S(1)}, bf16[512,256]{1,0:T(8,128)(2,1)S(1)}, u32[]{:S(2)}, u32[]{:S(2)}) collective-permute-start(bf16[512,256]{1,0:T(8,128)(2,1)S(1)} %collective-permute-done.2.refs_5_), channel_id=1, source_target_pairs={{4,0},{5,1},{8,4},{9,5},{12,8},{13,9},{14,12},{15,13},{10,14},{11,... | collective-permute-start | bytes 786440 | tf_op jit(solution)/shard_map/ppermute | solution.py:218
  23.5 11.2 %collective-permute-start.15 = (bf16[512,256]{1,0:T(8,128)(2,1)S(1)}, bf16[512,256]{1,0:T(8,128)(2,1)S(1)}, u32[]{:S(2)}, u32[]{:S(2)}) collective-permute-start(bf16[512,256]{1,0:T(8,128)(2,1)S(1)} %collective-permute-done.14.refs_10_), channel_id=1, source_target_pairs={{0,4},{1,5},{4,8},{5,9},{8,12},{9,13},{12,14},{13,15},{14,10},{15,... | collective-permute-start | bytes 786440 | tf_op jit(solution)/shard_map/ppermute | solution.py:217
  25.7 11.2 %collective-permute-start.12 = (bf16[512,256]{1,0:T(8,128)(2,1)S(1)}, bf16[512,256]{1,0:T(8,128)(2,1)S(1)}, u32[]{:S(2)}, u32[]{:S(2)}) collective-permute-start(bf16[512,256]{1,0:T(8,128)(2,1)S(1)} %collective-permute-done.11.refs_5_), channel_id=1, source_target_pairs={{4,0},{5,1},{8,4},{9,5},{12,8},{13,9},{14,12},{15,13},{10,14},{11,... | collective-permute-start | bytes 786440 | tf_op jit(solution)/shard_map/ppermute | solution.py:218
  29.2 11.2 %collective-permute-start.7 = (bf16[512,256]{1,0:T(8,128)(2,1)S(1)}, bf16[512,256]{1,0:T(8,128)(2,1)S(1)}, u32[]{:S(2)}, u32[]{:S(2)}) collective-permute-start(bf16[512,256]{1,0:T(8,128)(2,1)S(1)} %collective-permute-done.6.refs_9_), channel_id=1, source_target_pairs={{0,4},{1,5},{4,8},{5,9},{8,12},{9,13},{12,14},{13,15},{14,10},{15,... | collective-permute-start | bytes 786440 | tf_op jit(solution)/shard_map/ppermute | solution.py:217
  31.3 11.3 %collective-permute-start.4 = (bf16[512,256]{1,0:T(8,128)(2,1)S(1)}, bf16[512,256]{1,0:T(8,128)(2,1)S(1)}, u32[]{:S(2)}, u32[]{:S(2)}) collective-permute-start(bf16[512,256]{1,0:T(8,128)(2,1)S(1)} %collective-permute-done.3.refs_6_), channel_id=1, source_target_pairs={{4,0},{5,1},{8,4},{9,5},{12,8},{13,9},{14,12},{15,13},{10,14},{11,... | collective-permute-start | bytes 786440 | tf_op jit(solution)/shard_map/ppermute | solution.py:218
  34.8 11.2 %collective-permute-start.16 = (bf16[512,256]{1,0:T(8,128)(2,1)S(1)}, bf16[512,256]{1,0:T(8,128)(2,1)S(1)}, u32[]{:S(2)}, u32[]{:S(2)}) collective-permute-start(bf16[512,256]{1,0:T(8,128)(2,1)S(1)} %collective-permute-done.15.refs_9_), channel_id=1, source_target_pairs={{0,4},{1,5},{4,8},{5,9},{8,12},{9,13},{12,14},{13,15},{14,10},{15,... | collective-permute-start | bytes 786440 | tf_op jit(solution)/shard_map/ppermute | solution.py:217
  36.9 11.3 %collective-permute-start.13 = (bf16[512,256]{1,0:T(8,128)(2,1)S(1)}, bf16[512,256]{1,0:T(8,128)(2,1)S(1)}, u32[]{:S(2)}, u32[]{:S(2)}) collective-permute-start(bf16[512,256]{1,0:T(8,128)(2,1)S(1)} %collective-permute-done.12.refs_6_), channel_id=1, source_target_pairs={{4,0},{5,1},{8,4},{9,5},{12,8},{13,9},{14,12},{15,13},{10,14},{11,... | collective-permute-start | bytes 786440 | tf_op jit(solution)/shard_map/ppermute | solution.py:218
  46.0 28.0 %collective-permute-start.17 = (bf16[256,256]{1,0:T(8,128)(2,1)S(1)}, bf16[256,256]{1,0:T(8,128)(2,1)S(1)}, u32[]{:S(2)}, u32[]{:S(2)}) collective-permute-start(bf16[256,256]{1,0:T(8,128)(2,1)S(1)} %slice.133), channel_id=1, source_target_pairs={{0,4},{1,5},{4,8},{5,9},{8,12},{9,13},{12,14},{13,15},{14,10},{15,... | collective-permute-start | bytes 393224 | tf_op jit(solution)/shard_map/ppermute | solution.py:219
  48.2 25.8 %collective-permute-start.18 = (bf16[256,256]{1,0:T(8,128)(2,1)S(1)}, bf16[256,256]{1,0:T(8,128)(2,1)S(1)}, u32[]{:S(2)}, u32[]{:S(2)}) collective-permute-start(bf16[256,256]{1,0:T(8,128)(2,1)S(1)} %slice.134), channel_id=1, source_target_pairs={{4,0},{5,1},{8,4},{9,5},{12,8},{13,9},{14,12},{15,13},{10,14},{11,... | collective-permute-start | bytes 393224 | tf_op jit(solution)/shard_map/ppermute | solution.py:220
  69.8 28.7 %collective-permute-start.20 = (bf16[256,256]{1,0:T(8,128)(2,1)}, bf16[256,256]{1,0:T(8,128)(2,1)S(1)}, u32[]{:S(2)}, u32[]{:S(2)}) collective-permute-start(bf16[256,256]{1,0:T(8,128)(2,1)} %get-tuple-element.18), channel_id=1, source_target_pairs={{0,4},{1,5},{4,8},{5,9},{8,12},{9,13},{12,14},{13,15},{14,10},{15,... | collective-permute-start | bytes 393224 | tf_op jit(solution)/shard_map/ppermute | solution.py:230
  74.0 24.5 %collective-permute-start.24 = (bf16[256,256]{1,0:T(8,128)(2,1)}, bf16[256,256]{1,0:T(8,128)(2,1)S(1)}, u32[]{:S(2)}, u32[]{:S(2)}) collective-permute-start(bf16[256,256]{1,0:T(8,128)(2,1)} %get-tuple-element.19), channel_id=1, source_target_pairs={{4,0},{5,1},{8,4},{9,5},{12,8},{13,9},{14,12},{15,13},{10,14},{11,... | collective-permute-start | bytes 393224 | tf_op jit(solution)/shard_map/ppermute | solution.py:231
  98.6 9.5 %collective-permute-start.21 = (bf16[512,256]{1,0:T(8,128)(2,1)S(1)}, bf16[512,256]{1,0:T(8,128)(2,1)}, u32[]{:S(2)}, u32[]{:S(2)}) collective-permute-start(bf16[512,256]{1,0:T(8,128)(2,1)S(1)} %get-tuple-element.27), channel_id=1, source_target_pairs={{0,4},{1,5},{4,8},{5,9},{8,12},{9,13},{12,14},{13,15},{14,10},{15,... | collective-permute-start | bytes 786440 | tf_op jit(solution)/shard_map/ppermute | solution.py:235
  100.7 9.4 %collective-permute-start.25 = (bf16[512,256]{1,0:T(8,128)(2,1)S(1)}, bf16[512,256]{1,0:T(8,128)(2,1)}, u32[]{:S(2)}, u32[]{:S(2)}) collective-permute-start(bf16[512,256]{1,0:T(8,128)(2,1)S(1)} %get-tuple-element.28), channel_id=1, source_target_pairs={{4,0},{5,1},{8,4},{9,5},{12,8},{13,9},{14,12},{15,13},{10,14},{11,... | collective-permute-start | bytes 786440 | tf_op jit(solution)/shard_map/ppermute | solution.py:236
  108.1 22.5 %collective-permute-start.19 = (bf16[256,640]{1,0:T(8,128)(2,1)}, bf16[256,640]{1,0:T(8,128)(2,1)S(1)}, u32[]{:S(2)}, u32[]{:S(2)}) collective-permute-start(bf16[256,640]{1,0:T(8,128)(2,1)} %get-tuple-element.16), channel_id=1, source_target_pairs={{0,1},{1,0},{2,3},{3,2},{4,5},{5,4},{6,7},{7,6},{8,9},{9,8},{10,11... | collective-permute-start | bytes 983048 | tf_op jit(solution)/shard_map/ppermute | solution.py:275
  112.5 9.2 %collective-permute-start.26 = (bf16[512,256]{1,0:T(8,128)(2,1)S(1)}, bf16[512,256]{1,0:T(8,128)(2,1)S(1)}, u32[]{:S(2)}, u32[]{:S(2)}) collective-permute-start(bf16[512,256]{1,0:T(8,128)(2,1)S(1)} %get-tuple-element.26), channel_id=1, source_target_pairs={{4,0},{5,1},{8,4},{9,5},{12,8},{13,9},{14,12},{15,13},{10,14},{11,... | collective-permute-start | bytes 786440 | tf_op jit(solution)/shard_map/ppermute | solution.py:236
  114.7 11.2 %collective-permute-start.30 = (bf16[512,256]{1,0:T(8,128)(2,1)S(1)}, bf16[512,256]{1,0:T(8,128)(2,1)S(1)}, u32[]{:S(2)}, u32[]{:S(2)}) collective-permute-start(bf16[512,256]{1,0:T(8,128)(2,1)S(1)} %get-tuple-element.31), channel_id=1, source_target_pairs={{0,4},{1,5},{4,8},{5,9},{8,12},{9,13},{12,14},{13,15},{14,10},{15,... | collective-permute-start | bytes 786440 | tf_op jit(solution)/shard_map/ppermute | solution.py:235
  115.9 11.5 %collective-permute-start.34 = (bf16[512,256]{1,0:T(8,128)(2,1)S(1)}, bf16[512,256]{1,0:T(8,128)(2,1)S(1)}, u32[]{:S(2)}, u32[]{:S(2)}) collective-permute-start(bf16[512,256]{1,0:T(8,128)(2,1)S(1)} %get-tuple-element.32), channel_id=1, source_target_pairs={{4,0},{5,1},{8,4},{9,5},{12,8},{13,9},{14,12},{15,13},{10,14},{11,... | collective-permute-start | bytes 786440 | tf_op jit(solution)/shard_map/ppermute | solution.py:236
  122.6 10.4 %collective-permute-start.27 = (bf16[512,256]{1,0:T(8,128)(2,1)S(1)}, bf16[512,256]{1,0:T(8,128)(2,1)S(1)}, u32[]{:S(2)}, u32[]{:S(2)}) collective-permute-start(bf16[512,256]{1,0:T(8,128)(2,1)S(1)} %get-tuple-element.24), channel_id=1, source_target_pairs={{4,0},{5,1},{8,4},{9,5},{12,8},{13,9},{14,12},{15,13},{10,14},{11,... | collective-permute-start | bytes 786440 | tf_op jit(solution)/shard_map/ppermute | solution.py:236
  (36 other events, 573.0 us)

commit v4 on v3

--- a/solution.py
+++ b/solution.py
@@ -31,14 +31,13 @@
     return list(range(chips))
 
 
-def walk(device, me, places, parents, assignment, lengths, owner, block, reach, side):
+def walk(device, me, places, parents, assignment, lengths, owner, block, reach, side, turn):
     chips = places.shape[0]
-    here = places[me // 2]
 
     def place(held):
-        ahead = places[held // 2] - here
-        ahead = jnp.where(ahead < 0, ahead + chips, ahead)
-        return ahead * 2 + jnp.where(held % 2 == me % 2, 0, 1)
+        at = places[held // 2] - turn
+        at = jnp.where(at < 0, at + chips, at)
+        return at * 2 + jnp.where(held % 2 == me % 2, 0, 1)
 
     segment = assignment[device]
     block[side, 0] = place(device)
@@ -55,13 +54,17 @@
     block[side, SLOTS] = depth + 1
 
 
-def kernel(chips, head, me_ref, places, parents, assignment, lengths, *refs):
+def kernel(chips, head, ring_in, ring_out, me_ref, places, parents, assignment, lengths, *refs):
     mine, refs = refs[:3], refs[3:]
     other_ref, refs = refs[0], refs[1:]
-    kv_in, refs = refs[:chips + 1], refs[chips + 1:]
-    sum_ref, up_ref, down_ref, dq_mine, dq_other = refs[:5]
+    count = chips + 1 if ring_in else 1
+    kv_in, refs = refs[:count], refs[count:]
+    count = 3 if ring_out else 1
+    sums, refs = refs[:count], refs[count:]
+    sum_ref = sums[0]
+    dq_mine, dq_other = refs[:2]
     (owner, block, reach, q_ref, g_ref, o_ref, qt_ref, gt_ref, kv_ref, total_ref,
-     s_ref, kt_ref, dqt_ref, sems) = refs[5:]
+     s_ref, kt_ref, dqt_ref, sems) = refs[2:]
     rows = dq_mine.shape[0]
     far = chips // 2
     me = me_ref[0]
@@ -73,11 +76,14 @@
             copies.append((mine[at].at[:, pl.ds(column, DH)], held.at[0, h]))
             column = ((at * HALF + head) * PER + h) * DH
             copies.append((other_ref.at[:, column:column + DH], held.at[1, h]))
-    blocks = [at for at in range(chips) if at != far]
-    for at, held in zip(blocks, kv_in):
-        copies.append((held, kv_ref.at[at]))
-    copies.append((kv_in[chips - 1], kv_ref.at[far, :rows]))
-    copies.append((kv_in[chips], kv_ref.at[far, rows:]))
+    if ring_in:
+        blocks = [at for at in range(chips) if at != far]
+        for at, held in zip(blocks, kv_in):
+            copies.append((held, kv_ref.at[at]))
+        copies.append((kv_in[chips - 1], kv_ref.at[far, :rows]))
+        copies.append((kv_in[chips], kv_ref.at[far, rows:]))
+    else:
+        copies.append((kv_in[0], kv_ref))
     copies = [pltpu.make_async_copy(a, b, sems.at[i]) for i, (a, b) in enumerate(copies)]
     for copy in copies:
         copy.start()
@@ -87,8 +93,11 @@
         return carry
 
     lax.fori_loop(0, assignment.shape[0], invert, 0)
-    walk(me, me, places, parents, assignment, lengths, owner, block, reach, 0)
-    walk(me + 1 - me % 2 * 2, me, places, parents, assignment, lengths, owner, block, reach, 1)
+    here = places[me // 2]
+    turn_in = here if ring_in else 0
+    turn_out = (here if ring_in else 0) - (here if ring_out else 0)
+    walk(me, me, places, parents, assignment, lengths, owner, block, reach, 0, turn_in)
+    walk(me + 1 - me % 2 * 2, me, places, parents, assignment, lengths, owner, block, reach, 1, turn_in)
 
     def clear(at, carry):
         total_ref[at] = jnp.zeros(total_ref.shape[1:], total_ref.dtype)
@@ -113,10 +122,12 @@
             delta.append(jnp.sum(terms.T, axis=0, keepdims=True))
         delta = jnp.concatenate(delta, axis=1)
 
-        def key_rows(ref, slot):
+        def key_rows(ref, slot, turn=0):
             at = block[side, slot]
             first = pl.multiple_of(at % 2 * rows, rows)
-            return ref.at[at // 2, pl.ds(first, rows)]
+            chip = at // 2 + turn
+            chip = jnp.where(chip < 0, chip + chips, jnp.where(chip >= chips, chip - chips, chip))
+            return ref.at[chip, pl.ds(first, rows)]
 
         def fold(x, op):
             return op(x.reshape(rows // 8, 8, PER * rows), axis=0)
@@ -147,7 +158,7 @@
             v = key_rows(kv_ref, slot)[:, DH:]
             p = s_ref[slot] * inverse
             ds = (p * (dot(v, gt_ref[...]) - delta)).astype(jnp.bfloat16)
-            into = key_rows(total_ref, slot)
+            into = key_rows(total_ref, slot, turn_out)
             into[:, DH:] += dot(p.astype(jnp.bfloat16), g_ref[side].reshape(PER * rows, DH))
             into[:, :DH] += dot(ds, q_ref[side].reshape(PER * rows, DH))
             dqt_ref[...] += dot(kt_ref[slot], ds)
@@ -164,30 +175,30 @@
         return carry
 
     lax.fori_loop(0, chips, finish, 0)
-    up_ref[...] = sum_ref[far, :rows]
-    down_ref[...] = sum_ref[far, rows:]
-
-
-def attend(head, tables, mine, other, blocks):
+    if ring_out:
+        sums[1][...] = sum_ref[far, :rows]
+        sums[2][...] = sum_ref[far, rows:]
+
+
+def attend(head, ring_out, tables, mine, other, blocks):
     rows = other.shape[0]
-    chips = len(blocks) - 1
+    chips = tables[1].shape[0]
+    ring_in = len(blocks) > 1
     devices = 2 * chips
     smem = pl.BlockSpec(memory_space=pltpu.SMEM)
     hbm = pl.BlockSpec(memory_space=pl.ANY)
     vmem = pl.BlockSpec(memory_space=pltpu.VMEM)
     bf16, f32 = jnp.bfloat16, jnp.float32
+    outs = [jax.ShapeDtypeStruct((chips, 2 * rows, 2 * DH), bf16)]
+    if ring_out:
+        outs += [jax.ShapeDtypeStruct((rows, 2 * DH), bf16)] * 2
+    outs += [jax.ShapeDtypeStruct((rows, WIDE), bf16)] * 2
     work = 2 * 5 * 5 * PER * rows * rows * DH * 2
     return pl.pallas_call(
-        functools.partial(kernel, chips, head),
-        in_specs=[smem] * 5 + [hbm] * (4 + chips + 1),
-        out_specs=[vmem] * 5,
-        out_shape=[
-            jax.ShapeDtypeStruct((chips, 2 * rows, 2 * DH), bf16),
-            jax.ShapeDtypeStruct((rows, 2 * DH), bf16),
-            jax.ShapeDtypeStruct((rows, 2 * DH), bf16),
-            jax.ShapeDtypeStruct((rows, WIDE), bf16),
-            jax.ShapeDtypeStruct((rows, WIDE), bf16),
-        ],
+        functools.partial(kernel, chips, head, ring_in, ring_out),
+        in_specs=[smem] * 5 + [hbm] * (4 + len(blocks)),
+        out_specs=[vmem] * len(outs),
+        out_shape=outs,
         scratch_shapes=[
             pltpu.SMEM((devices,), jnp.int32),
             pltpu.SMEM((2, SLOTS + 1), jnp.int32),
@@ -245,6 +256,7 @@
     right = [(2 * a + c, 2 * b + c) for a, b in ahead for c in range(2)]
     left = [(b, a) for a, b in right]
     swap = [(2 * a + c, 2 * a + 1 - c) for a in range(chips) for c in range(2)]
+    rings = [[2 * chip + c for chip in order] for c in range(2)]
     places = jnp.asarray([order.index(chip) for chip in range(chips)], jnp.int32)
     index = lax.axis_index("leaf").astype(jnp.int32)
     core = index % 2
@@ -263,14 +275,21 @@
     for head in range(HALF):
         cols = slice(head * 2 * DH, (head + 1) * 2 * DH)
         block = jnp.concatenate([kept[:, cols], got[:, cols]], axis=0)
-        gathered.append(spread(block, right, left, chips))
+        if head == 0:
+            gathered.append(spread(block, right, left, chips))
+        else:
+            gathered.append([lax.all_gather(block, "leaf", axis_index_groups=rings)])
     mine = (queries, grad_out, saved_out)
     other = jnp.concatenate([part(array, 1 - core, HALF * WIDE) for array in mine], axis=1)
     other = lax.ppermute(other, "leaf", swap)
     sums, ours, theirs = [], [], []
     for head in range(HALF):
-        terms, up, down, dq_mine, dq_other = attend(head, tables, mine, other, gathered[head])
-        sums.append(collect(terms, up, down, right, left))
+        *terms, dq_mine, dq_other = attend(head, head > 0, tables, mine, other, gathered[head])
+        if head > 0:
+            sums.append(collect(*terms, right, left))
+        else:
+            total = lax.psum_scatter(terms[0], "leaf", axis_index_groups=rings)
+            sums.append(total)
         ours.append(dq_mine)
         theirs.append(lax.ppermute(dq_other, "leaf", swap))
 

time: 140 us -> 152 us (1.086); the launches traced: 141 us -> 150 us
  between operations: 1.03 us -> 14.4 us
  starting transfers between devices: 40.1 us -> 28 us
  waiting for transfers between devices: 48.9 us -> 60.2 us
  Pallas kernels: 37 us -> 34.5 us
    ppermute x6 -> x3, waiting for transfers between devices: 22.1 us -> 31.1 us  [spread(): up = got[chips - step] = lax.ppermute(up, 'leaf', right)]
    ppermute x6 -> x3, waiting for transfers between devices: 8.74 us -> 1.88 us  [collect(): lax.ppermute((down + wide(terms[chips - step])).astype(terms.dtype), 'lea...]
    ppermute x6 -> x3, starting transfers between devices: 13.5 us -> 7.75 us  [spread(): up = got[chips - step] = lax.ppermute(up, 'leaf', right)]
    ppermute x6 -> x3, waiting for transfers between devices: 8.13 us -> 12.7 us  [collect(): lax.ppermute((up + wide(terms[step])).astype(terms.dtype), 'leaf', right)]
    ppermute x2 -> x1, waiting for transfers between devices: 2.1 us -> 6.04 us  [collect(): up = lax.ppermute(up, 'leaf', right)]
    ppermute x6 -> x3, starting transfers between devices: 5.47 us -> 1.77 us  [collect(): lax.ppermute((up + wide(terms[step])).astype(terms.dtype), 'leaf', right)]
    pallas_call x2, Pallas kernels: 37 us -> 34.5 us  [attend(): pl.pallas_call(functools.partial(kernel, chips, head, ring_in, ring_out),...]
    ppermute x2 -> x1, starting transfers between devices: 4.33 us -> 2.53 us  [spread(): up = lax.ppermute(up[:rows], 'leaf', right)]
  transfers between devices with their start and end apart: 37 -> 23, of which waited for: 21 -> 15; matrix products, arithmetic and copies ran while one was open for 5% -> 5% of each run, Pallas kernels for 26% -> 23%
where the time goes in v4:
time: 152 us; the launch traced here: 150 us
  waiting for transfers between devices  60.2 us (40%)
  Pallas kernels  34.5 us (23%)
  starting transfers between devices  28 us (18%)
  between operations  14.4 us (9%)
  other arithmetic  9.21 us (6%)
  local copies, waits for them, and re-layouts  3.94 us (3%)
    pallas_call x2, Pallas kernels, attend(): pl.pallas_call(functools.partial(kernel, chips, head, ring_in, ring_out),...  34.5 us
    ppermute x3, waiting for transfers between devices, spread(): up = got[chips - step] = lax.ppermute(up, 'leaf', right)  31.1 us
    ppermute x3, waiting for transfers between devices, collect(): lax.ppermute((up + wide(terms[step])).astype(terms.dtype), 'leaf', right)  12.7 us
    ppermute x1, starting transfers between devices, collect(): up = lax.ppermute(up, 'leaf', right)  9.71 us
    ppermute x3, starting transfers between devices, spread(): up = got[chips - step] = lax.ppermute(up, 'leaf', right)  7.75 us
    ppermute x1, waiting for transfers between devices, collect(): up = lax.ppermute(up, 'leaf', right)  6.04 us
    ppermute x3, starting transfers between devices, collect(): lax.ppermute((down + wide(terms[chips - step])).astype(terms.dtype), 'lea...  4.46 us
    convert_element_type x3, other arithmetic, collect(): (up + wide(terms[step])).astype(terms.dtype)  3.46 us
  transfers between devices with their start and end apart: 23, of which 15 were waited for; matrix products, arithmetic and copies ran while one was open for 5% of the time, Pallas kernels for 23%

profile of v4, /device:TPU:0, one launch (start us, length us, event | category | flops | bytes accessed | tf_op | source)
XLA Modules:
  0.0 150.3 jit_solution(6257219283675210831)
XLA Ops:
  7.3 1.3 constant_dynamic-slice_fusion.6
  9.1 1.2 collective-permute-done.1
  11.2 1.2 constant_dynamic-slice_fusion.8
  13.0 2.8 %collective-permute-start.5 = (bf16[512,256]{1,0:T(8,128)(2,1)S(1)}, bf16[512,256]{1,0:T(8,128)(2,1)S(1)}, u32[]{:S(2)}, u32[]{:S(2)}) collective-permute-start(bf16[512,256]{1,0:T(8,128)(2,1)S(1)} %pad_maximum_fusion.4.refs_4_), channel_id=1, source_target_pairs={{0,4},{1,5},{4,8},{5,9},{8,12},{9,13},{12,14},{13,15},{14,10},{15,... | collective-permute-start | bytes 786440 | tf_op jit(solution)/shard_map/ppermute | solution.py:228
  15.8 8.8 %collective-permute-done.5.refs_10_ = bf16[512,256]{1,0:T(8,128)(2,1)S(1)} collective-permute-done((bf16[512,256]{1,0:T(8,128)(2,1)S(1)}, bf16[512,256]{1,0:T(8,128)(2,1)S(1)}, u32[]{:S(2)}, u32[]{:S(2)}) %collective-permute-start.5) | collective-permute-done | bytes 262176 | tf_op jit(solution)/shard_map/ppermute | solution.py:228
  24.5 2.5 %collective-permute-start.6 = (bf16[512,256]{1,0:T(8,128)(2,1)S(1)}, bf16[512,256]{1,0:T(8,128)(2,1)S(1)}, u32[]{:S(2)}, u32[]{:S(2)}) collective-permute-start(bf16[512,256]{1,0:T(8,128)(2,1)S(1)} %collective-permute-done.5.refs_10_), channel_id=1, source_target_pairs={{0,4},{1,5},{4,8},{5,9},{8,12},{9,13},{12,14},{13,15},{14,10},{15,... | collective-permute-start | bytes 786440 | tf_op jit(solution)/shard_map/ppermute | solution.py:228
  27.1 11.3 %collective-permute-done.6.refs_9_ = bf16[512,256]{1,0:T(8,128)(2,1)S(1)} collective-permute-done((bf16[512,256]{1,0:T(8,128)(2,1)S(1)}, bf16[512,256]{1,0:T(8,128)(2,1)S(1)}, u32[]{:S(2)}, u32[]{:S(2)}) %collective-permute-start.6) | collective-permute-done | bytes 262176 | tf_op jit(solution)/shard_map/ppermute | solution.py:228
  38.3 2.5 %collective-permute-start.7 = (bf16[512,256]{1,0:T(8,128)(2,1)S(1)}, bf16[512,256]{1,0:T(8,128)(2,1)S(1)}, u32[]{:S(2)}, u32[]{:S(2)}) collective-permute-start(bf16[512,256]{1,0:T(8,128)(2,1)S(1)} %collective-permute-done.6.refs_9_), channel_id=1, source_target_pairs={{0,4},{1,5},{4,8},{5,9},{8,12},{9,13},{12,14},{13,15},{14,10},{15,... | collective-permute-start | bytes 786440 | tf_op jit(solution)/shard_map/ppermute | solution.py:228
  40.8 11.0 %collective-permute-done.7.refs_8_ = bf16[512,256]{1,0:T(8,128)(2,1)S(1)} collective-permute-done((bf16[512,256]{1,0:T(8,128)(2,1)S(1)}, bf16[512,256]{1,0:T(8,128)(2,1)S(1)}, u32[]{:S(2)}, u32[]{:S(2)}) %collective-permute-start.7) | collective-permute-done | bytes 262176 | tf_op jit(solution)/shard_map/ppermute | solution.py:228
  51.9 2.5 %collective-permute-start.8 = (bf16[256,256]{1,0:T(8,128)(2,1)S(1)}, bf16[256,256]{1,0:T(8,128)(2,1)S(1)}, u32[]{:S(2)}, u32[]{:S(2)}) collective-permute-start(bf16[256,256]{1,0:T(8,128)(2,1)S(1)} %slice.94), channel_id=1, source_target_pairs={{0,4},{1,5},{4,8},{5,9},{8,12},{9,13},{12,14},{13,15},{14,10},{15,... | collective-permute-start | bytes 393224 | tf_op jit(solution)/shard_map/ppermute | solution.py:230
  54.6 2.3 %collective-permute-done.8.refs_11_ = bf16[256,256]{1,0:T(8,128)(2,1)S(1)} collective-permute-done((bf16[256,256]{1,0:T(8,128)(2,1)S(1)}, bf16[256,256]{1,0:T(8,128)(2,1)S(1)}, u32[]{:S(2)}, u32[]{:S(2)}) %collective-permute-start.8) | collective-permute-done | bytes 131104 | tf_op jit(solution)/shard_map/ppermute | solution.py:230
  56.9 2.5 %collective-permute-done.9.refs_12_ = bf16[256,256]{1,0:T(8,128)(2,1)S(1)} collective-permute-done((bf16[256,256]{1,0:T(8,128)(2,1)S(1)}, bf16[256,256]{1,0:T(8,128)(2,1)S(1)}, u32[]{:S(2)}, u32[]{:S(2)}) %collective-permute-start.9) | collective-permute-done | bytes 131104 | tf_op jit(solution)/shard_map/ppermute | solution.py:231
  60.9 17.2 %shard_map.112 = (bf16[8,512,256]{2,1,0:T(8,128)(2,1)}, bf16[256,640]{1,0:T(8,128)(2,1)}, bf16[256,640]{1,0:T(8,128)(2,1)}) custom-call(s32[1]{0:T(128)} %bitcast.me_ref, s32[8]{0:T(128)} %constant.35.clone.places, s32[16]{0:T(128)} %parents.3, s32[16]{0:T(128)} %assignment.3, s32[16]{0:T(128)} %lengths.3, bf16[256,2560]{1,0:T(8,128)(2,1)} %refs_0_.3, ...), custom_call_target="tpu_custom_call" | custom-call | flops 4194304000 | bytes 8388608 | tf_op jit(solution)/shard_map/pallas_call | solution.py:197
  78.1 17.3 %shard_map.113 = (bf16[8,512,256]{2,1,0:T(8,128)(2,1)}, bf16[256,256]{1,0:T(8,128)(2,1)}, bf16[256,256]{1,0:T(8,128)(2,1)}, bf16[256,640]{1,0:T(8,128)(2,1)}, bf16[256,640]{1,0:T(8,128)(2,1)}) custom-call(s32[1]{0:T(128)} %bitcast.me_ref, s32[8]{0:T(128)} %constant.35.clone.places, s32[16]{0:T(128)} %parents.3, s32[16]{0:T(128)} %assignment.3, s32[16]{0:T(128)} %lengths.3, ...), custom_call_target="tpu_custom_call" | custom-call | flops 4194304000 | bytes 8388608 | tf_op jit(solution)/shard_map/pallas_call | solution.py:197
  95.5 9.7 %collective-permute-start.12 = (bf16[256,256]{1,0:T(8,128)(2,1)}, bf16[256,256]{1,0:T(8,128)(2,1)S(1)}, u32[]{:S(2)}, u32[]{:S(2)}) collective-permute-start(bf16[256,256]{1,0:T(8,128)(2,1)} %get-tuple-element.17), channel_id=1, source_target_pairs={{0,4},{1,5},{4,8},{5,9},{8,12},{9,13},{12,14},{13,15},{14,10},{15,... | collective-permute-start | bytes 393224 | tf_op jit(solution)/shard_map/ppermute | solution.py:241
  105.2 6.0 %collective-permute-done.12 = bf16[256,256]{1,0:T(8,128)(2,1)S(1)} collective-permute-done((bf16[256,256]{1,0:T(8,128)(2,1)}, bf16[256,256]{1,0:T(8,128)(2,1)S(1)}, u32[]{:S(2)}, u32[]{:S(2)}) %collective-permute-start.12) | collective-permute-done | bytes 131104 | tf_op jit(solution)/shard_map/ppermute | solution.py:241
  111.2 2.0 %collective-permute-done.16 = bf16[256,256]{1,0:T(8,128)(2,1)S(1)} collective-permute-done((bf16[256,256]{1,0:T(8,128)(2,1)}, bf16[256,256]{1,0:T(8,128)(2,1)S(1)}, u32[]{:S(2)}, u32[]{:S(2)}) %collective-permute-start.16) | collective-permute-done | bytes 131104 | tf_op jit(solution)/shard_map/ppermute | solution.py:242
  114.8 1.7 %collective-permute-start.17 = (bf16[512,256]{1,0:T(8,128)(2,1)S(1)}, bf16[512,256]{1,0:T(8,128)(2,1)S(1)}, u32[]{:S(2)}, u32[]{:S(2)}) collective-permute-start(bf16[512,256]{1,0:T(8,128)(2,1)S(1)} %get-tuple-element.24), channel_id=1, source_target_pairs={{4,0},{5,1},{8,4},{9,5},{12,8},{13,9},{14,12},{15,13},{10,14},{11,... | collective-permute-start | bytes 786440 | tf_op jit(solution)/shard_map/ppermute | solution.py:247
  116.5 4.7 %collective-permute-done.13 = bf16[512,256]{1,0:T(8,128)(2,1)S(1)} collective-permute-done((bf16[512,256]{1,0:T(8,128)(2,1)S(1)}, bf16[512,256]{1,0:T(8,128)(2,1)S(1)}, u32[]{:S(2)}, u32[]{:S(2)}) %collective-permute-start.13) | collective-permute-done | bytes 262176 | tf_op jit(solution)/shard_map/ppermute | solution.py:246
  121.8 1.2 fusion.4
  125.6 3.8 %collective-permute-done.14 = bf16[512,256]{1,0:T(8,128)(2,1)S(1)} collective-permute-done((bf16[512,256]{1,0:T(8,128)(2,1)S(1)}, bf16[512,256]{1,0:T(8,128)(2,1)S(1)}, u32[]{:S(2)}, u32[]{:S(2)}) %collective-permute-start.14) | collective-permute-done | bytes 262176 | tf_op jit(solution)/shard_map/ppermute | solution.py:246
  130.4 1.2 fusion.3
  131.9 1.8 %collective-permute-start.19 = (bf16[512,256]{1,0:T(8,128)(2,1)S(1)}, bf16[512,256]{1,0:T(8,128)(2,1)S(1)}, u32[]{:S(2)}, u32[]{:S(2)}) collective-permute-start(bf16[512,256]{1,0:T(8,128)(2,1)S(1)} %get-tuple-element.20), channel_id=1, source_target_pairs={{4,0},{5,1},{8,4},{9,5},{12,8},{13,9},{14,12},{15,13},{10,14},{11,... | collective-permute-start | bytes 786440 | tf_op jit(solution)/shard_map/ppermute | solution.py:247
  133.9 4.2 %collective-permute-done.15 = bf16[512,256]{1,0:T(8,128)(2,1)S(1)} collective-permute-done((bf16[512,256]{1,0:T(8,128)(2,1)S(1)}, bf16[512,256]{1,0:T(8,128)(2,1)S(1)}, u32[]{:S(2)}, u32[]{:S(2)}) %collective-permute-start.15) | collective-permute-done | bytes 262176 | tf_op jit(solution)/shard_map/ppermute | solution.py:246
  (81 shorter events, 15.3 us)
Async XLA Ops:
  7.2 70.9 %all-gather.3.cloned.1.call-start = ((), (), s32[]{:S(2)}) async-start(), calls=%async_computation.2 | async-start | bytes 2359296 | tf_op jit(solution)/shard_map/all_gather | solution.py:281
  8.6 1.7 %collective-permute-start.1 = (bf16[256,512]{1,0:T(8,128)(2,1)S(1)}, bf16[256,512]{1,0:T(8,128)(2,1)S(1)}, u32[]{:S(2)}, u32[]{:S(2)}) collective-permute-start(bf16[256,512]{1,0:T(8,128)(2,1)S(1)} %pad_maximum_fusion.3), channel_id=1, source_target_pairs={{0,1},{1,0},{2,3},{3,2},{4,5},{5,4},{6,7},{7,6},{8,9},{9,8},{10,11... | collective-permute-start | bytes 786440 | tf_op jit(solution)/shard_map/ppermute | solution.py:273
  11.0 128.3 %reduce-scatter.2.cloned.1.call-start = ((), (), s32[]{:S(2)}) async-start(), calls=%async_computation.1 | async-start | bytes 2359296 | tf_op jit(solution)/shard_map/reduce_scatter | solution.py:291
  12.5 47.0 %collective-permute-start = (bf16[256,3840]{1,0:T(8,128)(2,1)S(1)}, bf16[256,3840]{1,0:T(8,128)(2,1)S(1)}, u32[]{:S(2)}, u32[]{:S(2)}) collective-permute-start(bf16[256,3840]{1,0:T(8,128)(2,1)S(1)} %pad_maximum_fusion), channel_id=1, source_target_pairs={{0,1},{1,0},{2,3},{3,2},{4,5},{5,4},{6,7},{7,6},{8,9},{9,8},{10,11... | collective-permute-start | bytes 5898248 | tf_op jit(solution)/shard_map/ppermute | solution.py:284
  13.0 46.5 %copy-start.5 = (bf16[512,256]{1,0:T(8,128)(2,1)}, bf16[512,256]{1,0:T(8,128)(2,1)S(1)}, u32[]{:S(2)}) copy-start(bf16[512,256]{1,0:T(8,128)(2,1)S(1)} %pad_maximum_fusion.4.refs_4_) | copy-start | bytes 786436
  13.0 11.6 %collective-permute-start.5 = (bf16[512,256]{1,0:T(8,128)(2,1)S(1)}, bf16[512,256]{1,0:T(8,128)(2,1)S(1)}, u32[]{:S(2)}, u32[]{:S(2)}) collective-permute-start(bf16[512,256]{1,0:T(8,128)(2,1)S(1)} %pad_maximum_fusion.4.refs_4_), channel_id=1, source_target_pairs={{0,4},{1,5},{4,8},{5,9},{8,12},{9,13},{12,14},{13,15},{14,10},{15,... | collective-permute-start | bytes 786440 | tf_op jit(solution)/shard_map/ppermute | solution.py:228
  15.8 11.3 %collective-permute-start.2 = (bf16[512,256]{1,0:T(8,128)(2,1)S(1)}, bf16[512,256]{1,0:T(8,128)(2,1)S(1)}, u32[]{:S(2)}, u32[]{:S(2)}) collective-permute-start(bf16[512,256]{1,0:T(8,128)(2,1)S(1)} %pad_maximum_fusion.4.refs_4_), channel_id=1, source_target_pairs={{4,0},{5,1},{8,4},{9,5},{12,8},{13,9},{14,12},{15,13},{10,14},{11,... | collective-permute-start | bytes 786440 | tf_op jit(solution)/shard_map/ppermute | solution.py:229
  24.5 13.8 %collective-permute-start.6 = (bf16[512,256]{1,0:T(8,128)(2,1)S(1)}, bf16[512,256]{1,0:T(8,128)(2,1)S(1)}, u32[]{:S(2)}, u32[]{:S(2)}) collective-permute-start(bf16[512,256]{1,0:T(8,128)(2,1)S(1)} %collective-permute-done.5.refs_10_), channel_id=1, source_target_pairs={{0,4},{1,5},{4,8},{5,9},{8,12},{9,13},{12,14},{13,15},{14,10},{15,... | collective-permute-start | bytes 786440 | tf_op jit(solution)/shard_map/ppermute | solution.py:228
  27.1 13.8 %collective-permute-start.3 = (bf16[512,256]{1,0:T(8,128)(2,1)S(1)}, bf16[512,256]{1,0:T(8,128)(2,1)S(1)}, u32[]{:S(2)}, u32[]{:S(2)}) collective-permute-start(bf16[512,256]{1,0:T(8,128)(2,1)S(1)} %collective-permute-done.2.refs_5_), channel_id=1, source_target_pairs={{4,0},{5,1},{8,4},{9,5},{12,8},{13,9},{14,12},{15,13},{10,14},{11,... | collective-permute-start | bytes 786440 | tf_op jit(solution)/shard_map/ppermute | solution.py:229
  38.3 13.5 %collective-permute-start.7 = (bf16[512,256]{1,0:T(8,128)(2,1)S(1)}, bf16[512,256]{1,0:T(8,128)(2,1)S(1)}, u32[]{:S(2)}, u32[]{:S(2)}) collective-permute-start(bf16[512,256]{1,0:T(8,128)(2,1)S(1)} %collective-permute-done.6.refs_9_), channel_id=1, source_target_pairs={{0,4},{1,5},{4,8},{5,9},{8,12},{9,13},{12,14},{13,15},{14,10},{15,... | collective-permute-start | bytes 786440 | tf_op jit(solution)/shard_map/ppermute | solution.py:228
  40.8 13.6 %collective-permute-start.4 = (bf16[512,256]{1,0:T(8,128)(2,1)S(1)}, bf16[512,256]{1,0:T(8,128)(2,1)S(1)}, u32[]{:S(2)}, u32[]{:S(2)}) collective-permute-start(bf16[512,256]{1,0:T(8,128)(2,1)S(1)} %collective-permute-done.3.refs_6_), channel_id=1, source_target_pairs={{4,0},{5,1},{8,4},{9,5},{12,8},{13,9},{14,12},{15,13},{10,14},{11,... | collective-permute-start | bytes 786440 | tf_op jit(solution)/shard_map/ppermute | solution.py:229
  51.9 5.1 %collective-permute-start.8 = (bf16[256,256]{1,0:T(8,128)(2,1)S(1)}, bf16[256,256]{1,0:T(8,128)(2,1)S(1)}, u32[]{:S(2)}, u32[]{:S(2)}) collective-permute-start(bf16[256,256]{1,0:T(8,128)(2,1)S(1)} %slice.94), channel_id=1, source_target_pairs={{0,4},{1,5},{4,8},{5,9},{8,12},{9,13},{12,14},{13,15},{14,10},{15,... | collective-permute-start | bytes 393224 | tf_op jit(solution)/shard_map/ppermute | solution.py:230
  54.4 5.0 %collective-permute-start.9 = (bf16[256,256]{1,0:T(8,128)(2,1)S(1)}, bf16[256,256]{1,0:T(8,128)(2,1)S(1)}, u32[]{:S(2)}, u32[]{:S(2)}) collective-permute-start(bf16[256,256]{1,0:T(8,128)(2,1)S(1)} %slice.95), channel_id=1, source_target_pairs={{4,0},{5,1},{8,4},{9,5},{12,8},{13,9},{14,12},{15,13},{10,14},{11,... | collective-permute-start | bytes 393224 | tf_op jit(solution)/shard_map/ppermute | solution.py:231
  95.5 15.8 %collective-permute-start.12 = (bf16[256,256]{1,0:T(8,128)(2,1)}, bf16[256,256]{1,0:T(8,128)(2,1)S(1)}, u32[]{:S(2)}, u32[]{:S(2)}) collective-permute-start(bf16[256,256]{1,0:T(8,128)(2,1)} %get-tuple-element.17), channel_id=1, source_target_pairs={{0,4},{1,5},{4,8},{5,9},{8,12},{9,13},{12,14},{13,15},{14,10},{15,... | collective-permute-start | bytes 393224 | tf_op jit(solution)/shard_map/ppermute | solution.py:241
  105.2 8.1 %collective-permute-start.16 = (bf16[256,256]{1,0:T(8,128)(2,1)}, bf16[256,256]{1,0:T(8,128)(2,1)S(1)}, u32[]{:S(2)}, u32[]{:S(2)}) collective-permute-start(bf16[256,256]{1,0:T(8,128)(2,1)} %get-tuple-element.18), channel_id=1, source_target_pairs={{4,0},{5,1},{8,4},{9,5},{12,8},{13,9},{14,12},{15,13},{10,14},{11,... | collective-permute-start | bytes 393224 | tf_op jit(solution)/shard_map/ppermute | solution.py:242
  114.4 6.8 %collective-permute-start.13 = (bf16[512,256]{1,0:T(8,128)(2,1)S(1)}, bf16[512,256]{1,0:T(8,128)(2,1)S(1)}, u32[]{:S(2)}, u32[]{:S(2)}) collective-permute-start(bf16[512,256]{1,0:T(8,128)(2,1)S(1)} %get-tuple-element.23), channel_id=1, source_target_pairs={{0,4},{1,5},{4,8},{5,9},{8,12},{9,13},{12,14},{13,15},{14,10},{15,... | collective-permute-start | bytes 786440 | tf_op jit(solution)/shard_map/ppermute | solution.py:246
  114.8 7.0 %collective-permute-start.17 = (bf16[512,256]{1,0:T(8,128)(2,1)S(1)}, bf16[512,256]{1,0:T(8,128)(2,1)S(1)}, u32[]{:S(2)}, u32[]{:S(2)}) collective-permute-start(bf16[512,256]{1,0:T(8,128)(2,1)S(1)} %get-tuple-element.24), channel_id=1, source_target_pairs={{4,0},{5,1},{8,4},{9,5},{12,8},{13,9},{14,12},{15,13},{10,14},{11,... | collective-permute-start | bytes 786440 | tf_op jit(solution)/shard_map/ppermute | solution.py:247
  123.0 6.4 %collective-permute-start.14 = (bf16[512,256]{1,0:T(8,128)(2,1)S(1)}, bf16[512,256]{1,0:T(8,128)(2,1)S(1)}, u32[]{:S(2)}, u32[]{:S(2)}) collective-permute-start(bf16[512,256]{1,0:T(8,128)(2,1)S(1)} %get-tuple-element.21), channel_id=1, source_target_pairs={{0,4},{1,5},{4,8},{5,9},{8,12},{9,13},{12,14},{13,15},{14,10},{15,... | collective-permute-start | bytes 786440 | tf_op jit(solution)/shard_map/ppermute | solution.py:246
  124.1 6.4 %collective-permute-start.18 = (bf16[512,256]{1,0:T(8,128)(2,1)S(1)}, bf16[512,256]{1,0:T(8,128)(2,1)S(1)}, u32[]{:S(2)}, u32[]{:S(2)}) collective-permute-start(bf16[512,256]{1,0:T(8,128)(2,1)S(1)} %get-tuple-element.22), channel_id=1, source_target_pairs={{4,0},{5,1},{8,4},{9,5},{12,8},{13,9},{14,12},{15,13},{10,14},{11,... | collective-permute-start | bytes 786440 | tf_op jit(solution)/shard_map/ppermute | solution.py:247
  125.1 8.6 %collective-permute-start.10 = (bf16[256,640]{1,0:T(8,128)(2,1)S(1)}, bf16[256,640]{1,0:T(8,128)(2,1)S(1)}, u32[]{:S(2)}, u32[]{:S(2)}) collective-permute-start(bf16[256,640]{1,0:T(8,128)(2,1)S(1)} %copy-done.9), channel_id=1, source_target_pairs={{0,1},{1,0},{2,3},{3,2},{4,5},{5,4},{6,7},{7,6},{8,9},{9,8},{10,11... | collective-permute-start | bytes 983048 | tf_op jit(solution)/shard_map/ppermute | solution.py:294
  125.1 8.7 %collective-permute-start.11 = (bf16[256,640]{1,0:T(8,128)(2,1)S(1)}, bf16[256,640]{1,0:T(8,128)(2,1)S(1)}, u32[]{:S(2)}, u32[]{:S(2)}) collective-permute-start(bf16[256,640]{1,0:T(8,128)(2,1)S(1)} %copy-done.10), channel_id=1, source_target_pairs={{0,1},{1,0},{2,3},{3,2},{4,5},{5,4},{6,7},{7,6},{8,9},{9,8},{10,11... | collective-permute-start | bytes 983048 | tf_op jit(solution)/shard_map/ppermute | solution.py:294
  131.6 6.4 %collective-permute-start.15 = (bf16[512,256]{1,0:T(8,128)(2,1)S(1)}, bf16[512,256]{1,0:T(8,128)(2,1)S(1)}, u32[]{:S(2)}, u32[]{:S(2)}) collective-permute-start(bf16[512,256]{1,0:T(8,128)(2,1)S(1)} %get-tuple-element.19), channel_id=1, source_target_pairs={{0,4},{1,5},{4,8},{5,9},{8,12},{9,13},{12,14},{13,15},{14,10},{15,... | collective-permute-start | bytes 786440 | tf_op jit(solution)/shard_map/ppermute | solution.py:246
  131.9 6.4 %collective-permute-start.19 = (bf16[512,256]{1,0:T(8,128)(2,1)S(1)}, bf16[512,256]{1,0:T(8,128)(2,1)S(1)}, u32[]{:S(2)}, u32[]{:S(2)}) collective-permute-start(bf16[512,256]{1,0:T(8,128)(2,1)S(1)} %get-tuple-element.20), channel_id=1, source_target_pairs={{4,0},{5,1},{8,4},{9,5},{12,8},{13,9},{14,12},{15,13},{10,14},{11,... | collective-permute-start | bytes 786440 | tf_op jit(solution)/shard_map/ppermute | solution.py:247
  140.3 1.6 %collective-permute-start.20 = (bf16[256,512]{1,0:T(8,128)(2,1)S(1)}, bf16[256,512]{1,0:T(8,128)(2,1)S(1)}, u32[]{:S(2)}, u32[]{:S(2)}) collective-permute-start(bf16[256,512]{1,0:T(8,128)(2,1)S(1)} %pad_maximum_fusion.2), channel_id=1, source_target_pairs={{0,1},{1,0},{2,3},{3,2},{4,5},{5,4},{6,7},{7,6},{8,9},{9,8},{10,11... | collective-permute-start | bytes 786440 | tf_op jit(solution)/shard_map/ppermute | solution.py:302
  (16 other events, 233.6 us)
Sparse Core Ops, SparseCore 0:
  11.2 45.3 all-gather.2
  78.2 42.0 reduce-scatter.1

commit v5 on v3

v5 whole, which is shorter than its diff:
```python
import functools
import math

import jax
import jax.numpy as jnp
from jax import lax
from jax.experimental import pallas as pl
from jax.experimental.pallas import tpu as pltpu
from jax.sharding import PartitionSpec as P

HQ = 20
HK = 4
DH = 128
PER = HQ // HK
HALF = HK // 2
WIDE = PER * DH
ANCESTORS = 5
SLOTS = ANCESTORS + 1
REACH = 8
PLAN = 16
SCALE = 1.0 / math.sqrt(DH)
EXP_SCALE = SCALE / math.log(2.0)
NN = (((1,), (0,)), ((), ()))
SMEM = pl.BlockSpec(memory_space=pltpu.SMEM)
HBM = pl.BlockSpec(memory_space=pl.ANY)
VMEM = pl.BlockSpec(memory_space=pltpu.VMEM)
PARAMS = pltpu.CompilerParams(vmem_limit_bytes=56 * 1024 * 1024)


def dot(a, b):
    return lax.dot_general(a, b, NN, preferred_element_type=jnp.float32)


def ring_order(chips):
    if chips == 8:
        return [0, 2, 4, 6, 7, 5, 3, 1]
    return list(range(chips))


def walk(device, me, places, parents, assignment, lengths, owner, plan, side):
    chips = places.shape[0]
    here = places[me // 2]

    def place(held):
        at = places[held // 2] - here
        at = jnp.where(at < 0, at + chips, at)
        return at * 2 + jnp.where(held % 2 == me % 2, 0, 1)

    first = side * PLAN
    segment = assignment[device]
    plan[first] = place(device)
    plan[first + REACH] = lengths[segment]
    depth = jnp.int32(0)
    up = parents[segment]
    for slot in range(1, SLOTS):
        usable = up >= 0
        at = jnp.maximum(up, 0)
        plan[first + slot] = place(owner[at])
        plan[first + REACH + slot] = lengths[at]
        depth = depth + usable.astype(jnp.int32)
        up = jnp.where(usable, parents[at], -1)
    plan[first + SLOTS] = depth + 1


def run_copies(pairs, sems):
    copies = [pltpu.make_async_copy(a, b, sems.at[i]) for i, (a, b) in enumerate(pairs)]
    for copy in copies:
        copy.start()
    return copies


def column_of(me, head, h):
    return pl.multiple_of(((me % 2 * HALF + head) * PER + h) * DH, DH)


def prepare_kernel(me_ref, places, parents, assignment, lengths, queries, grads, saved, other,
                   plan, qt_ref, gt_ref, gm_ref, delta_ref, owner, q_ref, g_ref, o_ref, sems):
    rows = queries.shape[0]
    me = me_ref[0]
    width = HALF * WIDE
    column = pl.multiple_of(me % 2 * width, width)
    pairs = []
    for at, (array, held) in enumerate(zip((queries, grads, saved), (q_ref, g_ref, o_ref))):
        pairs.append((array.at[:, pl.ds(column, width)], held.at[0]))
        pairs.append((other.at[:, at * width:(at + 1) * width], held.at[1]))
    copies = run_copies(pairs, sems)

    def invert(d, carry):
        owner[assignment[d]] = d
        return carry

    lax.fori_loop(0, assignment.shape[0], invert, 0)
    walk(me, me, places, parents, assignment, lengths, owner, plan, 0)
    walk(me + 1 - me % 2 * 2, me, places, parents, assignment, lengths, owner, plan, 1)
    row_at = lax.broadcasted_iota(jnp.int32, (rows, 1), 0)
    for copy in copies:
        copy.wait()
    for side in range(2):
        live = row_at < plan[side * PLAN + REACH]
        for head in range(HALF):
            for h in range(PER):
                lanes = slice(h * rows, (h + 1) * rows)
                cols = slice((head * PER + h) * DH, (head * PER + h + 1) * DH)
                masked = jnp.where(live, g_ref[side, :, cols], jnp.zeros((), g_ref.dtype))
                gm_ref[head, side, h] = masked
                gt_ref[head, side, :, lanes] = masked.T
                qt_ref[head, side, :, lanes] = q_ref[side, :, cols].T
                terms = masked.astype(jnp.float32) * o_ref[side, :, cols].astype(jnp.float32)
                delta_ref[head, side, :, lanes] = jnp.sum(terms.T, axis=0, keepdims=True)


def prepare(tables, mine, other):
    rows = other.shape[0]
    bf16, f32 = jnp.bfloat16, jnp.float32
    return pl.pallas_call(
        prepare_kernel,
        in_specs=[SMEM] * 5 + [HBM] * 4,
        out_specs=[SMEM] + [VMEM] * 4,
        out_shape=[
            jax.ShapeDtypeStruct((2 * PLAN,), jnp.int32),
            jax.ShapeDtypeStruct((HALF, 2, DH, PER * rows), bf16),
            jax.ShapeDtypeStruct((HALF, 2, DH, PER * rows), bf16),
            jax.ShapeDtypeStruct((HALF, 2, PER, rows, DH), bf16),
            jax.ShapeDtypeStruct((HALF, 2, 1, PER * rows), f32),
        ],
        scratch_shapes=[pltpu.SMEM(tables[3].shape, jnp.int32)]
        + [pltpu.VMEM((2, rows, HALF * WIDE), bf16)] * 3
        + [pltpu.SemaphoreType.DMA((6,))],
        compiler_params=PARAMS,
        cost_estimate=pl.CostEstimate(flops=0, bytes_accessed=16 << 20, transcendentals=0),
    )(*tables, *mine, other)


def kernel(chips, head, side, add, me_ref, plan, delta_in, qt_in, gt_in, gm_in, q_in, *refs):
    kv_in, refs = refs[:chips + 1], refs[chips + 1:]
    sum_in = None
    if add:
        sum_in, refs = refs[0], refs[1:]
    outs = 4 if add else 2
    scratch = refs[-9:]
    sum_ref, dq_ref, *halves = refs[-9 - outs:-9]
    q_ref, gm_ref, qt_ref, gt_ref, delta_ref, kv_ref, s_ref, dqt_ref, sems = scratch
    rows = dq_ref.shape[0]
    far = chips // 2

    pairs = []
    for h in range(PER):
        if side == 0:
            pairs.append((q_in.at[:, pl.ds(column_of(me_ref[0], head, h), DH)], q_ref.at[h]))
        else:
            column = (head * PER + h) * DH
            pairs.append((q_in.at[:, column:column + DH], q_ref.at[h]))
    pairs.append((gm_in.at[head, side], gm_ref))
    pairs.append((qt_in.at[head, side], qt_ref))
    pairs.append((gt_in.at[head, side], gt_ref))
    pairs.append((delta_in.at[head, side], delta_ref))
    blocks = [at for at in range(chips) if at != far]
    for at, held in zip(blocks, kv_in):
        pairs.append((held, kv_ref.at[at]))
    pairs.append((kv_in[chips - 1], kv_ref.at[far, :rows]))
    pairs.append((kv_in[chips], kv_ref.at[far, rows:]))
    if add:
        pairs.append((sum_in, sum_ref))
    copies = run_copies(pairs, sems)

    first = side * PLAN
    slots = plan[first + SLOTS]
    lane_at = lax.broadcasted_iota(jnp.int32, (1, PER * rows), 1) % rows
    key_at = lax.broadcasted_iota(jnp.int32, (rows, 1), 0)
    dqt_ref[...] = jnp.zeros_like(dqt_ref)
    if not add:
        def clear(at, carry):
            sum_ref[at] = jnp.zeros(sum_ref.shape[1:], sum_ref.dtype)
            return carry

        lax.fori_loop(0, chips, clear, 0)
    for copy in copies:
        copy.wait()

    def key_rows(ref, slot):
        at = plan[first + slot]
        return ref.at[at // 2, pl.ds(pl.multiple_of(at % 2 * rows, rows), rows)]

    def fold(x, op):
        return op(x.reshape(rows // 8, 8, PER * rows), axis=0)

    def scores(slot, highest):
        k = key_rows(kv_ref, slot)[:, :DH]
        limit = jnp.where(slot == 0, lane_at, plan[first + REACH + slot] - 1)
        s = jnp.where(key_at <= limit, dot(k, qt_ref[...]), -1e30)
        s_ref[slot] = s
        return jnp.maximum(highest, fold(s, jnp.max))

    highest = jnp.full((8, PER * rows), -1e30, jnp.float32)
    highest = lax.fori_loop(0, slots, scores, highest)
    highest = jnp.max(highest, axis=0, keepdims=True)

    def weigh(slot, total):
        w = jnp.exp2((s_ref[slot] - highest) * EXP_SCALE)
        s_ref[slot] = w
        return total + fold(w, jnp.sum)

    total = jnp.zeros((8, PER * rows), jnp.float32)
    total = lax.fori_loop(0, slots, weigh, total)
    inverse = 1.0 / jnp.sum(total, axis=0, keepdims=True)

    def grads(slot, carry):
        kv = key_rows(kv_ref, slot)
        p = s_ref[slot] * inverse
        ds = (p * (dot(kv[:, DH:], gt_ref[...]) - delta_ref[...])).astype(jnp.bfloat16)
        dv = dot(p.astype(jnp.bfloat16), gm_ref[...].reshape(PER * rows, DH))
        dk = dot(ds, q_ref[...].reshape(PER * rows, DH)) * SCALE
        dqt_ref[...] += dot(kv[:, :DH].T, ds)
        into = key_rows(sum_ref, slot)
        if add:
            dk = dk + into[:, :DH].astype(jnp.float32)
            dv = dv + into[:, DH:].astype(jnp.float32)
        into[:, :DH] = dk.astype(into.dtype)
        into[:, DH:] = dv.astype(into.dtype)
        return carry

    lax.fori_loop(0, slots, grads, 0)
    for h in range(PER):
        dq = dqt_ref[:, h * rows:(h + 1) * rows].T * SCALE
        dq_ref[:, h * DH:(h + 1) * DH] = dq.astype(dq_ref.dtype)
    if add:
        halves[0][...] = sum_ref[far, :rows]
        halves[1][...] = sum_ref[far, rows:]


def attend(head, side, me, prepared, query, blocks, before, after):
    rows = query.shape[0]
    chips = len(blocks) - 1
    bf16, f32 = jnp.bfloat16, jnp.float32
    add = before is not None
    plan, qt, gt, gm, delta = prepared
    outs = [
        jax.ShapeDtypeStruct((chips, 2 * rows, 2 * DH), bf16),
        jax.ShapeDtypeStruct((rows, WIDE), bf16),
    ]
    if add:
        outs += [jax.ShapeDtypeStruct((rows, 2 * DH), bf16)] * 2
    arrays = (delta, qt, gt, gm, query, *blocks, *([before] if add else []), *after)
    work = 4 * 5 * 5 * PER * rows * rows * DH * 2
    return pl.pallas_call(
        functools.partial(kernel, chips, head, side, add),
        in_specs=[SMEM] * 2 + [HBM] * len(arrays),
        out_specs=[VMEM] * len(outs),
        out_shape=outs,
        scratch_shapes=[
            pltpu.VMEM((PER, rows, DH), bf16),
            pltpu.VMEM((PER, rows, DH), bf16),
            pltpu.VMEM((DH, PER * rows), bf16),
            pltpu.VMEM((DH, PER * rows), bf16),
            pltpu.VMEM((1, PER * rows), f32),
            pltpu.VMEM((chips, 2 * rows, 2 * DH), bf16),
            pltpu.VMEM((SLOTS, rows, PER * rows), f32),
            pltpu.VMEM((DH, PER * rows), f32),
            pltpu.SemaphoreType.DMA((PER + chips + 6,)),
        ],
        compiler_params=PARAMS,
        cost_estimate=pl.CostEstimate(flops=work, bytes_accessed=8 << 20, transcendentals=0),
    )(me, plan, *arrays)


def spread(block, right, left, chips):
    far, rows = chips // 2, block.shape[0] // 2
    got = {0: block}
    steps = []
    up = down = block
    for step in range(1, far):
        up = got[chips - step] = lax.ppermute(up, "leaf", right)
        down = got[step] = lax.ppermute(down, "leaf", left)
        steps.append([up, down])
    up = lax.ppermute(up[:rows], "leaf", right)
    down = lax.ppermute(down[rows:], "leaf", left)
    steps.append([up, down])
    return [got[at] for at in range(chips) if at != far] + [up, down], steps


def wide(x):
    return x.astype(jnp.float32)


def collect_first(terms, up, down, right, left):
    chips, rows = terms.shape[0], up.shape[0]
    up = jnp.pad(wide(lax.ppermute(up, "leaf", right)), ((0, rows), (0, 0)))
    down = jnp.pad(wide(lax.ppermute(down, "leaf", left)), ((rows, 0), (0, 0)))
    near = chips // 2 - 1
    return (
        (up + wide(terms[near])).astype(terms.dtype),
        (down + wide(terms[chips - near])).astype(terms.dtype),
    )


def collect_rest(terms, up, down, right, left):
    chips = terms.shape[0]
    for step in range(chips // 2 - 1, 0, -1):
        up = wide(lax.ppermute(up, "leaf", right))
        down = wide(lax.ppermute(down, "leaf", left))
        if step > 1:
            up = (up + wide(terms[step - 1])).astype(terms.dtype)
            down = (down + wide(terms[chips - step + 1])).astype(terms.dtype)
    return (wide(terms[0]) + up + down).astype(terms.dtype)


def local(queries, keys, values, saved_out, grad_out, parents, assignment, lengths):
    rows = keys.shape[0]
    chips = lax.axis_size("leaf") // 2
    order = ring_order(chips)
    ahead = [(order[i], order[(i + 1) % chips]) for i in range(chips)]
    right = [(2 * a + c, 2 * b + c) for a, b in ahead for c in range(2)]
    left = [(b, a) for a, b in right]
    swap = [(2 * a + c, 2 * a + 1 - c) for a in range(chips) for c in range(2)]
    places = jnp.asarray([order.index(chip) for chip in range(chips)], jnp.int32)
    index = lax.axis_index("leaf").astype(jnp.int32)
    core = index % 2
    me = index.reshape(1)
    tables = (me, places, parents, assignment, lengths)

    def part(array, which, width):
        return lax.dynamic_slice(array, (0, which * width), (rows, width))

    def heads_of(which):
        pieces = [part(array, which * HALF + head, DH) for head in range(HALF) for array in (keys, values)]
        return jnp.concatenate(pieces, axis=1)

    kept = heads_of(core)
    got = lax.ppermute(heads_of(1 - core), "leaf", swap)
    mine = (queries, grad_out, saved_out)
    other = jnp.concatenate([part(array, 1 - core, HALF * WIDE) for array in mine], axis=1)
    other = lax.ppermute(other, "leaf", swap)
    prepared = prepare(tables, mine, other)
    present = prepared[0][REACH] > 0
    gathered, steps = [], []
    for head in range(HALF):
        cols = slice(head * 2 * DH, (head + 1) * 2 * DH)
        block = jnp.concatenate([kept[:, cols], got[:, cols]], axis=0)
        if head > 0:
            block = jnp.where(present, block, steps[0][1][0])
        blocks, arrivals = spread(block, right, left, chips)
        gathered.append(blocks)
        steps.append(arrivals)

    ours, theirs, kept, got = [], [], [], []
    after = [steps[1][-3], steps[1][-2]]
    returned = []
    for head in range(HALF):
        common = (me, prepared)
        terms, dq = attend(head, 1, *common, other, gathered[head], None, after[0])
        theirs.append(lax.ppermute(dq, "leaf", swap))
        if head > 0:
            after[1] = returned[-1][1:]
        terms, dq, up, down = attend(head, 0, *common, queries, gathered[head], terms, after[1])
        ours.append(dq)
        returned.append((terms, *collect_first(terms, up, down, right, left)))
        after = [[], []]
    for parts in returned:
        total = collect_rest(*parts, right, left)
        kept.append(total[:rows])
        got.append(lax.ppermute(total[rows:], "leaf", swap))

    def whole(kept, got):
        low = [jnp.where(core == 0, a, b) for a, b in zip(kept, got)]
        high = [jnp.where(core == 0, b, a) for a, b in zip(kept, got)]
        return jnp.concatenate(low + high, axis=1)

    key_grad = whole([a[:, :DH] for a in kept], [a[:, :DH] for a in got])
    value_grad = whole([a[:, DH:] for a in kept], [a[:, DH:] for a in got])
    return (whole(ours, theirs), key_grad, value_grad)


def solution(mesh):
    tokens = P(("groups", "leaf"), None)
    tables = P("groups")
    return jax.shard_map(
        local,
        mesh=mesh,
        in_specs=(tokens,) * 5 + (tables,) * 3,
        out_specs=(tokens,) * 3,
        check_vma=False,
    )
```

time: 140 us -> 153 us (1.093)
  Pallas kernels: 37 us -> 55 us
  starting transfers between devices: 40.1 us -> 35.2 us
  waiting for transfers between devices: 48.9 us -> 46.6 us
  local copies, waits for them, and re-layouts: 4.95 us -> 7.14 us
  other arithmetic: 9.14 us -> 7.16 us
    pallas_call x2 -> x5, Pallas kernels: 37 us -> 55 us  [the longest x4 48.5 us: attend(): pl.pallas_call(functools.partial(kernel, chips, head, side, add), in_spec...]
    ppermute x19 -> x20, starting transfers between devices: 21 us -> 17.4 us  [the longest x6 12.2 us: collect_rest(): down = wide(lax.ppermute(down, 'leaf', left))]
    ppermute x6, waiting for transfers between devices: 22.1 us -> 18.8 us  [spread(): up = got[chips - step] = lax.ppermute(up, 'leaf', right)]
    convert_element_type x8, other arithmetic: 6.11 us -> 2.84 us  [the longest x1 1.24 us: collect_first(): (up + wide(terms[near])).astype(terms.dtype)]
    ppermute x2, starting transfers between devices: 4.33 us -> 1.91 us  [spread(): up = lax.ppermute(up[:rows], 'leaf', right)]
    ppermute x2, starting transfers between devices: 0.12 us -> 2.33 us  [spread(): down = lax.ppermute(down[rows:], 'leaf', left)]
    ppermute x6, starting transfers between devices: 13.5 us -> 11.9 us  [spread(): up = got[chips - step] = lax.ppermute(up, 'leaf', right)]
    unnamed x46 -> x56, local copies, waits for them, and re-layouts: 2.29 us -> 3.27 us
  transfers between devices with their start and end apart: 37 -> 38, of which waited for: 21 -> 22; matrix products, arithmetic and copies ran while one was open for 5% -> 3% of each run, Pallas kernels for 26% -> 27%
where the time goes in v5:
time: 153 us
  Pallas kernels  55 us (36%)
  waiting for transfers between devices  46.6 us (30%)
  starting transfers between devices  35.2 us (23%)
  other arithmetic  7.16 us (5%)
  local copies, waits for them, and re-layouts  7.14 us (5%)
  between operations  1.78 us (1%)
    pallas_call x4, Pallas kernels, attend(): pl.pallas_call(functools.partial(kernel, chips, head, side, add), in_spec...  48.5 us
    ppermute x6, waiting for transfers between devices, collect_rest(): up = wide(lax.ppermute(up, 'leaf', right))  18.9 us
    ppermute x6, waiting for transfers between devices, spread(): up = got[chips - step] = lax.ppermute(up, 'leaf', right)  18.8 us
    ppermute x6, starting transfers between devices, collect_rest(): down = wide(lax.ppermute(down, 'leaf', left))  12.2 us
    ppermute x6, starting transfers between devices, spread(): up = got[chips - step] = lax.ppermute(up, 'leaf', right)  11.9 us
    pallas_call x1, Pallas kernels, prepare(): pl.pallas_call(prepare_kernel, in_specs=[SMEM] * 5 + [HBM] * 4, out_specs...  6.46 us
    ppermute x2, starting transfers between devices, collect_first(): down = jnp.pad(wide(lax.ppermute(down, 'leaf', left)), ((rows, 0), (0, 0)))  4.02 us
    ppermute x1, waiting for transfers between devices, local(): got = lax.ppermute(heads_of(1 - core), 'leaf', swap)  3.71 us
  transfers between devices with their start and end apart: 38, of which 22 were waited for; matrix products, arithmetic and copies ran while one was open for 3% of the time, Pallas kernels for 27%

profile of v5, /device:TPU:0, one launch (start us, length us, event | category | flops | bytes accessed | tf_op | source)
XLA Modules:
  0.0 152.9 jit_solution(16303014954649586251)
XLA Ops:
  5.3 3.7 %collective-permute-done.1 = bf16[256,512]{1,0:T(8,128)(2,1)S(1)} collective-permute-done((bf16[256,512]{1,0:T(8,128)(2,1)S(1)}, bf16[256,512]{1,0:T(8,128)(2,1)S(1)}, u32[]{:S(2)}, u32[]{:S(2)}) %collective-permute-start.1) | collective-permute-done | bytes 262176 | tf_op jit(solution)/shard_map/ppermute | solution.py:329
  9.1 2.8 %collective-permute-start.5 = (bf16[512,256]{1,0:T(8,128)(2,1)S(1)}, bf16[512,256]{1,0:T(8,128)(2,1)S(1)}, u32[]{:S(2)}, u32[]{:S(2)}) collective-permute-start(bf16[512,256]{1,0:T(8,128)(2,1)S(1)} %pad_maximum_fusion.3.refs_0_), channel_id=1, source_target_pairs={{0,4},{1,5},{4,8},{5,9},{8,12},{9,13},{12,14},{13,15},{14,10},{15,... | collective-permute-start | bytes 786440 | tf_op jit(solution)/shard_map/ppermute | solution.py:272
  11.9 6.6 %collective-permute-done.5.refs_6_ = bf16[512,256]{1,0:T(8,128)(2,1)S(1)} collective-permute-done((bf16[512,256]{1,0:T(8,128)(2,1)S(1)}, bf16[512,256]{1,0:T(8,128)(2,1)S(1)}, u32[]{:S(2)}, u32[]{:S(2)}) %collective-permute-start.5) | collective-permute-done | bytes 262176 | tf_op jit(solution)/shard_map/ppermute | solution.py:272
  21.8 6.5 %shard_map.112 = (s32[32]{0:T(128)}, bf16[2,2,128,1280]{3,2,1,0:T(8,128)(2,1)}, bf16[2,2,128,1280]{3,2,1,0:T(8,128)(2,1)}, bf16[2,2,5,256,128]{4,3,2,1,0:T(8,128)(2,1)}, f32[2,2,1,1280]{3,2,1,0:T(1,128)}) custom-call(s32[1]{0:T(128)} %bitcast.me_ref, s32[8]{0:T(128)} %constant.37.clone.places, s32[16]{0:T(128)} %parents.1, s32[16]{0:T(128)} %assignment.1, ...), custom_call_target="tpu_custom_call" | custom-call | bytes 16777216 | tf_op jit(solution)/shard_map/pallas_call | solution.py:115
  34.4 5.2 %collective-permute-done.10.refs_6_ = bf16[512,256]{1,0:T(8,128)(2,1)S(1)} collective-permute-done((bf16[512,256]{1,0:T(8,128)(2,1)S(1)}, bf16[512,256]{1,0:T(8,128)(2,1)S(1)}, u32[]{:S(2)}, u32[]{:S(2)}) %collective-permute-start.10) | collective-permute-done | bytes 262176 | tf_op jit(solution)/shard_map/ppermute | solution.py:272
  41.6 3.6 %collective-permute-done.7.refs_4_ = bf16[512,256]{1,0:T(8,128)(2,1)S(1)} collective-permute-done((bf16[512,256]{1,0:T(8,128)(2,1)S(1)}, bf16[512,256]{1,0:T(8,128)(2,1)S(1)}, u32[]{:S(2)}, u32[]{:S(2)}) %collective-permute-start.7) | collective-permute-done | bytes 262176 | tf_op jit(solution)/shard_map/ppermute | solution.py:272
  47.3 3.5 %collective-permute-done.11.refs_9_.refs_5_ = bf16[512,256]{1,0:T(8,128)(2,1)S(1)} collective-permute-done((bf16[512,256]{1,0:T(8,128)(2,1)S(1)}, bf16[512,256]{1,0:T(8,128)(2,1)S(1)}, u32[]{:S(2)}, u32[]{:S(2)}) %collective-permute-start.11) | collective-permute-done | bytes 262176 | tf_op jit(solution)/shard_map/ppermute | solution.py:272
  55.8 11.1 %shard_map.113 = (bf16[8,512,256]{2,1,0:T(8,128)(2,1)}, bf16[256,640]{1,0:T(8,128)(2,1)}) custom-call(s32[1]{0:T(128)} %bitcast.me_ref, s32[32]{0:T(128)} %get-tuple-element.20.plan, f32[2,2,1,1280]{3,2,1,0:T(1,128)} %get-tuple-element.21.delta_in, bf16[2,2,128,1280]{3,2,1,0:T(8,128)(2,1)} %get-tuple-element.22.qt_in, ...), custom_call_target="tpu_custom_call" | custom-call | flops 8388608000 | bytes 8388608 | tf_op jit(solution)/shard_map/pallas_call | solution.py:245
  67.1 2.0 %collective-permute-start.18 = (bf16[256,256]{1,0:T(8,128)(2,1)S(1)}, bf16[256,256]{1,0:T(8,128)(2,1)S(1)}, u32[]{:S(2)}, u32[]{:S(2)}) collective-permute-start(bf16[256,256]{1,0:T(8,128)(2,1)S(1)} %slice.139), channel_id=1, source_target_pairs={{4,0},{5,1},{8,4},{9,5},{12,8},{13,9},{14,12},{15,13},{10,14},{11,... | collective-permute-start | bytes 393224 | tf_op jit(solution)/shard_map/ppermute | solution.py:276
  69.1 13.1 %shard_map.114 = (bf16[8,512,256]{2,1,0:T(8,128)(2,1)}, bf16[256,640]{1,0:T(8,128)(2,1)}, bf16[256,256]{1,0:T(8,128)(2,1)}, bf16[256,256]{1,0:T(8,128)(2,1)}) custom-call(s32[1]{0:T(128)} %bitcast.me_ref, s32[32]{0:T(128)} %get-tuple-element.20.plan, f32[2,2,1,1280]{3,2,1,0:T(1,128)} %get-tuple-element.21.delta_in, ...), custom_call_target="tpu_custom_call" | custom-call | flops 8388608000 | bytes 8388608 | tf_op jit(solution)/shard_map/pallas_call | solution.py:245
  82.3 2.0 %collective-permute-start.20 = (bf16[256,256]{1,0:T(8,128)(2,1)}, bf16[256,256]{1,0:T(8,128)(2,1)S(1)}, u32[]{:S(2)}, u32[]{:S(2)}) collective-permute-start(bf16[256,256]{1,0:T(8,128)(2,1)} %get-tuple-element.31), channel_id=1, source_target_pairs={{4,0},{5,1},{8,4},{9,5},{12,8},{13,9},{14,12},{15,13},{10,14},{11,... | collective-permute-start | bytes 393224 | tf_op jit(solution)/shard_map/ppermute | solution.py:288
  85.6 11.1 %shard_map.115 = (bf16[8,512,256]{2,1,0:T(8,128)(2,1)}, bf16[256,640]{1,0:T(8,128)(2,1)}) custom-call(s32[1]{0:T(128)} %bitcast.me_ref, s32[32]{0:T(128)} %get-tuple-element.20.plan, f32[2,2,1,1280]{3,2,1,0:T(1,128)} %get-tuple-element.21.delta_in, bf16[2,2,128,1280]{3,2,1,0:T(8,128)(2,1)} %get-tuple-element.22.qt_in, ...), custom_call_target="tpu_custom_call" | custom-call | flops 8388608000 | bytes 8388608 | tf_op jit(solution)/shard_map/pallas_call | solution.py:245
  97.7 13.2 %shard_map.116 = (bf16[8,512,256]{2,1,0:T(8,128)(2,1)}, bf16[256,640]{1,0:T(8,128)(2,1)}, bf16[256,256]{1,0:T(8,128)(2,1)}, bf16[256,256]{1,0:T(8,128)(2,1)}) custom-call(s32[1]{0:T(128)} %bitcast.me_ref, s32[32]{0:T(128)} %get-tuple-element.20.plan, f32[2,2,1,1280]{3,2,1,0:T(1,128)} %get-tuple-element.21.delta_in, ...), custom_call_target="tpu_custom_call" | custom-call | flops 8388608000 | bytes 8388608 | tf_op jit(solution)/shard_map/pallas_call | solution.py:245
  110.9 2.0 %collective-permute-start.33 = (bf16[256,256]{1,0:T(8,128)(2,1)}, bf16[256,256]{1,0:T(8,128)(2,1)S(1)}, u32[]{:S(2)}, u32[]{:S(2)}) collective-permute-start(bf16[256,256]{1,0:T(8,128)(2,1)} %get-tuple-element.36), channel_id=1, source_target_pairs={{4,0},{5,1},{8,4},{9,5},{12,8},{13,9},{14,12},{15,13},{10,14},{11,... | collective-permute-start | bytes 393224 | tf_op jit(solution)/shard_map/ppermute | solution.py:288
  117.6 2.3 %collective-permute-start.34 = (bf16[512,256]{1,0:T(8,128)(2,1)S(1)}, bf16[512,256]{1,0:T(8,128)(2,1)S(1)}, u32[]{:S(2)}, u32[]{:S(2)}) collective-permute-start(bf16[512,256]{1,0:T(8,128)(2,1)S(1)} %get-tuple-element.46), channel_id=1, source_target_pairs={{4,0},{5,1},{8,4},{9,5},{12,8},{13,9},{14,12},{15,13},{10,14},{11,... | collective-permute-start | bytes 786440 | tf_op jit(solution)/shard_map/ppermute | solution.py:300
  122.4 2.0 %collective-permute-start.26 = (bf16[512,256]{1,0:T(8,128)(2,1)S(1)}, bf16[512,256]{1,0:T(8,128)(2,1)S(1)}, u32[]{:S(2)}, u32[]{:S(2)}) collective-permute-start(bf16[512,256]{1,0:T(8,128)(2,1)S(1)} %get-tuple-element.40), channel_id=1, source_target_pairs={{4,0},{5,1},{8,4},{9,5},{12,8},{13,9},{14,12},{15,13},{10,14},{11,... | collective-permute-start | bytes 786440 | tf_op jit(solution)/shard_map/ppermute | solution.py:300
  124.4 3.3 %collective-permute-done.30 = bf16[512,256]{1,0:T(8,128)(2,1)S(1)} collective-permute-done((bf16[512,256]{1,0:T(8,128)(2,1)S(1)}, bf16[512,256]{1,0:T(8,128)(2,1)S(1)}, u32[]{:S(2)}, u32[]{:S(2)}) %collective-permute-start.30) | collective-permute-done | bytes 262176 | tf_op jit(solution)/shard_map/ppermute | solution.py:299
  128.1 2.0 %collective-permute-start.35 = (bf16[512,256]{1,0:T(8,128)(2,1)S(1)}, bf16[512,256]{1,0:T(8,128)(2,1)S(1)}, u32[]{:S(2)}, u32[]{:S(2)}) collective-permute-start(bf16[512,256]{1,0:T(8,128)(2,1)S(1)} %get-tuple-element.44), channel_id=1, source_target_pairs={{4,0},{5,1},{8,4},{9,5},{12,8},{13,9},{14,12},{15,13},{10,14},{11,... | collective-permute-start | bytes 786440 | tf_op jit(solution)/shard_map/ppermute | solution.py:300
  130.1 3.2 %collective-permute-done.23 = bf16[512,256]{1,0:T(8,128)(2,1)S(1)} collective-permute-done((bf16[512,256]{1,0:T(8,128)(2,1)S(1)}, bf16[512,256]{1,0:T(8,128)(2,1)S(1)}, u32[]{:S(2)}, u32[]{:S(2)}) %collective-permute-start.23) | collective-permute-done | bytes 262176 | tf_op jit(solution)/shard_map/ppermute | solution.py:299
  133.7 2.0 %collective-permute-start.27 = (bf16[512,256]{1,0:T(8,128)(2,1)S(1)}, bf16[512,256]{1,0:T(8,128)(2,1)S(1)}, u32[]{:S(2)}, u32[]{:S(2)}) collective-permute-start(bf16[512,256]{1,0:T(8,128)(2,1)S(1)} %get-tuple-element.38), channel_id=1, source_target_pairs={{4,0},{5,1},{8,4},{9,5},{12,8},{13,9},{14,12},{15,13},{10,14},{11,... | collective-permute-start | bytes 786440 | tf_op jit(solution)/shard_map/ppermute | solution.py:300
  135.6 3.3 %collective-permute-done.31 = bf16[512,256]{1,0:T(8,128)(2,1)S(1)} collective-permute-done((bf16[512,256]{1,0:T(8,128)(2,1)S(1)}, bf16[512,256]{1,0:T(8,128)(2,1)S(1)}, u32[]{:S(2)}, u32[]{:S(2)}) %collective-permute-start.31) | collective-permute-done | bytes 262176 | tf_op jit(solution)/shard_map/ppermute | solution.py:299
  139.3 2.0 %collective-permute-start.36 = (bf16[512,256]{1,0:T(8,128)(2,1)S(1)}, bf16[512,256]{1,0:T(8,128)(2,1)S(1)}, u32[]{:S(2)}, u32[]{:S(2)}) collective-permute-start(bf16[512,256]{1,0:T(8,128)(2,1)S(1)} %get-tuple-element.42), channel_id=1, source_target_pairs={{4,0},{5,1},{8,4},{9,5},{12,8},{13,9},{14,12},{15,13},{10,14},{11,... | collective-permute-start | bytes 786440 | tf_op jit(solution)/shard_map/ppermute | solution.py:300
  142.4 2.1 %collective-permute-done.24 = bf16[512,256]{1,0:T(8,128)(2,1)S(1)} collective-permute-done((bf16[512,256]{1,0:T(8,128)(2,1)S(1)}, bf16[512,256]{1,0:T(8,128)(2,1)S(1)}, u32[]{:S(2)}, u32[]{:S(2)}) %collective-permute-start.24) | collective-permute-done | bytes 262176 | tf_op jit(solution)/shard_map/ppermute | solution.py:299
  144.9 4.9 %collective-permute-done.32 = bf16[512,256]{1,0:T(8,128)(2,1)S(1)} collective-permute-done((bf16[512,256]{1,0:T(8,128)(2,1)S(1)}, bf16[512,256]{1,0:T(8,128)(2,1)S(1)}, u32[]{:S(2)}, u32[]{:S(2)}) %collective-permute-start.32) | collective-permute-done | bytes 262176 | tf_op jit(solution)/shard_map/ppermute | solution.py:299
  (143 shorter events, 37.6 us)
Async XLA Ops:
  4.6 15.9 %collective-permute-start = (bf16[256,3840]{1,0:T(8,128)(2,1)}, bf16[256,3840]{1,0:T(8,128)(2,1)S(1)}, u32[]{:S(2)}, u32[]{:S(2)}) collective-permute-start(bf16[256,3840]{1,0:T(8,128)(2,1)} %pad_maximum_fusion), channel_id=1, source_target_pairs={{0,1},{1,0},{2,3},{3,2},{4,5},{5,4},{6,7},{7,6},{8,9},{9,8},{10,11... | collective-permute-start | bytes 5898248 | tf_op jit(solution)/shard_map/ppermute | solution.py:332
  18.5 11.6 %collective-permute-start.6 = (bf16[512,256]{1,0:T(8,128)(2,1)S(1)}, bf16[512,256]{1,0:T(8,128)(2,1)S(1)}, u32[]{:S(2)}, u32[]{:S(2)}) collective-permute-start(bf16[512,256]{1,0:T(8,128)(2,1)S(1)} %collective-permute-done.5.refs_6_), channel_id=1, source_target_pairs={{0,4},{1,5},{4,8},{5,9},{8,12},{9,13},{12,14},{13,15},{14,10},{15,... | collective-permute-start | bytes 786440 | tf_op jit(solution)/shard_map/ppermute | solution.py:272
  20.3 13.8 %collective-permute-start.3 = (bf16[512,256]{1,0:T(8,128)(2,1)S(1)}, bf16[512,256]{1,0:T(8,128)(2,1)S(1)}, u32[]{:S(2)}, u32[]{:S(2)}) collective-permute-start(bf16[512,256]{1,0:T(8,128)(2,1)S(1)} %collective-permute-done.2.refs_1_), channel_id=1, source_target_pairs={{4,0},{5,1},{8,4},{9,5},{12,8},{13,9},{14,12},{15,13},{10,14},{11,... | collective-permute-start | bytes 786440 | tf_op jit(solution)/shard_map/ppermute | solution.py:273
  32.3 12.8 %collective-permute-start.7 = (bf16[512,256]{1,0:T(8,128)(2,1)S(1)}, bf16[512,256]{1,0:T(8,128)(2,1)S(1)}, u32[]{:S(2)}, u32[]{:S(2)}) collective-permute-start(bf16[512,256]{1,0:T(8,128)(2,1)S(1)} %collective-permute-done.6.refs_5_), channel_id=1, source_target_pairs={{0,4},{1,5},{4,8},{5,9},{8,12},{9,13},{12,14},{13,15},{14,10},{15,... | collective-permute-start | bytes 786440 | tf_op jit(solution)/shard_map/ppermute | solution.py:272
  34.1 12.9 %collective-permute-start.4 = (bf16[512,256]{1,0:T(8,128)(2,1)S(1)}, bf16[512,256]{1,0:T(8,128)(2,1)S(1)}, u32[]{:S(2)}, u32[]{:S(2)}) collective-permute-start(bf16[512,256]{1,0:T(8,128)(2,1)S(1)} %collective-permute-done.3.refs_2_), channel_id=1, source_target_pairs={{4,0},{5,1},{8,4},{9,5},{12,8},{13,9},{14,12},{15,13},{10,14},{11,... | collective-permute-start | bytes 786440 | tf_op jit(solution)/shard_map/ppermute | solution.py:273
  39.5 11.2 %collective-permute-start.11 = (bf16[512,256]{1,0:T(8,128)(2,1)S(1)}, bf16[512,256]{1,0:T(8,128)(2,1)S(1)}, u32[]{:S(2)}, u32[]{:S(2)}) collective-permute-start(bf16[512,256]{1,0:T(8,128)(2,1)S(1)} %collective-permute-done.10.refs_6_), channel_id=1, source_target_pairs={{0,4},{1,5},{4,8},{5,9},{8,12},{9,13},{12,14},{13,15},{14,10},{15,... | collective-permute-start | bytes 786440 | tf_op jit(solution)/shard_map/ppermute | solution.py:272
  41.3 11.2 %collective-permute-start.13 = (bf16[512,256]{1,0:T(8,128)(2,1)S(1)}, bf16[512,256]{1,0:T(8,128)(2,1)S(1)}, u32[]{:S(2)}, u32[]{:S(2)}) collective-permute-start(bf16[512,256]{1,0:T(8,128)(2,1)S(1)} %collective-permute-done.12.refs_1_), channel_id=1, source_target_pairs={{4,0},{5,1},{8,4},{9,5},{12,8},{13,9},{14,12},{15,13},{10,14},{11,... | collective-permute-start | bytes 786440 | tf_op jit(solution)/shard_map/ppermute | solution.py:273
  50.8 16.2 %collective-permute-start.14 = (bf16[512,256]{1,0:T(8,128)(2,1)S(1)}, bf16[512,256]{1,0:T(8,128)(2,1)S(1)}, u32[]{:S(2)}, u32[]{:S(2)}) collective-permute-start(bf16[512,256]{1,0:T(8,128)(2,1)S(1)} %collective-permute-done.11.refs_9_.refs_5_), channel_id=1, source_target_pairs={{0,4},{1,5},{4,8},{5,9},{8,12},{9,13},{12,14},{13,15},{14,10},{15,... | collective-permute-start | bytes 786440 | tf_op jit(solution)/shard_map/ppermute | solution.py:272
  52.6 14.5 %collective-permute-start.15 = (bf16[512,256]{1,0:T(8,128)(2,1)S(1)}, bf16[512,256]{1,0:T(8,128)(2,1)S(1)}, u32[]{:S(2)}, u32[]{:S(2)}) collective-permute-start(bf16[512,256]{1,0:T(8,128)(2,1)S(1)} %collective-permute-done.13.refs_10_.refs_2_), channel_id=1, source_target_pairs={{4,0},{5,1},{8,4},{9,5},{12,8},{13,9},{14,12},{15,13},{10,14},{11,... | collective-permute-start | bytes 786440 | tf_op jit(solution)/shard_map/ppermute | solution.py:273
  67.0 17.3 %collective-permute-start.17 = (bf16[256,256]{1,0:T(8,128)(2,1)S(1)}, bf16[256,256]{1,0:T(8,128)(2,1)S(1)}, u32[]{:S(2)}, u32[]{:S(2)}) collective-permute-start(bf16[256,256]{1,0:T(8,128)(2,1)S(1)} %slice.138), channel_id=1, source_target_pairs={{0,4},{1,5},{4,8},{5,9},{8,12},{9,13},{12,14},{13,15},{14,10},{15,... | collective-permute-start | bytes 393224 | tf_op jit(solution)/shard_map/ppermute | solution.py:275
  67.1 17.2 %collective-permute-start.18 = (bf16[256,256]{1,0:T(8,128)(2,1)S(1)}, bf16[256,256]{1,0:T(8,128)(2,1)S(1)}, u32[]{:S(2)}, u32[]{:S(2)}) collective-permute-start(bf16[256,256]{1,0:T(8,128)(2,1)S(1)} %slice.139), channel_id=1, source_target_pairs={{4,0},{5,1},{8,4},{9,5},{12,8},{13,9},{14,12},{15,13},{10,14},{11,... | collective-permute-start | bytes 393224 | tf_op jit(solution)/shard_map/ppermute | solution.py:276
  82.2 14.6 %collective-permute-start.19 = (bf16[256,256]{1,0:T(8,128)(2,1)}, bf16[256,256]{1,0:T(8,128)(2,1)S(1)}, u32[]{:S(2)}, u32[]{:S(2)}) collective-permute-start(bf16[256,256]{1,0:T(8,128)(2,1)} %get-tuple-element.29), channel_id=1, source_target_pairs={{0,4},{1,5},{4,8},{5,9},{8,12},{9,13},{12,14},{13,15},{14,10},{15,... | collective-permute-start | bytes 393224 | tf_op jit(solution)/shard_map/ppermute | solution.py:287
  82.3 14.5 %collective-permute-start.20 = (bf16[256,256]{1,0:T(8,128)(2,1)}, bf16[256,256]{1,0:T(8,128)(2,1)S(1)}, u32[]{:S(2)}, u32[]{:S(2)}) collective-permute-start(bf16[256,256]{1,0:T(8,128)(2,1)} %get-tuple-element.31), channel_id=1, source_target_pairs={{4,0},{5,1},{8,4},{9,5},{12,8},{13,9},{14,12},{15,13},{10,14},{11,... | collective-permute-start | bytes 393224 | tf_op jit(solution)/shard_map/ppermute | solution.py:288
  117.4 10.3 %collective-permute-start.30 = (bf16[512,256]{1,0:T(8,128)(2,1)S(1)}, bf16[512,256]{1,0:T(8,128)(2,1)S(1)}, u32[]{:S(2)}, u32[]{:S(2)}) collective-permute-start(bf16[512,256]{1,0:T(8,128)(2,1)S(1)} %get-tuple-element.45), channel_id=1, source_target_pairs={{0,4},{1,5},{4,8},{5,9},{8,12},{9,13},{12,14},{13,15},{14,10},{15,... | collective-permute-start | bytes 786440 | tf_op jit(solution)/shard_map/ppermute | solution.py:299
  117.6 10.1 %collective-permute-start.34 = (bf16[512,256]{1,0:T(8,128)(2,1)S(1)}, bf16[512,256]{1,0:T(8,128)(2,1)S(1)}, u32[]{:S(2)}, u32[]{:S(2)}) collective-permute-start(bf16[512,256]{1,0:T(8,128)(2,1)S(1)} %get-tuple-element.46), channel_id=1, source_target_pairs={{4,0},{5,1},{8,4},{9,5},{12,8},{13,9},{14,12},{15,13},{10,14},{11,... | collective-permute-start | bytes 786440 | tf_op jit(solution)/shard_map/ppermute | solution.py:300
  120.1 10.0 %collective-permute-start.21 = (bf16[256,640]{1,0:T(8,128)(2,1)S(1)}, bf16[256,640]{1,0:T(8,128)(2,1)S(1)}, u32[]{:S(2)}, u32[]{:S(2)}) collective-permute-start(bf16[256,640]{1,0:T(8,128)(2,1)S(1)} %copy-done.16), channel_id=1, source_target_pairs={{0,1},{1,0},{2,3},{3,2},{4,5},{5,4},{6,7},{7,6},{8,9},{9,8},{10,11... | collective-permute-start | bytes 983048 | tf_op jit(solution)/shard_map/ppermute | solution.py:351
  122.3 11.0 %collective-permute-start.23 = (bf16[512,256]{1,0:T(8,128)(2,1)S(1)}, bf16[512,256]{1,0:T(8,128)(2,1)S(1)}, u32[]{:S(2)}, u32[]{:S(2)}) collective-permute-start(bf16[512,256]{1,0:T(8,128)(2,1)S(1)} %get-tuple-element.39), channel_id=1, source_target_pairs={{0,4},{1,5},{4,8},{5,9},{8,12},{9,13},{12,14},{13,15},{14,10},{15,... | collective-permute-start | bytes 786440 | tf_op jit(solution)/shard_map/ppermute | solution.py:299
  122.4 11.0 %collective-permute-start.26 = (bf16[512,256]{1,0:T(8,128)(2,1)S(1)}, bf16[512,256]{1,0:T(8,128)(2,1)S(1)}, u32[]{:S(2)}, u32[]{:S(2)}) collective-permute-start(bf16[512,256]{1,0:T(8,128)(2,1)S(1)} %get-tuple-element.40), channel_id=1, source_target_pairs={{4,0},{5,1},{8,4},{9,5},{12,8},{13,9},{14,12},{15,13},{10,14},{11,... | collective-permute-start | bytes 786440 | tf_op jit(solution)/shard_map/ppermute | solution.py:300
  127.9 11.0 %collective-permute-start.31 = (bf16[512,256]{1,0:T(8,128)(2,1)S(1)}, bf16[512,256]{1,0:T(8,128)(2,1)S(1)}, u32[]{:S(2)}, u32[]{:S(2)}) collective-permute-start(bf16[512,256]{1,0:T(8,128)(2,1)S(1)} %get-tuple-element.43), channel_id=1, source_target_pairs={{0,4},{1,5},{4,8},{5,9},{8,12},{9,13},{12,14},{13,15},{14,10},{15,... | collective-permute-start | bytes 786440 | tf_op jit(solution)/shard_map/ppermute | solution.py:299
  128.1 11.0 %collective-permute-start.35 = (bf16[512,256]{1,0:T(8,128)(2,1)S(1)}, bf16[512,256]{1,0:T(8,128)(2,1)S(1)}, u32[]{:S(2)}, u32[]{:S(2)}) collective-permute-start(bf16[512,256]{1,0:T(8,128)(2,1)S(1)} %get-tuple-element.44), channel_id=1, source_target_pairs={{4,0},{5,1},{8,4},{9,5},{12,8},{13,9},{14,12},{15,13},{10,14},{11,... | collective-permute-start | bytes 786440 | tf_op jit(solution)/shard_map/ppermute | solution.py:300
  133.5 11.0 %collective-permute-start.24 = (bf16[512,256]{1,0:T(8,128)(2,1)S(1)}, bf16[512,256]{1,0:T(8,128)(2,1)S(1)}, u32[]{:S(2)}, u32[]{:S(2)}) collective-permute-start(bf16[512,256]{1,0:T(8,128)(2,1)S(1)} %get-tuple-element.37), channel_id=1, source_target_pairs={{0,4},{1,5},{4,8},{5,9},{8,12},{9,13},{12,14},{13,15},{14,10},{15,... | collective-permute-start | bytes 786440 | tf_op jit(solution)/shard_map/ppermute | solution.py:299
  133.7 11.0 %collective-permute-start.27 = (bf16[512,256]{1,0:T(8,128)(2,1)S(1)}, bf16[512,256]{1,0:T(8,128)(2,1)S(1)}, u32[]{:S(2)}, u32[]{:S(2)}) collective-permute-start(bf16[512,256]{1,0:T(8,128)(2,1)S(1)} %get-tuple-element.38), channel_id=1, source_target_pairs={{4,0},{5,1},{8,4},{9,5},{12,8},{13,9},{14,12},{15,13},{10,14},{11,... | collective-permute-start | bytes 786440 | tf_op jit(solution)/shard_map/ppermute | solution.py:300
  139.2 10.6 %collective-permute-start.32 = (bf16[512,256]{1,0:T(8,128)(2,1)S(1)}, bf16[512,256]{1,0:T(8,128)(2,1)S(1)}, u32[]{:S(2)}, u32[]{:S(2)}) collective-permute-start(bf16[512,256]{1,0:T(8,128)(2,1)S(1)} %get-tuple-element.41), channel_id=1, source_target_pairs={{0,4},{1,5},{4,8},{5,9},{8,12},{9,13},{12,14},{13,15},{14,10},{15,... | collective-permute-start | bytes 786440 | tf_op jit(solution)/shard_map/ppermute | solution.py:299
  139.3 10.6 %collective-permute-start.36 = (bf16[512,256]{1,0:T(8,128)(2,1)S(1)}, bf16[512,256]{1,0:T(8,128)(2,1)S(1)}, u32[]{:S(2)}, u32[]{:S(2)}) collective-permute-start(bf16[512,256]{1,0:T(8,128)(2,1)S(1)} %get-tuple-element.42), channel_id=1, source_target_pairs={{4,0},{5,1},{8,4},{9,5},{12,8},{13,9},{14,12},{15,13},{10,14},{11,... | collective-permute-start | bytes 786440 | tf_op jit(solution)/shard_map/ppermute | solution.py:300
  (42 other events, 486.7 us)

commit v6 on v3

v6 whole, which is shorter than its diff:
```python
import functools
import math

import jax
import jax.numpy as jnp
from jax import lax
from jax.experimental import pallas as pl
from jax.experimental.pallas import tpu as pltpu
from jax.sharding import PartitionSpec as P

HQ = 20
HK = 4
DH = 128
PER = HQ // HK
HALF = HK // 2
WIDE = PER * DH
ANCESTORS = 5
SLOTS = ANCESTORS + 1
OWN = 1 << 20
SCALE = 1.0 / math.sqrt(DH)
EXP_SCALE = SCALE / math.log(2.0)
NN = (((1,), (0,)), ((), ()))
SMEM = pl.BlockSpec(memory_space=pltpu.SMEM)
HBM = pl.BlockSpec(memory_space=pl.ANY)
VMEM = pl.BlockSpec(memory_space=pltpu.VMEM)


def dot(a, b):
    return lax.dot_general(a, b, NN, preferred_element_type=jnp.float32)


def ring_order(chips):
    if chips == 8:
        return [0, 2, 4, 6, 7, 5, 3, 1]
    return list(range(chips))


def walk(device, me, places, parents, assignment, lengths, owner, plan, side):
    chips = places.shape[0]
    here = places[me // 2]

    def place(held):
        at = places[held // 2] - here
        at = jnp.where(at < 0, at + chips, at)
        return side * 2 * chips + at * 2 + jnp.where(held % 2 == me % 2, 0, 1)

    def clear(at, carry):
        plan[side * 2 * chips + at] = 0
        return carry

    lax.fori_loop(0, 2 * chips, clear, 0)
    segment = assignment[device]
    plan[place(device)] = OWN
    up = parents[segment]
    for _ in range(ANCESTORS):
        at = jnp.maximum(up, 0)

        @pl.when(up >= 0)
        def _():
            plan[place(owner[at])] = lengths[at]

        up = jnp.where(up >= 0, parents[at], -1)


def run_copies(pairs, sems):
    copies = [pltpu.make_async_copy(a, b, sems.at[i]) for i, (a, b) in enumerate(pairs)]
    for copy in copies:
        copy.start()
    return copies


def column_of(me, head, h):
    return pl.multiple_of(((me % 2 * HALF + head) * PER + h) * DH, DH)


def masked_scores(keys, queries, sees):
    rows = keys.shape[0]
    lane_at = lax.broadcasted_iota(jnp.int32, (1, PER * rows), 1) % rows
    key_at = lax.broadcasted_iota(jnp.int32, (rows, 1), 0)
    seen = key_at <= jnp.where(sees == OWN, lane_at, sees - 1)
    return dot(keys, queries), seen


def measure_block(sees, keys, queries, top_ref, sum_ref, at):
    rows = keys.shape[0]
    s, seen = masked_scores(keys, queries, sees)
    s = jnp.where(seen, s, -1e30)
    old = top_ref[at]
    top = jnp.maximum(old, jnp.max(s, axis=0, keepdims=True))
    w = jnp.exp2((s - top) * EXP_SCALE)
    top_ref[at] = top
    total = jnp.sum(w.reshape(rows // 8, 8, PER * rows), axis=0)
    sum_ref[at] = sum_ref[at] * jnp.exp2((old - top) * EXP_SCALE) + jnp.sum(total, axis=0, keepdims=True)


def measure_blocks(plan, offsets, kv_ref, qt_ref, top_ref, sum_ref):
    rows = kv_ref.shape[2] // 2
    chips = plan.shape[0] // 4
    for slot, offset in enumerate(offsets):
        def visit(i, carry):
            half, side = i // 2, i % 2
            sees = plan[side * 2 * chips + offset * 2 + half]

            @pl.when(sees > 0)
            def _():
                for head in range(HALF):
                    keys = kv_ref[slot, head, pl.ds(pl.multiple_of(half * rows, rows), rows), :DH]
                    measure_block(sees, keys, qt_ref[head, side], top_ref, sum_ref, (head, side))

            return carry

        lax.fori_loop(0, 4, visit, 0)


def prepare_kernel(me_ref, places, parents, assignment, lengths, queries, grads, saved, other, *refs):
    blocks, refs = refs[:HALF], refs[HALF:]
    (plan, qt_ref, gt_ref, gm_ref, qm_ref, delta_ref, top_ref, sum_ref,
     owner, q_ref, g_ref, o_ref, kv_ref, sems) = refs
    rows = queries.shape[0]
    me = me_ref[0]
    width = HALF * WIDE
    column = pl.multiple_of(me % 2 * width, width)
    pairs = []
    for at, (array, held) in enumerate(zip((queries, grads, saved), (q_ref, g_ref, o_ref))):
        pairs.append((array.at[:, pl.ds(column, width)], held.at[0]))
        pairs.append((other.at[:, at * width:(at + 1) * width], held.at[1]))
    for head in range(HALF):
        pairs.append((blocks[head], kv_ref.at[0, head]))
    copies = run_copies(pairs, sems)

    def invert(d, carry):
        owner[assignment[d]] = d
        return carry

    lax.fori_loop(0, assignment.shape[0], invert, 0)
    walk(me, me, places, parents, assignment, lengths, owner, plan, 0)
    walk(me + 1 - me % 2 * 2, me, places, parents, assignment, lengths, owner, plan, 1)
    row_at = lax.broadcasted_iota(jnp.int32, (rows, 1), 0)
    top_ref[...] = jnp.full(top_ref.shape, -1e30, top_ref.dtype)
    sum_ref[...] = jnp.zeros_like(sum_ref)
    for copy in copies:
        copy.wait()
    for side, device in enumerate((me, me + 1 - me % 2 * 2)):
        live = row_at < lengths[assignment[device]]
        for head in range(HALF):
            for h in range(PER):
                lanes = slice(h * rows, (h + 1) * rows)
                cols = slice((head * PER + h) * DH, (head * PER + h + 1) * DH)
                masked = jnp.where(live, g_ref[side, :, cols], jnp.zeros((), g_ref.dtype))
                query = q_ref[side, :, cols]
                gm_ref[head, side, lanes, :] = masked
                qm_ref[head, side, lanes, :] = query
                gt_ref[head, side, :, lanes] = masked.T
                qt_ref[head, side, :, lanes] = query.T
                terms = masked.astype(jnp.float32) * o_ref[side, :, cols].astype(jnp.float32)
                delta_ref[head, side, :, lanes] = jnp.sum(terms.T, axis=0, keepdims=True)
    measure_blocks(plan, [0], kv_ref, qt_ref, top_ref, sum_ref)


def row_stats(rows):
    return jax.ShapeDtypeStruct((HALF, 2, 1, PER * rows), jnp.float32)


def prepare(tables, mine, other, blocks):
    rows = other.shape[0]
    chips = tables[1].shape[0]
    bf16 = jnp.bfloat16
    return pl.pallas_call(
        prepare_kernel,
        in_specs=[SMEM] * 5 + [HBM] * (4 + HALF),
        out_specs=[SMEM] + [VMEM] * 7,
        out_shape=[
            jax.ShapeDtypeStruct((4 * chips,), jnp.int32),
            jax.ShapeDtypeStruct((HALF, 2, DH, PER * rows), bf16),
            jax.ShapeDtypeStruct((HALF, 2, DH, PER * rows), bf16),
            jax.ShapeDtypeStruct((HALF, 2, PER * rows, DH), bf16),
            jax.ShapeDtypeStruct((HALF, 2, PER * rows, DH), bf16),
            row_stats(rows),
            row_stats(rows),
            row_stats(rows),
        ],
        scratch_shapes=[pltpu.SMEM(tables[3].shape, jnp.int32)]
        + [pltpu.VMEM((2, rows, HALF * WIDE), bf16)] * 3
        + [pltpu.VMEM((1, HALF, 2 * rows, 2 * DH), bf16), pltpu.SemaphoreType.DMA((6 + HALF,))],
        compiler_params=pltpu.CompilerParams(vmem_limit_bytes=28 << 20),
        cost_estimate=pl.CostEstimate(flops=0, bytes_accessed=24 << 20, transcendentals=0),
    )(*tables, *mine, other, *blocks)


def measure_kernel(offsets, plan, qt_in, top_in, sum_in, *refs):
    count = len(offsets) * HALF
    blocks, (top_ref, sum_ref, qt_ref, kv_ref, sems) = refs[:count], refs[count:]
    pairs = [(qt_in, qt_ref), (top_in, top_ref), (sum_in, sum_ref)]
    pairs += [(held, kv_ref.at[i // HALF, i % HALF]) for i, held in enumerate(blocks)]
    for copy in run_copies(pairs, sems):
        copy.wait()
    measure_blocks(plan, offsets, kv_ref, qt_ref, top_ref, sum_ref)


def measure(offsets, plan, qt, top, total, blocks):
    rows = blocks[0].shape[0] // 2
    return pl.pallas_call(
        functools.partial(measure_kernel, offsets),
        in_specs=[SMEM] + [HBM] * (3 + len(blocks)),
        out_specs=[VMEM] * 2,
        out_shape=[row_stats(rows)] * 2,
        scratch_shapes=[
            pltpu.VMEM(qt.shape, qt.dtype),
            pltpu.VMEM((len(offsets), HALF, 2 * rows, 2 * DH), jnp.bfloat16),
            pltpu.SemaphoreType.DMA((3 + len(blocks),)),
        ],
        compiler_params=pltpu.CompilerParams(vmem_limit_bytes=20 << 20),
        cost_estimate=pl.CostEstimate(flops=0, bytes_accessed=12 << 20, transcendentals=0),
    )(plan, qt, top, total, *blocks)


def grads_kernel(chips, plan, qt_in, gt_in, gm_in, qm_in, delta_in, top_in, sum_in, *refs):
    count = HALF * (chips + 1)
    blocks, refs = refs[:count], refs[count:]
    terms, ups, downs = refs[:HALF], refs[HALF:2 * HALF], refs[2 * HALF:3 * HALF]
    (dq_mine, dq_other, qt_ref, gt_ref, gm_ref, qm_ref, delta_ref, top_ref, sum_ref, kv_ref,
     acc_ref, stage_ref, dqt_ref, sems, kv_sems, out_sems) = refs[3 * HALF:]
    rows = dq_mine.shape[0]
    far = chips // 2
    pairs = []
    for head in range(HALF):
        pairs.append((blocks[head * (chips + 1) + chips - 1], kv_ref.at[far, head, :rows]))
        pairs.append((blocks[head * (chips + 1) + chips], kv_ref.at[far, head, rows:]))
    shared = zip((qt_in, gt_in, gm_in, qm_in, delta_in, top_in, sum_in),
                 (qt_ref, gt_ref, gm_ref, qm_ref, delta_ref, top_ref, sum_ref))
    copies = run_copies(pairs + list(shared), sems)
    rest = [at for at in range(chips) if at != far]
    for slot, at in enumerate(rest):
        for head in range(HALF):
            pltpu.make_async_copy(
                blocks[head * (chips + 1) + slot], kv_ref.at[at, head], kv_sems.at[at, head]
            ).start()
    dqt_ref[...] = jnp.zeros_like(dqt_ref)
    for copy in copies:
        copy.wait()
    measure_blocks(plan, [far], kv_ref.at[pl.ds(far, 1)], qt_ref, top_ref, sum_ref)
    top_ref[...] = top_ref[...] * EXP_SCALE + jnp.log2(sum_ref[...])

    def out_copy(slot, head, target):
        return pltpu.make_async_copy(stage_ref.at[slot, head], target, out_sems.at[slot, head])

    def visit(i, carry):
        step = i // 2
        half = i % 2
        offset = jnp.where(step % 2 == 1, far + (step + 1) // 2, far - step // 2)
        offset = jnp.where(offset >= chips, offset - chips, offset)
        slot = i % 2
        here = pl.ds(pl.multiple_of(half * rows, rows), rows)

        @pl.when((half == 0) & (offset != far))
        def _():
            for head in range(HALF):
                pltpu.make_async_copy(
                    blocks[0], kv_ref.at[offset, head], kv_sems.at[offset, head]
                ).wait()

        @pl.when(i >= 2)
        def _():
            for head in range(HALF):
                out_copy(slot, head, ups[0]).wait()

        acc_ref[...] = jnp.zeros_like(acc_ref)

        def look(side, carry):
            sees = plan[side * 2 * chips + offset * 2 + half]

            @pl.when(sees > 0)
            def _():
                for head in range(HALF):
                    at = (head, side)
                    k = kv_ref[offset, head, here, :DH]
                    v = kv_ref[offset, head, here, DH:]
                    s, seen = masked_scores(k, qt_ref[at], sees)
                    p = jnp.where(seen, jnp.exp2(s * EXP_SCALE - top_ref[at]), 0.0)
                    ds = (p * (dot(v, gt_ref[at]) - delta_ref[at])).astype(jnp.bfloat16)
                    acc_ref[head, :, DH:] += dot(p.astype(jnp.bfloat16), gm_ref[at])
                    acc_ref[head, :, :DH] += dot(ds, qm_ref[at])
                    dqt_ref[at] += dot(k.T, ds)

            return carry

        lax.fori_loop(0, 2, look, 0)
        for head in range(HALF):
            stage_ref[slot, head, :, :DH] = (acc_ref[head, :, :DH] * SCALE).astype(stage_ref.dtype)
            stage_ref[slot, head, :, DH:] = acc_ref[head, :, DH:].astype(stage_ref.dtype)

        for head in range(HALF):
            @pl.when(offset != far)
            def _():
                out_copy(slot, head, terms[head].at[offset, here]).start()

            @pl.when((offset == far) & (half == 0))
            def _():
                out_copy(slot, head, ups[head]).start()

            @pl.when((offset == far) & (half == 1))
            def _():
                out_copy(slot, head, downs[head]).start()

        return carry

    lax.fori_loop(0, 2 * chips, visit, 0)
    for side, dq_ref in enumerate((dq_mine, dq_other)):
        for head in range(HALF):
            for h in range(PER):
                dq = dqt_ref[head, side, :, h * rows:(h + 1) * rows].T * SCALE
                dq_ref[:, (head * PER + h) * DH:(head * PER + h + 1) * DH] = dq.astype(dq_ref.dtype)
    for slot in range(2):
        for head in range(HALF):
            out_copy(slot, head, ups[0]).wait()


def gradients(prepared, top, total, gathered):
    plan, qt, gt, gm, qm, delta = prepared[:6]
    chips = plan.shape[0] // 4
    rows = gm.shape[2] // PER
    bf16, f32 = jnp.bfloat16, jnp.float32
    blocks = [block for head in gathered for block in head]
    shared = (qt, gt, gm, qm, delta, top, total)
    dense = jax.ShapeDtypeStruct((chips, 2 * rows, 2 * DH), bf16)
    piece = jax.ShapeDtypeStruct((rows, 2 * DH), bf16)
    query = jax.ShapeDtypeStruct((rows, HALF * WIDE), bf16)
    return pl.pallas_call(
        functools.partial(grads_kernel, chips),
        in_specs=[SMEM] + [HBM] * (len(shared) + len(blocks)),
        out_specs=[HBM] * (3 * HALF) + [VMEM] * 2,
        out_shape=[dense] * HALF + [piece] * (2 * HALF) + [query] * 2,
        scratch_shapes=[pltpu.VMEM(array.shape, array.dtype) for array in shared]
        + [
            pltpu.VMEM((chips, HALF, 2 * rows, 2 * DH), bf16),
            pltpu.VMEM((HALF, rows, 2 * DH), f32),
            pltpu.VMEM((2, HALF, rows, 2 * DH), bf16),
            pltpu.VMEM((HALF, 2, DH, PER * rows), f32),
            pltpu.SemaphoreType.DMA((2 * HALF + len(shared),)),
            pltpu.SemaphoreType.DMA((chips, HALF)),
            pltpu.SemaphoreType.DMA((2, HALF)),
        ],
        compiler_params=pltpu.CompilerParams(vmem_limit_bytes=(32 << 20) + (chips << 19)),
        cost_estimate=pl.CostEstimate(flops=20 << 30, bytes_accessed=16 << 20, transcendentals=0),
    )(plan, *shared, *blocks)


def spread(block, right, left, chips):
    far, rows = chips // 2, block.shape[0] // 2
    got = {0: block}
    up = down = block
    for step in range(1, far):
        up = got[chips - step] = lax.ppermute(up, "leaf", right)
        down = got[step] = lax.ppermute(down, "leaf", left)
    up = lax.ppermute(up[:rows], "leaf", right)
    down = lax.ppermute(down[rows:], "leaf", left)
    return [got[at] for at in range(chips) if at != far] + [up, down]


def wide(x):
    return x.astype(jnp.float32)


def collect(terms, up, down, right, left):
    chips, rows = terms.shape[0], up.shape[0]
    up = lax.ppermute(up, "leaf", right)
    down = lax.ppermute(down, "leaf", left)
    up = jnp.pad(wide(up), ((0, rows), (0, 0)))
    down = jnp.pad(wide(down), ((rows, 0), (0, 0)))
    for step in range(chips // 2 - 1, 0, -1):
        up = wide(lax.ppermute((up + wide(terms[step])).astype(terms.dtype), "leaf", right))
        down = wide(lax.ppermute((down + wide(terms[chips - step])).astype(terms.dtype), "leaf", left))
    return (wide(terms[0]) + up + down).astype(terms.dtype)


def local(queries, keys, values, saved_out, grad_out, parents, assignment, lengths):
    rows = keys.shape[0]
    chips = lax.axis_size("leaf") // 2
    order = ring_order(chips)
    ahead = [(order[i], order[(i + 1) % chips]) for i in range(chips)]
    right = [(2 * a + c, 2 * b + c) for a, b in ahead for c in range(2)]
    left = [(b, a) for a, b in right]
    swap = [(2 * a + c, 2 * a + 1 - c) for a in range(chips) for c in range(2)]
    places = jnp.asarray([order.index(chip) for chip in range(chips)], jnp.int32)
    index = lax.axis_index("leaf").astype(jnp.int32)
    core = index % 2
    me = index.reshape(1)
    tables = (me, places, parents, assignment, lengths)

    def part(array, which, width):
        return lax.dynamic_slice(array, (0, which * width), (rows, width))

    def heads_of(which):
        pieces = [part(array, which * HALF + head, DH) for head in range(HALF) for array in (keys, values)]
        return jnp.concatenate(pieces, axis=1)

    kept = heads_of(core)
    got = lax.ppermute(heads_of(1 - core), "leaf", swap)
    gathered = []
    for head in range(HALF):
        cols = slice(head * 2 * DH, (head + 1) * 2 * DH)
        block = jnp.concatenate([kept[:, cols], got[:, cols]], axis=0)
        gathered.append(spread(block, right, left, chips))
    mine = (queries, grad_out, saved_out)
    late = lax.optimization_barrier((*mine, got))[:3]
    other = jnp.concatenate([part(array, 1 - core, HALF * WIDE) for array in late], axis=1)
    other = lax.ppermute(other, "leaf", swap)
    prepared = prepare(tables, mine, other, [blocks[0] for blocks in gathered])
    plan, qt, top, total = prepared[0], prepared[1], prepared[6], prepared[7]
    far = chips // 2
    for step in range(1, far):
        arrived = [blocks[at] for at in (step, chips - step - 1) for blocks in gathered]
        top, total = measure((step, chips - step), plan, qt, top, total, arrived)
    *terms, ours, theirs = gradients(prepared, top, total, gathered)
    theirs = lax.ppermute(theirs, "leaf", swap)
    kept, got = [], []
    for head in range(HALF):
        summed = collect(*terms[head::HALF], right, left)
        kept.append(summed[:rows])
        got.append(lax.ppermute(summed[rows:], "leaf", swap))

    def whole(kept, got):
        low = [jnp.where(core == 0, a, b) for a, b in zip(kept, got)]
        high = [jnp.where(core == 0, b, a) for a, b in zip(kept, got)]
        return jnp.concatenate(low + high, axis=1)

    key_grad = whole([a[:, :DH] for a in kept], [a[:, :DH] for a in got])
    value_grad = whole([a[:, DH:] for a in kept], [a[:, DH:] for a in got])
    return (whole([ours], [theirs]), key_grad, value_grad)


def solution(mesh):
    tokens = P(("groups", "leaf"), None)
    tables = P("groups")
    return jax.shard_map(
        local,
        mesh=mesh,
        in_specs=(tokens,) * 5 + (tables,) * 3,
        out_specs=(tokens,) * 3,
        check_vma=False,
    )
```

time: 140 us -> 144 us (1.029)
  waiting for transfers between devices: 48.9 us -> 36.4 us
  Pallas kernels: 37 us -> 47.2 us
  starting transfers between devices: 40.1 us -> 50.3 us
  local copies, waits for them, and re-layouts: 4.95 us -> 1.58 us
    ppermute x2, starting transfers between devices: 0.01 us -> 10.4 us  [collect(): down = lax.ppermute(down, 'leaf', left)]
    pallas_call x2 -> x5, Pallas kernels: 37 us -> 47.2 us  [the longest x1 34.4 us: gradients(): pl.pallas_call(functools.partial(grads_kernel, chips), in_specs=[SMEM] +...]
    ppermute x2, starting transfers between devices: 8.91 us -> 0.06 us  [collect(): up = lax.ppermute(up, 'leaf', right)]
    ppermute x6, starting transfers between devices: 5.47 us -> 13.1 us  [collect(): lax.ppermute((up + wide(terms[step])).astype(terms.dtype), 'leaf', right)]
    ppermute x6, waiting for transfers between devices: 8.74 us -> 4.04 us  [collect(): lax.ppermute((down + wide(terms[chips - step])).astype(terms.dtype), 'lea...]
    ppermute x6, waiting for transfers between devices: 8.13 us -> 5.72 us  [collect(): lax.ppermute((up + wide(terms[step])).astype(terms.dtype), 'leaf', right)]
    ppermute x6, starting transfers between devices: 6.08 us -> 8.32 us  [collect(): lax.ppermute((down + wide(terms[chips - step])).astype(terms.dtype), 'lea...]
    unnamed x46 -> x16, local copies, waits for them, and re-layouts: 2.29 us -> 0.1 us
  transfers between devices with their start and end apart: 37 -> 37, of which waited for: 21 -> 16; matrix products, arithmetic and copies ran while one was open for 5% -> 6% of each run, Pallas kernels for 26% -> 9%
where the time goes in v6:
time: 144 us; the launch traced here: 146 us
  starting transfers between devices  50.3 us (35%)
  Pallas kernels  47.2 us (33%)
  waiting for transfers between devices  36.4 us (25%)
  other arithmetic  9.66 us (7%)
  local copies, waits for them, and re-layouts  1.58 us (1%)
    pallas_call x1, Pallas kernels, gradients(): pl.pallas_call(functools.partial(grads_kernel, chips), in_specs=[SMEM] +...  34.4 us
    ppermute x6, waiting for transfers between devices, spread(): up = got[chips - step] = lax.ppermute(up, 'leaf', right)  22.5 us
    ppermute x6, starting transfers between devices, collect(): lax.ppermute((up + wide(terms[step])).astype(terms.dtype), 'leaf', right)  13.1 us
    ppermute x6, starting transfers between devices, spread(): up = got[chips - step] = lax.ppermute(up, 'leaf', right)  13 us
    ppermute x2, starting transfers between devices, collect(): down = lax.ppermute(down, 'leaf', left)  10.4 us
    ppermute x6, starting transfers between devices, collect(): lax.ppermute((down + wide(terms[chips - step])).astype(terms.dtype), 'lea...  8.32 us
    pallas_call x1, Pallas kernels, prepare(): pl.pallas_call(prepare_kernel, in_specs=[SMEM] * 5 + [HBM] * (4 + HALF),...  6.44 us
    pallas_call x3, Pallas kernels, measure(): pl.pallas_call(functools.partial(measure_kernel, offsets), in_specs=[SMEM...  6.3 us
  transfers between devices with their start and end apart: 37, of which 16 were waited for; matrix products, arithmetic and copies ran while one was open for 6% of the time, Pallas kernels for 9%

profile of v6, /device:TPU:0, one launch (start us, length us, event | category | flops | bytes accessed | tf_op | source)
XLA Modules:
  0.0 146.1 jit_solution(3654286430722088542)
XLA Ops:
  4.6 2.8 %collective-permute-start.4 = (bf16[512,256]{1,0:T(8,128)(2,1)S(1)}, bf16[512,256]{1,0:T(8,128)(2,1)S(1)}, u32[]{:S(2)}, u32[]{:S(2)}) collective-permute-start(bf16[512,256]{1,0:T(8,128)(2,1)S(1)} %pad_maximum_fusion.3.refs_0_), channel_id=1, source_target_pairs={{0,4},{1,5},{4,8},{5,9},{8,12},{9,13},{12,14},{13,15},{14,10},{15,... | collective-permute-start | bytes 786440 | tf_op jit(solution)/shard_map/ppermute | solution.py:353
  7.4 2.1 %collective-permute-start.5 = (bf16[512,256]{1,0:T(8,128)(2,1)S(1)}, bf16[512,256]{1,0:T(8,128)(2,1)S(1)}, u32[]{:S(2)}, u32[]{:S(2)}) collective-permute-start(bf16[512,256]{1,0:T(8,128)(2,1)S(1)} %pad_maximum_fusion.4.refs_1_.refs_9_), channel_id=1, source_target_pairs={{0,4},{1,5},{4,8},{5,9},{8,12},{9,13},{12,14},{13,15},{14,10},{15,... | collective-permute-start | bytes 786440 | tf_op jit(solution)/shard_map/ppermute | solution.py:353
  9.5 5.0 %collective-permute-done.4.refs_2_.refs_6_ = bf16[512,256]{1,0:T(8,128)(2,1)S(1)} collective-permute-done((bf16[512,256]{1,0:T(8,128)(2,1)S(1)}, bf16[512,256]{1,0:T(8,128)(2,1)S(1)}, u32[]{:S(2)}, u32[]{:S(2)}) %collective-permute-start.4) | collective-permute-done | bytes 262176 | tf_op jit(solution)/shard_map/ppermute | solution.py:353
  14.4 2.0 %collective-permute-start.8 = (bf16[512,256]{1,0:T(8,128)(2,1)S(1)}, bf16[512,256]{1,0:T(8,128)(2,1)S(1)}, u32[]{:S(2)}, u32[]{:S(2)}) collective-permute-start(bf16[512,256]{1,0:T(8,128)(2,1)S(1)} %collective-permute-done.4.refs_2_.refs_6_), channel_id=1, source_target_pairs={{0,4},{1,5},{4,8},{5,9},{8,12},{9,13},{12,14},{13,15},{14,10},{15,... | collective-permute-start | bytes 786440 | tf_op jit(solution)/shard_map/ppermute | solution.py:353
  16.5 3.5 %collective-permute-done.5.refs_3_.refs_15_ = bf16[512,256]{1,0:T(8,128)(2,1)S(1)} collective-permute-done((bf16[512,256]{1,0:T(8,128)(2,1)S(1)}, bf16[512,256]{1,0:T(8,128)(2,1)S(1)}, u32[]{:S(2)}, u32[]{:S(2)}) %collective-permute-start.5) | collective-permute-done | bytes 262176 | tf_op jit(solution)/shard_map/ppermute | solution.py:353
  22.1 3.5 %collective-permute-done.8.refs_2_.refs_5_ = bf16[512,256]{1,0:T(8,128)(2,1)S(1)} collective-permute-done((bf16[512,256]{1,0:T(8,128)(2,1)S(1)}, bf16[512,256]{1,0:T(8,128)(2,1)S(1)}, u32[]{:S(2)}, u32[]{:S(2)}) %collective-permute-start.8) | collective-permute-done | bytes 262176 | tf_op jit(solution)/shard_map/ppermute | solution.py:353
  27.7 3.5 %collective-permute-done.9.refs_3_.refs_14_ = bf16[512,256]{1,0:T(8,128)(2,1)S(1)} collective-permute-done((bf16[512,256]{1,0:T(8,128)(2,1)S(1)}, bf16[512,256]{1,0:T(8,128)(2,1)S(1)}, u32[]{:S(2)}, u32[]{:S(2)}) %collective-permute-start.9) | collective-permute-done | bytes 262176 | tf_op jit(solution)/shard_map/ppermute | solution.py:353
  33.4 3.5 %collective-permute-done.12.refs_2_.refs_4_ = bf16[512,256]{1,0:T(8,128)(2,1)S(1)} collective-permute-done((bf16[512,256]{1,0:T(8,128)(2,1)S(1)}, bf16[512,256]{1,0:T(8,128)(2,1)S(1)}, u32[]{:S(2)}, u32[]{:S(2)}) %collective-permute-start.12) | collective-permute-done | bytes 262176 | tf_op jit(solution)/shard_map/ppermute | solution.py:353
  36.9 2.1 %collective-permute-start.14 = (bf16[256,256]{1,0:T(8,128)(2,1)S(1)}, bf16[256,256]{1,0:T(8,128)(2,1)S(1)}, u32[]{:S(2)}, u32[]{:S(2)}) collective-permute-start(bf16[256,256]{1,0:T(8,128)(2,1)S(1)} %slice.132), channel_id=1, source_target_pairs={{0,4},{1,5},{4,8},{5,9},{8,12},{9,13},{12,14},{13,15},{14,10},{15,... | collective-permute-start | bytes 393224 | tf_op jit(solution)/shard_map/ppermute | solution.py:355
  39.1 3.4 %collective-permute-done.13.refs_3_.refs_13_ = bf16[512,256]{1,0:T(8,128)(2,1)S(1)} collective-permute-done((bf16[512,256]{1,0:T(8,128)(2,1)S(1)}, bf16[512,256]{1,0:T(8,128)(2,1)S(1)}, u32[]{:S(2)}, u32[]{:S(2)}) %collective-permute-start.13) | collective-permute-done | bytes 262176 | tf_op jit(solution)/shard_map/ppermute | solution.py:353
  42.5 2.1 %collective-permute-start.16 = (bf16[256,256]{1,0:T(8,128)(2,1)S(1)}, bf16[256,256]{1,0:T(8,128)(2,1)S(1)}, u32[]{:S(2)}, u32[]{:S(2)}) collective-permute-start(bf16[256,256]{1,0:T(8,128)(2,1)S(1)} %slice.134), channel_id=1, source_target_pairs={{0,4},{1,5},{4,8},{5,9},{8,12},{9,13},{12,14},{13,15},{14,10},{15,... | collective-permute-start | bytes 393224 | tf_op jit(solution)/shard_map/ppermute | solution.py:355
  44.8 6.4 %shard_map.112 = (s32[32]{0:T(128)S(1)}, bf16[2,2,128,1280]{3,2,1,0:T(8,128)(2,1)S(1)}, bf16[2,2,128,1280]{3,2,1,0:T(8,128)(2,1)S(1)}, bf16[2,2,1280,128]{3,2,1,...) custom-call(s32[1]{0:T(128)} %bitcast.me_ref, ...), custom_call_target="tpu_custom_call" | custom-call | bytes 25165824 | tf_op jit(solution)/shard_map/pallas_call | solution.py:168
  52.2 3.2 %shard_map.114 = (f32[2,2,1,1280]{3,2,1,0:T(1,128)S(1)}, f32[2,2,1,1280]{3,2,1,0:T(1,128)S(1)}) custom-call(s32[32]{0:T(128)S(1)} %get-tuple-element.31.plan, bf16[2,2,128,1280]{3,2,1,0:T(8,128)(2,1)S(1)} %get-tuple-element.32.qt_in, f32[2,2,1,1280]{3,2,1,0:T(1,128)S(1)} %get-tuple-element.39.top_in, f32[2,2,1,1280]{3,2,1,0:T(1,128)S(1)} %get-tuple-element.40.sum_in, ...), custom_call_target="tpu_custom_call" | custom-call | bytes 12582912 | tf_op jit(solution)/shard_map/pallas_call | solution.py:202
  55.4 2.1 %shard_map.115 = (f32[2,2,1,1280]{3,2,1,0:T(1,128)S(1)}, f32[2,2,1,1280]{3,2,1,0:T(1,128)S(1)}) custom-call(s32[32]{0:T(128)S(1)} %get-tuple-element.31.plan, bf16[2,2,128,1280]{3,2,1,0:T(8,128)(2,1)S(1)} %get-tuple-element.32.qt_in, f32[2,2,1,1280]{3,2,1,0:T(1,128)S(1)} %get-tuple-element.41.top_in, f32[2,2,1,1280]{3,2,1,0:T(1,128)S(1)} %get-tuple-element.42.sum_in, ...), custom_call_target="tpu_custom_call" | custom-call | bytes 12582912 | tf_op jit(solution)/shard_map/pallas_call | solution.py:202
  57.6 34.4 %shard_map.116 = (bf16[8,512,256]{2,1,0:T(8,128)(2,1)S(1)}, bf16[8,512,256]{2,1,0:T(8,128)(2,1)S(1)}, bf16[256,256]{1,0:T(8,128)(2,1)S(1)}, bf16[256,256]{1,0:T(...) custom-call(s32[32]{0:T(128)S(1)} %get-tuple-element.31.plan, ...), custom_call_target="tpu_custom_call" | custom-call | flops 21474836480 | bytes 16777216 | tf_op jit(solution)/shard_map/pallas_call | solution.py:328
  92.1 8.3 %collective-permute-start.23 = (bf16[256,256]{1,0:T(8,128)(2,1)S(1)}, bf16[256,256]{1,0:T(8,128)(2,1)S(1)}, u32[]{:S(2)}, u32[]{:S(2)}) collective-permute-start(bf16[256,256]{1,0:T(8,128)(2,1)S(1)} %get-tuple-element.49), channel_id=1, source_target_pairs={{4,0},{5,1},{8,4},{9,5},{12,8},{13,9},{14,12},{15,13},{10,14},{11,... | collective-permute-start | bytes 393224 | tf_op jit(solution)/shard_map/ppermute | solution.py:367
  104.1 2.9 %collective-permute-start.24 = (bf16[512,256]{1,0:T(8,128)(2,1)S(1)}, bf16[512,256]{1,0:T(8,128)(2,1)S(1)}, u32[]{:S(2)}, u32[]{:S(2)}) collective-permute-start(bf16[512,256]{1,0:T(8,128)(2,1)S(1)} %get-tuple-element.58), channel_id=1, source_target_pairs={{4,0},{5,1},{8,4},{9,5},{12,8},{13,9},{14,12},{15,13},{10,14},{11,... | collective-permute-start | bytes 786440 | tf_op jit(solution)/shard_map/ppermute | solution.py:372
  107.1 4.0 %collective-permute-start.33 = (bf16[512,256]{1,0:T(8,128)(2,1)S(1)}, bf16[512,256]{1,0:T(8,128)(2,1)S(1)}, u32[]{:S(2)}, u32[]{:S(2)}) collective-permute-start(bf16[512,256]{1,0:T(8,128)(2,1)S(1)} %get-tuple-element.64), channel_id=1, source_target_pairs={{4,0},{5,1},{8,4},{9,5},{12,8},{13,9},{14,12},{15,13},{10,14},{11,... | collective-permute-start | bytes 786440 | tf_op jit(solution)/shard_map/ppermute | solution.py:372
  111.1 2.9 %collective-permute-done.20 = bf16[512,256]{1,0:T(8,128)(2,1)S(1)} collective-permute-done((bf16[512,256]{1,0:T(8,128)(2,1)S(1)}, bf16[512,256]{1,0:T(8,128)(2,1)S(1)}, u32[]{:S(2)}, u32[]{:S(2)}) %collective-permute-start.20) | collective-permute-done | bytes 262176 | tf_op jit(solution)/shard_map/ppermute | solution.py:371
  114.9 4.0 %collective-permute-start.21 = (bf16[512,256]{1,0:T(8,128)(2,1)}, bf16[512,256]{1,0:T(8,128)(2,1)}, u32[]{:S(2)}, u32[]{:S(2)}) collective-permute-start(bf16[512,256]{1,0:T(8,128)(2,1)} %get-tuple-element.55), channel_id=1, source_target_pairs={{0,4},{1,5},{4,8},{5,9},{8,12},{9,13},{12,14},{13,15},{14,10},{15,... | collective-permute-start | bytes 786440 | tf_op jit(solution)/shard_map/ppermute | solution.py:371
  119.9 3.2 %collective-permute-start.30 = (bf16[512,256]{1,0:T(8,128)(2,1)}, bf16[512,256]{1,0:T(8,128)(2,1)}, u32[]{:S(2)}, u32[]{:S(2)}) collective-permute-start(bf16[512,256]{1,0:T(8,128)(2,1)} %get-tuple-element.61), channel_id=1, source_target_pairs={{0,4},{1,5},{4,8},{5,9},{8,12},{9,13},{12,14},{13,15},{14,10},{15,... | collective-permute-start | bytes 786440 | tf_op jit(solution)/shard_map/ppermute | solution.py:371
  127.6 3.1 %collective-permute-start.22 = (bf16[512,256]{1,0:T(8,128)(2,1)S(1)}, bf16[512,256]{1,0:T(8,128)(2,1)S(1)}, u32[]{:S(2)}, u32[]{:S(2)}) collective-permute-start(bf16[512,256]{1,0:T(8,128)(2,1)S(1)} %get-tuple-element.53), channel_id=1, source_target_pairs={{0,4},{1,5},{4,8},{5,9},{8,12},{9,13},{12,14},{13,15},{14,10},{15,... | collective-permute-start | bytes 786440 | tf_op jit(solution)/shard_map/ppermute | solution.py:371
  132.9 2.6 %collective-permute-start.31 = (bf16[512,256]{1,0:T(8,128)(2,1)S(1)}, bf16[512,256]{1,0:T(8,128)(2,1)S(1)}, u32[]{:S(2)}, u32[]{:S(2)}) collective-permute-start(bf16[512,256]{1,0:T(8,128)(2,1)S(1)} %get-tuple-element.59), channel_id=1, source_target_pairs={{0,4},{1,5},{4,8},{5,9},{8,12},{9,13},{12,14},{13,15},{14,10},{15,... | collective-permute-start | bytes 786440 | tf_op jit(solution)/shard_map/ppermute | solution.py:371
  140.3 2.8 %collective-permute-done.35 = bf16[512,256]{1,0:T(8,128)(2,1)S(1)} collective-permute-done((bf16[512,256]{1,0:T(8,128)(2,1)S(1)}, bf16[512,256]{1,0:T(8,128)(2,1)S(1)}, u32[]{:S(2)}, u32[]{:S(2)}) %collective-permute-start.35) | collective-permute-done | bytes 262176 | tf_op jit(solution)/shard_map/ppermute | solution.py:372
  (100 shorter events, 31.4 us)
Async XLA Ops:
  4.1 40.6 %collective-permute-start.1 = (bf16[256,3840]{1,0:T(8,128)(2,1)S(1)}, bf16[256,3840]{1,0:T(8,128)(2,1)S(1)}, u32[]{:S(2)}, u32[]{:S(2)}) collective-permute-start(bf16[256,3840]{1,0:T(8,128)(2,1)S(1)} %pad_maximum_fusion), channel_id=1, source_target_pairs={{0,1},{1,0},{2,3},{3,2},{4,5},{5,4},{6,7},{7,6},{8,9},{9,8},{10,11... | collective-permute-start | bytes 5898248 | tf_op jit(solution)/shard_map/ppermute | solution.py:407
  7.4 12.7 %collective-permute-start.5 = (bf16[512,256]{1,0:T(8,128)(2,1)S(1)}, bf16[512,256]{1,0:T(8,128)(2,1)S(1)}, u32[]{:S(2)}, u32[]{:S(2)}) collective-permute-start(bf16[512,256]{1,0:T(8,128)(2,1)S(1)} %pad_maximum_fusion.4.refs_1_.refs_9_), channel_id=1, source_target_pairs={{0,4},{1,5},{4,8},{5,9},{8,12},{9,13},{12,14},{13,15},{14,10},{15,... | collective-permute-start | bytes 786440 | tf_op jit(solution)/shard_map/ppermute | solution.py:353
  9.4 12.7 %collective-permute-start.3 = (bf16[512,256]{1,0:T(8,128)(2,1)S(1)}, bf16[512,256]{1,0:T(8,128)(2,1)S(1)}, u32[]{:S(2)}, u32[]{:S(2)}) collective-permute-start(bf16[512,256]{1,0:T(8,128)(2,1)S(1)} %pad_maximum_fusion.4.refs_1_.refs_9_), channel_id=1, source_target_pairs={{4,0},{5,1},{8,4},{9,5},{12,8},{13,9},{14,12},{15,13},{10,14},{11,... | collective-permute-start | bytes 786440 | tf_op jit(solution)/shard_map/ppermute | solution.py:354
  14.4 11.2 %collective-permute-start.8 = (bf16[512,256]{1,0:T(8,128)(2,1)S(1)}, bf16[512,256]{1,0:T(8,128)(2,1)S(1)}, u32[]{:S(2)}, u32[]{:S(2)}) collective-permute-start(bf16[512,256]{1,0:T(8,128)(2,1)S(1)} %collective-permute-done.4.refs_2_.refs_6_), channel_id=1, source_target_pairs={{0,4},{1,5},{4,8},{5,9},{8,12},{9,13},{12,14},{13,15},{14,10},{15,... | collective-permute-start | bytes 786440 | tf_op jit(solution)/shard_map/ppermute | solution.py:353
  16.5 11.2 %collective-permute-start.6 = (bf16[512,256]{1,0:T(8,128)(2,1)S(1)}, bf16[512,256]{1,0:T(8,128)(2,1)S(1)}, u32[]{:S(2)}, u32[]{:S(2)}) collective-permute-start(bf16[512,256]{1,0:T(8,128)(2,1)S(1)} %collective-permute-done.2.refs_0_.refs_1_), channel_id=1, source_target_pairs={{4,0},{5,1},{8,4},{9,5},{12,8},{13,9},{14,12},{15,13},{10,14},{11,... | collective-permute-start | bytes 786440 | tf_op jit(solution)/shard_map/ppermute | solution.py:354
  20.0 11.2 %collective-permute-start.9 = (bf16[512,256]{1,0:T(8,128)(2,1)S(1)}, bf16[512,256]{1,0:T(8,128)(2,1)S(1)}, u32[]{:S(2)}, u32[]{:S(2)}) collective-permute-start(bf16[512,256]{1,0:T(8,128)(2,1)S(1)} %collective-permute-done.5.refs_3_.refs_15_), channel_id=1, source_target_pairs={{0,4},{1,5},{4,8},{5,9},{8,12},{9,13},{12,14},{13,15},{14,10},{15,... | collective-permute-start | bytes 786440 | tf_op jit(solution)/shard_map/ppermute | solution.py:353
  22.1 11.2 %collective-permute-start.7 = (bf16[512,256]{1,0:T(8,128)(2,1)S(1)}, bf16[512,256]{1,0:T(8,128)(2,1)S(1)}, u32[]{:S(2)}, u32[]{:S(2)}) collective-permute-start(bf16[512,256]{1,0:T(8,128)(2,1)S(1)} %collective-permute-done.3.refs_1_.refs_10_), channel_id=1, source_target_pairs={{4,0},{5,1},{8,4},{9,5},{12,8},{13,9},{14,12},{15,13},{10,14},{11,... | collective-permute-start | bytes 786440 | tf_op jit(solution)/shard_map/ppermute | solution.py:354
  25.7 11.2 %collective-permute-start.12 = (bf16[512,256]{1,0:T(8,128)(2,1)S(1)}, bf16[512,256]{1,0:T(8,128)(2,1)S(1)}, u32[]{:S(2)}, u32[]{:S(2)}) collective-permute-start(bf16[512,256]{1,0:T(8,128)(2,1)S(1)} %collective-permute-done.8.refs_2_.refs_5_), channel_id=1, source_target_pairs={{0,4},{1,5},{4,8},{5,9},{8,12},{9,13},{12,14},{13,15},{14,10},{15,... | collective-permute-start | bytes 786440 | tf_op jit(solution)/shard_map/ppermute | solution.py:353
  27.7 11.3 %collective-permute-start.10 = (bf16[512,256]{1,0:T(8,128)(2,1)S(1)}, bf16[512,256]{1,0:T(8,128)(2,1)S(1)}, u32[]{:S(2)}, u32[]{:S(2)}) collective-permute-start(bf16[512,256]{1,0:T(8,128)(2,1)S(1)} %collective-permute-done.6.refs_0_.refs_2_), channel_id=1, source_target_pairs={{4,0},{5,1},{8,4},{9,5},{12,8},{13,9},{14,12},{15,13},{10,14},{11,... | collective-permute-start | bytes 786440 | tf_op jit(solution)/shard_map/ppermute | solution.py:354
  31.3 11.2 %collective-permute-start.13 = (bf16[512,256]{1,0:T(8,128)(2,1)S(1)}, bf16[512,256]{1,0:T(8,128)(2,1)S(1)}, u32[]{:S(2)}, u32[]{:S(2)}) collective-permute-start(bf16[512,256]{1,0:T(8,128)(2,1)S(1)} %collective-permute-done.9.refs_3_.refs_14_), channel_id=1, source_target_pairs={{0,4},{1,5},{4,8},{5,9},{8,12},{9,13},{12,14},{13,15},{14,10},{15,... | collective-permute-start | bytes 786440 | tf_op jit(solution)/shard_map/ppermute | solution.py:353
  33.4 11.3 %collective-permute-start.11 = (bf16[512,256]{1,0:T(8,128)(2,1)S(1)}, bf16[512,256]{1,0:T(8,128)(2,1)S(1)}, u32[]{:S(2)}, u32[]{:S(2)}) collective-permute-start(bf16[512,256]{1,0:T(8,128)(2,1)S(1)} %collective-permute-done.7.refs_1_.refs_11_), channel_id=1, source_target_pairs={{4,0},{5,1},{8,4},{9,5},{12,8},{13,9},{14,12},{15,13},{10,14},{11,... | collective-permute-start | bytes 786440 | tf_op jit(solution)/shard_map/ppermute | solution.py:354
  36.9 20.6 %collective-permute-start.14 = (bf16[256,256]{1,0:T(8,128)(2,1)S(1)}, bf16[256,256]{1,0:T(8,128)(2,1)S(1)}, u32[]{:S(2)}, u32[]{:S(2)}) collective-permute-start(bf16[256,256]{1,0:T(8,128)(2,1)S(1)} %slice.132), channel_id=1, source_target_pairs={{0,4},{1,5},{4,8},{5,9},{8,12},{9,13},{12,14},{13,15},{14,10},{15,... | collective-permute-start | bytes 393224 | tf_op jit(solution)/shard_map/ppermute | solution.py:355
  39.0 18.5 %collective-permute-start.15 = (bf16[256,256]{1,0:T(8,128)(2,1)S(1)}, bf16[256,256]{1,0:T(8,128)(2,1)S(1)}, u32[]{:S(2)}, u32[]{:S(2)}) collective-permute-start(bf16[256,256]{1,0:T(8,128)(2,1)S(1)} %slice.133), channel_id=1, source_target_pairs={{4,0},{5,1},{8,4},{9,5},{12,8},{13,9},{14,12},{15,13},{10,14},{11,... | collective-permute-start | bytes 393224 | tf_op jit(solution)/shard_map/ppermute | solution.py:356
  42.5 15.0 %collective-permute-start.16 = (bf16[256,256]{1,0:T(8,128)(2,1)S(1)}, bf16[256,256]{1,0:T(8,128)(2,1)S(1)}, u32[]{:S(2)}, u32[]{:S(2)}) collective-permute-start(bf16[256,256]{1,0:T(8,128)(2,1)S(1)} %slice.134), channel_id=1, source_target_pairs={{0,4},{1,5},{4,8},{5,9},{8,12},{9,13},{12,14},{13,15},{14,10},{15,... | collective-permute-start | bytes 393224 | tf_op jit(solution)/shard_map/ppermute | solution.py:355
  44.6 12.9 %collective-permute-start.17 = (bf16[256,256]{1,0:T(8,128)(2,1)S(1)}, bf16[256,256]{1,0:T(8,128)(2,1)S(1)}, u32[]{:S(2)}, u32[]{:S(2)}) collective-permute-start(bf16[256,256]{1,0:T(8,128)(2,1)S(1)} %slice.135), channel_id=1, source_target_pairs={{4,0},{5,1},{8,4},{9,5},{12,8},{13,9},{14,12},{15,13},{10,14},{11,... | collective-permute-start | bytes 393224 | tf_op jit(solution)/shard_map/ppermute | solution.py:356
  92.0 11.9 %collective-permute-start.19 = (bf16[256,256]{1,0:T(8,128)(2,1)S(1)}, bf16[256,256]{1,0:T(8,128)(2,1)S(1)}, u32[]{:S(2)}, u32[]{:S(2)}) collective-permute-start(bf16[256,256]{1,0:T(8,128)(2,1)S(1)} %get-tuple-element.48), channel_id=1, source_target_pairs={{0,4},{1,5},{4,8},{5,9},{8,12},{9,13},{12,14},{13,15},{14,10},{15,... | collective-permute-start | bytes 393224 | tf_op jit(solution)/shard_map/ppermute | solution.py:366
  92.1 11.9 %collective-permute-start.23 = (bf16[256,256]{1,0:T(8,128)(2,1)S(1)}, bf16[256,256]{1,0:T(8,128)(2,1)S(1)}, u32[]{:S(2)}, u32[]{:S(2)}) collective-permute-start(bf16[256,256]{1,0:T(8,128)(2,1)S(1)} %get-tuple-element.49), channel_id=1, source_target_pairs={{4,0},{5,1},{8,4},{9,5},{12,8},{13,9},{14,12},{15,13},{10,14},{11,... | collective-permute-start | bytes 393224 | tf_op jit(solution)/shard_map/ppermute | solution.py:367
  104.0 10.0 %collective-permute-start.20 = (bf16[512,256]{1,0:T(8,128)(2,1)S(1)}, bf16[512,256]{1,0:T(8,128)(2,1)S(1)}, u32[]{:S(2)}, u32[]{:S(2)}) collective-permute-start(bf16[512,256]{1,0:T(8,128)(2,1)S(1)} %get-tuple-element.57), channel_id=1, source_target_pairs={{0,4},{1,5},{4,8},{5,9},{8,12},{9,13},{12,14},{13,15},{14,10},{15,... | collective-permute-start | bytes 786440 | tf_op jit(solution)/shard_map/ppermute | solution.py:371
  107.0 12.0 %collective-permute-start.29 = (bf16[512,256]{1,0:T(8,128)(2,1)S(1)}, bf16[512,256]{1,0:T(8,128)(2,1)S(1)}, u32[]{:S(2)}, u32[]{:S(2)}) collective-permute-start(bf16[512,256]{1,0:T(8,128)(2,1)S(1)} %get-tuple-element.63), channel_id=1, source_target_pairs={{0,4},{1,5},{4,8},{5,9},{8,12},{9,13},{12,14},{13,15},{14,10},{15,... | collective-permute-start | bytes 786440 | tf_op jit(solution)/shard_map/ppermute | solution.py:371
  107.1 11.9 %collective-permute-start.33 = (bf16[512,256]{1,0:T(8,128)(2,1)S(1)}, bf16[512,256]{1,0:T(8,128)(2,1)S(1)}, u32[]{:S(2)}, u32[]{:S(2)}) collective-permute-start(bf16[512,256]{1,0:T(8,128)(2,1)S(1)} %get-tuple-element.64), channel_id=1, source_target_pairs={{4,0},{5,1},{8,4},{9,5},{12,8},{13,9},{14,12},{15,13},{10,14},{11,... | collective-permute-start | bytes 786440 | tf_op jit(solution)/shard_map/ppermute | solution.py:372
  111.1 24.8 %collective-permute-start.18 = (bf16[256,1280]{1,0:T(8,128)(2,1)S(1)}, bf16[256,1280]{1,0:T(8,128)(2,1)}, u32[]{:S(2)}, u32[]{:S(2)}) collective-permute-start(bf16[256,1280]{1,0:T(8,128)(2,1)S(1)} %get-tuple-element.46), channel_id=1, source_target_pairs={{0,1},{1,0},{2,3},{3,2},{4,5},{5,4},{6,7},{7,6},{8,9},{9,8},{10,11... | collective-permute-start | bytes 1966088 | tf_op jit(solution)/shard_map/ppermute | solution.py:415
  114.9 10.8 %collective-permute-start.21 = (bf16[512,256]{1,0:T(8,128)(2,1)}, bf16[512,256]{1,0:T(8,128)(2,1)}, u32[]{:S(2)}, u32[]{:S(2)}) collective-permute-start(bf16[512,256]{1,0:T(8,128)(2,1)} %get-tuple-element.55), channel_id=1, source_target_pairs={{0,4},{1,5},{4,8},{5,9},{8,12},{9,13},{12,14},{13,15},{14,10},{15,... | collective-permute-start | bytes 786440 | tf_op jit(solution)/shard_map/ppermute | solution.py:371
  119.9 11.2 %collective-permute-start.30 = (bf16[512,256]{1,0:T(8,128)(2,1)}, bf16[512,256]{1,0:T(8,128)(2,1)}, u32[]{:S(2)}, u32[]{:S(2)}) collective-permute-start(bf16[512,256]{1,0:T(8,128)(2,1)} %get-tuple-element.61), channel_id=1, source_target_pairs={{0,4},{1,5},{4,8},{5,9},{8,12},{9,13},{12,14},{13,15},{14,10},{15,... | collective-permute-start | bytes 786440 | tf_op jit(solution)/shard_map/ppermute | solution.py:371
  127.6 10.6 %collective-permute-start.22 = (bf16[512,256]{1,0:T(8,128)(2,1)S(1)}, bf16[512,256]{1,0:T(8,128)(2,1)S(1)}, u32[]{:S(2)}, u32[]{:S(2)}) collective-permute-start(bf16[512,256]{1,0:T(8,128)(2,1)S(1)} %get-tuple-element.53), channel_id=1, source_target_pairs={{0,4},{1,5},{4,8},{5,9},{8,12},{9,13},{12,14},{13,15},{14,10},{15,... | collective-permute-start | bytes 786440 | tf_op jit(solution)/shard_map/ppermute | solution.py:371
  (21 other events, 280.7 us)

commit v7 on v6

--- a/solution.py
+++ b/solution.py
@@ -214,57 +214,91 @@
     )(plan, qt, top, total, *blocks)
 
 
-def grads_kernel(chips, plan, qt_in, gt_in, gm_in, qm_in, delta_in, top_in, sum_in, *refs):
-    count = HALF * (chips + 1)
+def grads_kernel(chips, offsets, first, last, plan, *refs):
+    far = chips // 2
+    count = HALF * (len(offsets) + first)
+    shared, refs = refs[:6 + first], refs[6 + first:]
     blocks, refs = refs[:count], refs[count:]
-    terms, ups, downs = refs[:HALF], refs[HALF:2 * HALF], refs[2 * HALF:3 * HALF]
-    (dq_mine, dq_other, qt_ref, gt_ref, gm_ref, qm_ref, delta_ref, top_ref, sum_ref, kv_ref,
-     acc_ref, stage_ref, dqt_ref, sems, kv_sems, out_sems) = refs[3 * HALF:]
-    rows = dq_mine.shape[0]
-    far = chips // 2
+    carried = None
+    if not first:
+        carried, refs = refs[0], refs[1:]
+    terms, refs = refs[:HALF], refs[HALF:]
+    if first:
+        ups, downs, refs = refs[:HALF], refs[HALF:2 * HALF], refs[2 * HALF:]
+        lse_out, refs = refs[0], refs[1:]
+    outs, refs = refs[:2 if last else 1], refs[2 if last else 1:]
+    held, refs = refs[:6 + first], refs[6 + first:]
+    qt_ref, gt_ref, gm_ref, qm_ref, delta_ref, lse_ref = held[:6]
+    kv_ref, acc_ref, stage_ref, zero_ref, dqt_ref, offset_ref, sems, kv_sems, out_sems = refs
+    rows = acc_ref.shape[1]
+
     pairs = []
-    for head in range(HALF):
-        pairs.append((blocks[head * (chips + 1) + chips - 1], kv_ref.at[far, head, :rows]))
-        pairs.append((blocks[head * (chips + 1) + chips], kv_ref.at[far, head, rows:]))
-    shared = zip((qt_in, gt_in, gm_in, qm_in, delta_in, top_in, sum_in),
-                 (qt_ref, gt_ref, gm_ref, qm_ref, delta_ref, top_ref, sum_ref))
-    copies = run_copies(pairs + list(shared), sems)
-    rest = [at for at in range(chips) if at != far]
-    for slot, at in enumerate(rest):
+    for slot, offset in enumerate(offsets):
+        offset_ref[slot] = offset
         for head in range(HALF):
-            pltpu.make_async_copy(
-                blocks[head * (chips + 1) + slot], kv_ref.at[at, head], kv_sems.at[at, head]
-            ).start()
-    dqt_ref[...] = jnp.zeros_like(dqt_ref)
+            at = head * (len(offsets) + first)
+            if offset == far:
+                pairs.append((blocks[at], kv_ref.at[slot, head, :rows]))
+                pairs.append((blocks[at + 1], kv_ref.at[slot, head, rows:]))
+            else:
+                pltpu.make_async_copy(
+                    blocks[at + slot + first], kv_ref.at[slot, head], kv_sems.at[slot, head]
+                ).start()
+    pairs += list(zip(shared, held))
+    if carried is not None:
+        pairs.append((carried, dqt_ref))
+    copies = run_copies(pairs, sems)
+    zero_ref[...] = jnp.zeros_like(zero_ref)
+    if first:
+        dqt_ref[...] = jnp.zeros_like(dqt_ref)
     for copy in copies:
         copy.wait()
-    measure_blocks(plan, [far], kv_ref.at[pl.ds(far, 1)], qt_ref, top_ref, sum_ref)
-    top_ref[...] = top_ref[...] * EXP_SCALE + jnp.log2(sum_ref[...])
-
-    def out_copy(slot, head, target):
-        return pltpu.make_async_copy(stage_ref.at[slot, head], target, out_sems.at[slot, head])
+    if first:
+        sum_ref = held[6]
+        measure_blocks(plan, [far], kv_ref, qt_ref, lse_ref, sum_ref)
+        lse_ref[...] = lse_ref[...] * EXP_SCALE + jnp.log2(sum_ref[...])
+        lse_out[...] = lse_ref[...]
+
+    def out_copy(source, slot, head, target):
+        return pltpu.make_async_copy(source, target, out_sems.at[slot, head])
 
     def visit(i, carry):
-        step = i // 2
+        at_block = i // 2
         half = i % 2
-        offset = jnp.where(step % 2 == 1, far + (step + 1) // 2, far - step // 2)
-        offset = jnp.where(offset >= chips, offset - chips, offset)
+        offset = offset_ref[at_block]
         slot = i % 2
         here = pl.ds(pl.multiple_of(half * rows, rows), rows)
+        seen_by = [plan[side * 2 * chips + offset * 2 + half] for side in range(2)]
+        any_seen = (seen_by[0] > 0) | (seen_by[1] > 0)
 
         @pl.when((half == 0) & (offset != far))
         def _():
             for head in range(HALF):
                 pltpu.make_async_copy(
-                    blocks[0], kv_ref.at[offset, head], kv_sems.at[offset, head]
+                    blocks[-1], kv_ref.at[at_block, head], kv_sems.at[at_block, head]
                 ).wait()
 
         @pl.when(i >= 2)
         def _():
             for head in range(HALF):
-                out_copy(slot, head, ups[0]).wait()
-
-        acc_ref[...] = jnp.zeros_like(acc_ref)
+                out_copy(zero_ref, slot, head, terms[0].at[0, :rows]).wait()
+
+        def send(sources):
+            for head in range(HALF):
+                if first:
+                    @pl.when(offset != far)
+                    def _():
+                        out_copy(sources[head], slot, head, terms[head].at[at_block, here]).start()
+
+                    @pl.when((offset == far) & (half == 0))
+                    def _():
+                        out_copy(sources[head], slot, head, ups[head]).start()
+
+                    @pl.when((offset == far) & (half == 1))
+                    def _():
+                        out_copy(sources[head], slot, head, downs[head]).start()
+                else:
+                    out_copy(sources[head], slot, head, terms[head].at[at_block, here]).start()
 
         def look(side, carry):
             sees = plan[side * 2 * chips + offset * 2 + half]
@@ -273,10 +307,10 @@
             def _():
                 for head in range(HALF):
                     at = (head, side)
-                    k = kv_ref[offset, head, here, :DH]
-                    v = kv_ref[offset, head, here, DH:]
+                    k = kv_ref[at_block, head, here, :DH]
+                    v = kv_ref[at_block, head, here, DH:]
                     s, seen = masked_scores(k, qt_ref[at], sees)
-                    p = jnp.where(seen, jnp.exp2(s * EXP_SCALE - top_ref[at]), 0.0)
+                    p = jnp.where(seen, jnp.exp2(s * EXP_SCALE - lse_ref[at]), 0.0)
                     ds = (p * (dot(v, gt_ref[at]) - delta_ref[at])).astype(jnp.bfloat16)
                     acc_ref[head, :, DH:] += dot(p.astype(jnp.bfloat16), gm_ref[at])
                     acc_ref[head, :, :DH] += dot(ds, qm_ref[at])
@@ -284,93 +318,79 @@
 
             return carry
 
-        lax.fori_loop(0, 2, look, 0)
-        for head in range(HALF):
-            stage_ref[slot, head, :, :DH] = (acc_ref[head, :, :DH] * SCALE).astype(stage_ref.dtype)
-            stage_ref[slot, head, :, DH:] = acc_ref[head, :, DH:].astype(stage_ref.dtype)
-
-        for head in range(HALF):
-            @pl.when(offset != far)
-            def _():
-                out_copy(slot, head, terms[head].at[offset, here]).start()
-
-            @pl.when((offset == far) & (half == 0))
-            def _():
-                out_copy(slot, head, ups[head]).start()
-
-            @pl.when((offset == far) & (half == 1))
-            def _():
-                out_copy(slot, head, downs[head]).start()
+        @pl.when(any_seen)
+        def _():
+            acc_ref[...] = jnp.zeros_like(acc_ref)
+            lax.fori_loop(0, 2, look, 0)
+            for head in range(HALF):
+                stage_ref[slot, head, :, :DH] = (acc_ref[head, :, :DH] * SCALE).astype(stage_ref.dtype)
+                stage_ref[slot, head, :, DH:] = acc_ref[head, :, DH:].astype(stage_ref.dtype)
+            send([stage_ref.at[slot, head] for head in range(HALF)])
+
+        @pl.when(jnp.logical_not(any_seen))
+        def _():
+            send([zero_ref] * HALF)
 
         return carry
 
-    lax.fori_loop(0, 2 * chips, visit, 0)
-    for side, dq_ref in enumerate((dq_mine, dq_other)):
-        for head in range(HALF):
-            for h in range(PER):
-                dq = dqt_ref[head, side, :, h * rows:(h + 1) * rows].T * SCALE
-                dq_ref[:, (head * PER + h) * DH:(head * PER + h + 1) * DH] = dq.astype(dq_ref.dtype)
+    lax.fori_loop(0, 2 * len(offsets), visit, 0)
+    if last:
+        for side, dq_ref in enumerate(outs):
+            for head in range(HALF):
+                for h in range(PER):
+                    dq = (dqt_ref[head, side, :, h * rows:(h + 1) * rows] * SCALE).astype(dq_ref.dtype)
+                    dq_ref[:, (head * PER + h) * DH:(head * PER + h + 1) * DH] = dq.T
+    else:
+        copy = pltpu.make_async_copy(dqt_ref, outs[0], sems.at[0])
+        copy.start()
+        copy.wait()
     for slot in range(2):
         for head in range(HALF):
-            out_copy(slot, head, ups[0]).wait()
-
-
-def gradients(prepared, top, total, gathered):
+            out_copy(zero_ref, slot, head, terms[0].at[0, :rows]).wait()
+
+
+def gradients(prepared, stats, offsets, blocks, carried, last):
     plan, qt, gt, gm, qm, delta = prepared[:6]
     chips = plan.shape[0] // 4
     rows = gm.shape[2] // PER
+    first = carried is None
     bf16, f32 = jnp.bfloat16, jnp.float32
-    blocks = [block for head in gathered for block in head]
-    shared = (qt, gt, gm, qm, delta, top, total)
-    dense = jax.ShapeDtypeStruct((chips, 2 * rows, 2 * DH), bf16)
+    shared = (qt, gt, gm, qm, delta, *stats)
+    arrays = [*shared, *blocks] + ([] if first else [carried])
+    dense = jax.ShapeDtypeStruct((len(offsets), 2 * rows, 2 * DH), bf16)
     piece = jax.ShapeDtypeStruct((rows, 2 * DH), bf16)
     query = jax.ShapeDtypeStruct((rows, HALF * WIDE), bf16)
+    sums = jax.ShapeDtypeStruct((HALF, 2, DH, PER * rows), f32)
+    out_shape, out_specs = [dense] * HALF, [HBM] * HALF
+    if first:
+        out_shape += [piece] * (2 * HALF) + [row_stats(rows)]
+        out_specs += [HBM] * (2 * HALF) + [VMEM]
+    out_shape += [query] * 2 if last else [sums]
+    out_specs += [VMEM] * 2 if last else [HBM]
     return pl.pallas_call(
-        functools.partial(grads_kernel, chips),
-        in_specs=[SMEM] + [HBM] * (len(shared) + len(blocks)),
-        out_specs=[HBM] * (3 * HALF) + [VMEM] * 2,
-        out_shape=[dense] * HALF + [piece] * (2 * HALF) + [query] * 2,
+        functools.partial(grads_kernel, chips, tuple(offsets), first, last),
+        in_specs=[SMEM] + [HBM] * len(arrays),
+        out_specs=out_specs,
+        out_shape=out_shape,
         scratch_shapes=[pltpu.VMEM(array.shape, array.dtype) for array in shared]
         + [
-            pltpu.VMEM((chips, HALF, 2 * rows, 2 * DH), bf16),
+            pltpu.VMEM((len(offsets), HALF, 2 * rows, 2 * DH), bf16),
             pltpu.VMEM((HALF, rows, 2 * DH), f32),
             pltpu.VMEM((2, HALF, rows, 2 * DH), bf16),
+            pltpu.VMEM((rows, 2 * DH), bf16),
             pltpu.VMEM((HALF, 2, DH, PER * rows), f32),
-            pltpu.SemaphoreType.DMA((2 * HALF + len(shared),)),
-            pltpu.SemaphoreType.DMA((chips, HALF)),
+            pltpu.SMEM((len(offsets),), jnp.int32),
+            pltpu.SemaphoreType.DMA((2 * HALF + 8,)),
+            pltpu.SemaphoreType.DMA((len(offsets), HALF)),
             pltpu.SemaphoreType.DMA((2, HALF)),
         ],
-        compiler_params=pltpu.CompilerParams(vmem_limit_bytes=(32 << 20) + (chips << 19)),
-        cost_estimate=pl.CostEstimate(flops=20 << 30, bytes_accessed=16 << 20, transcendentals=0),
-    )(plan, *shared, *blocks)
-
-
-def spread(block, right, left, chips):
-    far, rows = chips // 2, block.shape[0] // 2
-    got = {0: block}
-    up = down = block
-    for step in range(1, far):
-        up = got[chips - step] = lax.ppermute(up, "leaf", right)
-        down = got[step] = lax.ppermute(down, "leaf", left)
-    up = lax.ppermute(up[:rows], "leaf", right)
-    down = lax.ppermute(down[rows:], "leaf", left)
-    return [got[at] for at in range(chips) if at != far] + [up, down]
+        compiler_params=pltpu.CompilerParams(vmem_limit_bytes=(30 << 20) + (len(offsets) << 19)),
+        cost_estimate=pl.CostEstimate(flops=8 << 30, bytes_accessed=16 << 20, transcendentals=0),
+    )(plan, *arrays)
 
 
 def wide(x):
     return x.astype(jnp.float32)
-
-
-def collect(terms, up, down, right, left):
-    chips, rows = terms.shape[0], up.shape[0]
-    up = lax.ppermute(up, "leaf", right)
-    down = lax.ppermute(down, "leaf", left)
-    up = jnp.pad(wide(up), ((0, rows), (0, 0)))
-    down = jnp.pad(wide(down), ((rows, 0), (0, 0)))
-    for step in range(chips // 2 - 1, 0, -1):
-        up = wide(lax.ppermute((up + wide(terms[step])).astype(terms.dtype), "leaf", right))
-        down = wide(lax.ppermute((down + wide(terms[chips - step])).astype(terms.dtype), "leaf", left))
-    return (wide(terms[0]) + up + down).astype(terms.dtype)
 
 
 def local(queries, keys, values, saved_out, grad_out, parents, assignment, lengths):
@@ -396,26 +416,71 @@
 
     kept = heads_of(core)
     got = lax.ppermute(heads_of(1 - core), "leaf", swap)
-    gathered = []
+    own = []
     for head in range(HALF):
         cols = slice(head * 2 * DH, (head + 1) * 2 * DH)
-        block = jnp.concatenate([kept[:, cols], got[:, cols]], axis=0)
-        gathered.append(spread(block, right, left, chips))
+        own.append(jnp.concatenate([kept[:, cols], got[:, cols]], axis=0))
     mine = (queries, grad_out, saved_out)
     late = lax.optimization_barrier((*mine, got))[:3]
     other = jnp.concatenate([part(array, 1 - core, HALF * WIDE) for array in late], axis=1)
     other = lax.ppermute(other, "leaf", swap)
-    prepared = prepare(tables, mine, other, [blocks[0] for blocks in gathered])
-    plan, qt, top, total = prepared[0], prepared[1], prepared[6], prepared[7]
+
+    def shift(arrays, ring):
+        return [lax.ppermute(array, "leaf", ring) for array in arrays]
+
     far = chips // 2
+    blocks = {0: own}
+    ups, downs = own, own
+    prepared = stats = None
     for step in range(1, far):
-        arrived = [blocks[at] for at in (step, chips - step - 1) for blocks in gathered]
-        top, total = measure((step, chips - step), plan, qt, top, total, arrived)
-    *terms, ours, theirs = gradients(prepared, top, total, gathered)
-    theirs = lax.ppermute(theirs, "leaf", swap)
+        ups, downs = shift(ups, right), shift(downs, left)
+        blocks[chips - step], blocks[step] = ups, downs
+        if step == 1:
+            prepared = prepare(tables, mine, other, own)
+            stats = prepared[6:]
+        else:
+            seen = (step - 1, chips - step + 1)
+            stats = measure(seen, prepared[0], prepared[1], *stats, [b for at in seen for b in blocks[at]])
+        stats, held = lax.optimization_barrier((stats, (ups[1:], downs[1:])))
+        ups, downs = ups[:1] + held[0], downs[:1] + held[1]
+    halves = shift([a[:rows] for a in ups], right), shift([a[rows:] for a in downs], left)
+    seen = (far - 1, far + 1)
+    stats = measure(seen, prepared[0], prepared[1], *stats, [b for at in seen for b in blocks[at]])
+
+    offsets = [far]
+    for step in range(1, far - 1):
+        offsets += [far + step, far - step]
+    arrays = []
+    for head in range(HALF):
+        arrays += [halves[0][head], halves[1][head]] + [blocks[at][head] for at in offsets[1:]]
+    *terms, lse, carried = gradients(prepared, stats, offsets, arrays, None, False)
+    by_offset = {at: [terms[head][slot] for head in range(HALF)] for slot, at in enumerate(offsets)}
+    ups = [jnp.pad(wide(a), ((0, rows), (0, 0))) for a in shift(terms[HALF:2 * HALF], right)]
+    downs = [jnp.pad(wide(a), ((rows, 0), (0, 0))) for a in shift(terms[2 * HALF:], left)]
+
+    def add(sums, at):
+        return [(a + wide(b)).astype(jnp.bfloat16) for a, b in zip(sums, by_offset[at])]
+
+    later = {far - 1: [chips - 1, 1], max(far - 2, 1): [0]}
+    ours = theirs = None
+    for step in range(far - 1, 0, -1):
+        ups, downs = add(ups, step), add(downs, chips - step)
+        if step in later:
+            last = 0 in later[step]
+            (lse, carried), ups, downs = lax.optimization_barrier(((lse, carried), ups, downs))
+            arrays = [blocks[at][head] for head in range(HALF) for at in later[step]]
+            *terms, lead = gradients(prepared, (lse,), later[step], arrays, carried, last)
+            for slot, at in enumerate(later[step]):
+                by_offset[at] = [terms[head][slot] for head in range(HALF)]
+            if last:
+                ours, theirs = terms[HALF], lax.ppermute(lead, "leaf", swap)
+            else:
+                carried = lead
+        ups = [wide(a) for a in shift(ups, right)]
+        downs = [wide(a) for a in shift(downs, left)]
     kept, got = [], []
     for head in range(HALF):
-        summed = collect(*terms[head::HALF], right, left)
+        summed = (wide(by_offset[0][head]) + ups[head] + downs[head]).astype(jnp.bfloat16)
         kept.append(summed[:rows])
         got.append(lax.ppermute(summed[rows:], "leaf", swap))
 

time: 144 us -> 132 us (0.917)
  the two profiles are of different devices: /device:TPU:0 before, /device:TPU:3 now
where the time goes in v7:
time: 132 us; the launch traced here: 133 us
  starting transfers between devices  56.7 us (43%)
  Pallas kernels  41.7 us (32%)
  waiting for transfers between devices  26.5 us (20%)
  other arithmetic  5.69 us (4%)
  local copies, waits for them, and re-layouts  1.56 us (1%)
    ppermute x32, starting transfers between devices, shift(): return [lax.ppermute(array, 'leaf', ring) for array in arrays]  46.2 us
    pallas_call x3, Pallas kernels, gradients(): pl.pallas_call(functools.partial(grads_kernel, chips, tuple(offsets), fir...  26.8 us
    ppermute x32, waiting for transfers between devices, shift(): return [lax.ppermute(array, 'leaf', ring) for array in arrays]  25.4 us
    pallas_call x3, Pallas kernels, measure(): pl.pallas_call(functools.partial(measure_kernel, offsets), in_specs=[SMEM...  7.44 us
    pallas_call x1, Pallas kernels, prepare(): pl.pallas_call(prepare_kernel, in_specs=[SMEM] * 5 + [HBM] * (4 + HALF),...  7.41 us
    ppermute x1, starting transfers between devices, local(): ours, theirs = (terms[HALF], lax.ppermute(lead, 'leaf', swap))  7.23 us
  transfers between devices with their start and end apart: 37, of which 12 were waited for; matrix products, arithmetic and copies ran while one was open for 3% of the time, Pallas kernels for 23%

profile of v7, /device:TPU:3, one launch (start us, length us, event | category | flops | bytes accessed | tf_op | source)
XLA Modules:
  0.0 133.2 jit_solution(6921455835533142013)
XLA Ops:
  7.8 4.7 %collective-permute-done.4.refs_0_.refs_7_ = bf16[512,256]{1,0:T(8,128)(2,1)S(1)} collective-permute-done((bf16[512,256]{1,0:T(8,128)(2,1)S(1)}, bf16[512,256]{1,0:T(8,128)(2,1)S(1)}, u32[]{:S(2)}, u32[]{:S(2)}) %collective-permute-start.4) | collective-permute-done | bytes 262176 | tf_op jit(solution)/shard_map/ppermute | solution.py:429
  14.1 7.4 %shard_map.112 = (s32[32]{0:T(128)S(1)}, bf16[2,2,128,1280]{3,2,1,0:T(8,128)(2,1)S(1)}, bf16[2,2,128,1280]{3,2,1,0:T(8,128)(2,1)S(1)}, bf16[2,2,1280,128]{3,2,1,...) custom-call(s32[1]{0:T(128)} %bitcast.me_ref, ...), custom_call_target="tpu_custom_call" | custom-call | bytes 25165824 | tf_op jit(solution)/shard_map/pallas_call | solution.py:168
  25.3 3.2 %shard_map.113 = (f32[2,2,1,1280]{3,2,1,0:T(1,128)S(1)}, f32[2,2,1,1280]{3,2,1,0:T(1,128)S(1)}) custom-call(s32[32]{0:T(128)S(1)} %get-tuple-element.62.plan, bf16[2,2,128,1280]{3,2,1,0:T(8,128)(2,1)S(1)} %get-tuple-element.63.qt_in.refs_0_, f32[2,2,1,1280]{3,2,1,0:T(1,128)S(1)} %get-tuple-element.70.top_in, f32[2,2,1,1280]{3,2,1,0:T(1,128)S(1)} %get-tuple-element.71.sum_in, ...), custom_call_target="tpu_custom_call" | custom-call | bytes 12582912 | tf_op jit(solution)/shard_map/pallas_call | solution.py:202
  28.5 1.4 %collective-permute-done.6.refs_3_.refs_17_ = bf16[512,256]{1,0:T(8,128)(2,1)S(1)} collective-permute-done((bf16[512,256]{1,0:T(8,128)(2,1)S(1)}, bf16[512,256]{1,0:T(8,128)(2,1)S(1)}, u32[]{:S(2)}, u32[]{:S(2)}) %collective-permute-start.6) | collective-permute-done | bytes 262176 | tf_op jit(solution)/shard_map/ppermute | solution.py:429
  29.9 1.7 %collective-permute-start.11 = (bf16[512,256]{1,0:T(8,128)(2,1)S(1)}, bf16[512,256]{1,0:T(8,128)(2,1)S(1)}, u32[]{:S(2)}, u32[]{:S(2)}) collective-permute-start(bf16[512,256]{1,0:T(8,128)(2,1)S(1)} %collective-permute-done.7.refs_1_.refs_18_), channel_id=1, source_target_pairs={{4,0},{5,1},{8,4},{9,5},{12,8},{13,9},{14,12},{15,13},{10,14},{11,... | collective-permute-start | bytes 786440 | tf_op jit(solution)/shard_map/ppermute | solution.py:429
  31.7 3.9 %collective-permute-done.13.refs_2_.refs_9_ = bf16[512,256]{1,0:T(8,128)(2,1)S(1)} collective-permute-done((bf16[512,256]{1,0:T(8,128)(2,1)S(1)}, bf16[512,256]{1,0:T(8,128)(2,1)S(1)}, u32[]{:S(2)}, u32[]{:S(2)}) %collective-permute-start.13) | collective-permute-done | bytes 262176 | tf_op jit(solution)/shard_map/ppermute | solution.py:429
  35.7 1.8 %collective-permute-start.15 = (bf16[256,256]{1,0:T(8,128)(2,1)S(1)}, bf16[256,256]{1,0:T(8,128)(2,1)S(1)}, u32[]{:S(2)}, u32[]{:S(2)}) collective-permute-start(bf16[256,256]{1,0:T(8,128)(2,1)S(1)} %slice.125), channel_id=1, source_target_pairs={{4,0},{5,1},{8,4},{9,5},{12,8},{13,9},{14,12},{15,13},{10,14},{11,... | collective-permute-start | bytes 393224 | tf_op jit(solution)/shard_map/ppermute | solution.py:429
  37.4 3.2 %shard_map.114 = (f32[2,2,1,1280]{3,2,1,0:T(1,128)S(1)}, f32[2,2,1,1280]{3,2,1,0:T(1,128)S(1)}) custom-call(s32[32]{0:T(128)S(1)} %get-tuple-element.62.plan, bf16[2,2,128,1280]{3,2,1,0:T(8,128)(2,1)S(1)} %get-tuple-element.63.qt_in.refs_0_, f32[2,2,1,1280]{3,2,1,0:T(1,128)S(1)} %get-tuple-element.76.top_in, f32[2,2,1,1280]{3,2,1,0:T(1,128)S(1)} %get-tuple-element.77.sum_in, ...), custom_call_target="tpu_custom_call" | custom-call | bytes 12582912 | tf_op jit(solution)/shard_map/pallas_call | solution.py:202
  41.3 2.3 %collective-permute-start.17 = (bf16[256,256]{1,0:T(8,128)(2,1)S(1)}, bf16[256,256]{1,0:T(8,128)(2,1)S(1)}, u32[]{:S(2)}, u32[]{:S(2)}) collective-permute-start(bf16[256,256]{1,0:T(8,128)(2,1)S(1)} %slice.99), channel_id=1, source_target_pairs={{4,0},{5,1},{8,4},{9,5},{12,8},{13,9},{14,12},{15,13},{10,14},{11,... | collective-permute-start | bytes 393224 | tf_op jit(solution)/shard_map/ppermute | solution.py:429
  44.6 1.8 %collective-permute-done.16.refs_13_ = bf16[256,256]{1,0:T(8,128)(2,1)S(1)} collective-permute-done((bf16[256,256]{1,0:T(8,128)(2,1)S(1)}, bf16[256,256]{1,0:T(8,128)(2,1)S(1)}, u32[]{:S(2)}, u32[]{:S(2)}) %collective-permute-start.16) | collective-permute-done | bytes 131104 | tf_op jit(solution)/shard_map/ppermute | solution.py:429
  46.4 10.7 %shard_map.116 = (bf16[5,512,256]{2,1,0:T(8,128)(2,1)S(1)}, bf16[5,512,256]{2,1,0:T(8,128)(2,1)S(1)}, bf16[256,256]{1,0:T(8,128)(2,1)S(1)}, bf16[256,256]{1,0:T(...) custom-call(s32[32]{0:T(128)S(1)} %get-tuple-element.62.plan, ...), custom_call_target="tpu_custom_call" | custom-call | flops 8589934592 | bytes 16777216 | tf_op jit(solution)/shard_map/pallas_call | solution.py:370
  57.2 14.9 %collective-permute-start.21 = (bf16[256,256]{1,0:T(8,128)(2,1)S(1)}, bf16[256,256]{1,0:T(8,128)(2,1)S(1)}, u32[]{:S(2)}, u32[]{:S(2)}) collective-permute-start(bf16[256,256]{1,0:T(8,128)(2,1)S(1)} %get-tuple-element.95), channel_id=1, source_target_pairs={{4,0},{5,1},{8,4},{9,5},{12,8},{13,9},{14,12},{15,13},{10,14},{11,... | collective-permute-start | bytes 393224 | tf_op jit(solution)/shard_map/ppermute | solution.py:429
  72.1 6.4 %collective-permute-start.20 = (bf16[256,256]{1,0:T(8,128)(2,1)S(1)}, bf16[256,256]{1,0:T(8,128)(2,1)S(1)}, u32[]{:S(2)}, u32[]{:S(2)}) collective-permute-start(bf16[256,256]{1,0:T(8,128)(2,1)S(1)} %get-tuple-element.94), channel_id=1, source_target_pairs={{4,0},{5,1},{8,4},{9,5},{12,8},{13,9},{14,12},{15,13},{10,14},{11,... | collective-permute-start | bytes 393224 | tf_op jit(solution)/shard_map/ppermute | solution.py:429
  78.6 2.3 %collective-permute-done.18 = bf16[256,256]{1,0:T(8,128)(2,1)S(1)} collective-permute-done((bf16[256,256]{1,0:T(8,128)(2,1)S(1)}, bf16[256,256]{1,0:T(8,128)(2,1)S(1)}, u32[]{:S(2)}, u32[]{:S(2)}) %collective-permute-start.18) | collective-permute-done | bytes 131104 | tf_op jit(solution)/shard_map/ppermute | solution.py:429
  81.0 1.8 %collective-permute-start.25 = (bf16[512,256]{1,0:T(8,128)(2,1)S(1)}, bf16[512,256]{1,0:T(8,128)(2,1)S(1)}, u32[]{:S(2)}, u32[]{:S(2)}) collective-permute-start(bf16[512,256]{1,0:T(8,128)(2,1)S(1)} %get-tuple-element.102), channel_id=1, source_target_pairs={{4,0},{5,1},{8,4},{9,5},{12,8},{13,9},{14,12},{15,13},{10,14},{11,... | collective-permute-start | bytes 786440 | tf_op jit(solution)/shard_map/ppermute | solution.py:429
  84.3 7.3 %shard_map.117 = (bf16[2,512,256]{2,1,0:T(8,128)(2,1)S(1)}, bf16[2,512,256]{2,1,0:T(8,128)(2,1)S(1)}, f32[2,2,128,1280]{3,2,1,0:T(8,128)S(1)}) custom-call(s32[32]{0:T(128)S(1)} %get-tuple-element.62.plan, bf16[2,2,128,1280]{3,2,1,0:T(8,128)(2,1)S(1)} %get-tuple-element.63.qt_in.refs_0_, bf16[2,2,128,1280]{3,2,1,0:T(8,128)(2,1)S(1)} %get-tuple-element.64.refs_1_, ...), custom_call_target="tpu_custom_call" | custom-call | flops 8589934592 | bytes 16777216 | tf_op jit(solution)/shard_map/pallas_call | solution.py:370
  94.9 8.9 %shard_map.118 = (bf16[1,512,256]{2,1,0:T(8,128)(2,1)S(1)}, bf16[1,512,256]{2,1,0:T(8,128)(2,1)S(1)}, bf16[256,1280]{1,0:T(8,128)(2,1)S(1)}, bf16[256,1280]{1,0:T(8,128)(2,1)S(1)}) custom-call(s32[32]{0:T(128)S(1)} %get-tuple-element.62.plan, bf16[2,2,128,1280]{3,2,1,0:T(8,128)(2,1)S(1)} %get-tuple-element.63.qt_in.refs_0_, ...), custom_call_target="tpu_custom_call" | custom-call | flops 8589934592 | bytes 16777216 | tf_op jit(solution)/shard_map/pallas_call | solution.py:370
  103.8 7.2 %collective-permute-start.26 = (bf16[256,1280]{1,0:T(8,128)(2,1)S(1)}, bf16[256,1280]{1,0:T(8,128)(2,1)S(1)}, u32[]{:S(2)}, u32[]{:S(2)}) collective-permute-start(bf16[256,1280]{1,0:T(8,128)(2,1)S(1)} %get-tuple-element.106), channel_id=1, source_target_pairs={{0,1},{1,0},{2,3},{3,2},{4,5},{5,4},{6,7},{7,6},{8,9},{9,8},{10,11... | collective-permute-start | bytes 1966088 | tf_op jit(solution)/shard_map/ppermute | solution.py:476
  111.2 3.3 %collective-permute-start.28 = (bf16[512,256]{1,0:T(8,128)(2,1)S(1)}, bf16[512,256]{1,0:T(8,128)(2,1)S(1)}, u32[]{:S(2)}, u32[]{:S(2)}) collective-permute-start(bf16[512,256]{1,0:T(8,128)(2,1)S(1)} %get-tuple-element.125), channel_id=1, source_target_pairs={{0,4},{1,5},{4,8},{5,9},{8,12},{9,13},{12,14},{13,15},{14,10},{15,... | collective-permute-start | bytes 786440 | tf_op jit(solution)/shard_map/ppermute | solution.py:429
  115.4 1.7 %collective-permute-start.33 = (bf16[512,256]{1,0:T(8,128)(2,1)}, bf16[512,256]{1,0:T(8,128)(2,1)}, u32[]{:S(2)}, u32[]{:S(2)}) collective-permute-start(bf16[512,256]{1,0:T(8,128)(2,1)} %get-tuple-element.127), channel_id=1, source_target_pairs={{0,4},{1,5},{4,8},{5,9},{8,12},{9,13},{12,14},{13,15},{14,10},{15,... | collective-permute-start | bytes 786440 | tf_op jit(solution)/shard_map/ppermute | solution.py:429
  117.2 3.0 %collective-permute-done.28 = bf16[512,256]{1,0:T(8,128)(2,1)S(1)} collective-permute-done((bf16[512,256]{1,0:T(8,128)(2,1)S(1)}, bf16[512,256]{1,0:T(8,128)(2,1)S(1)}, u32[]{:S(2)}, u32[]{:S(2)}) %collective-permute-start.28) | collective-permute-done | bytes 262176 | tf_op jit(solution)/shard_map/ppermute | solution.py:429
  120.2 2.6 %collective-permute-done.30 = bf16[512,256]{1,0:T(8,128)(2,1)S(1)} collective-permute-done((bf16[512,256]{1,0:T(8,128)(2,1)S(1)}, bf16[512,256]{1,0:T(8,128)(2,1)S(1)}, u32[]{:S(2)}, u32[]{:S(2)}) %collective-permute-start.30) | collective-permute-done | bytes 262176 | tf_op jit(solution)/shard_map/ppermute | solution.py:429
  124.1 1.8 %collective-permute-done.33 = bf16[512,256]{1,0:T(8,128)(2,1)} collective-permute-done((bf16[512,256]{1,0:T(8,128)(2,1)}, bf16[512,256]{1,0:T(8,128)(2,1)}, u32[]{:S(2)}, u32[]{:S(2)}) %collective-permute-start.33) | collective-permute-done | bytes 262176 | tf_op jit(solution)/shard_map/ppermute | solution.py:429
  125.9 2.5 %collective-permute-done.35 = bf16[512,256]{1,0:T(8,128)(2,1)} collective-permute-done((bf16[512,256]{1,0:T(8,128)(2,1)}, bf16[512,256]{1,0:T(8,128)(2,1)}, u32[]{:S(2)}, u32[]{:S(2)}) %collective-permute-start.35) | collective-permute-done | bytes 262176 | tf_op jit(solution)/shard_map/ppermute | solution.py:429
  (100 shorter events, 26.2 us)
Async XLA Ops:
  4.3 9.8 %collective-permute-start.1 = (bf16[256,3840]{1,0:T(8,128)(2,1)S(1)}, bf16[256,3840]{1,0:T(8,128)(2,1)S(1)}, u32[]{:S(2)}, u32[]{:S(2)}) collective-permute-start(bf16[256,3840]{1,0:T(8,128)(2,1)S(1)} %pad_maximum_fusion), channel_id=1, source_target_pairs={{0,1},{1,0},{2,3},{3,2},{4,5},{5,4},{6,7},{7,6},{8,9},{9,8},{10,11... | collective-permute-start | bytes 5898248 | tf_op jit(solution)/shard_map/ppermute | solution.py:426
  6.3 15.2 %collective-permute-start.2 = (bf16[512,256]{1,0:T(8,128)(2,1)S(1)}, bf16[512,256]{1,0:T(8,128)(2,1)S(1)}, u32[]{:S(2)}, u32[]{:S(2)}) collective-permute-start(bf16[512,256]{1,0:T(8,128)(2,1)S(1)} %pad_maximum_fusion.4.refs_1_.refs_7_), channel_id=1, source_target_pairs={{0,4},{1,5},{4,8},{5,9},{8,12},{9,13},{12,14},{13,15},{14,10},{15,... | collective-permute-start | bytes 786440 | tf_op jit(solution)/shard_map/ppermute | solution.py:429
  7.7 13.8 %collective-permute-start.3 = (bf16[512,256]{1,0:T(8,128)(2,1)S(1)}, bf16[512,256]{1,0:T(8,128)(2,1)S(1)}, u32[]{:S(2)}, u32[]{:S(2)}) collective-permute-start(bf16[512,256]{1,0:T(8,128)(2,1)S(1)} %pad_maximum_fusion.4.refs_1_.refs_7_), channel_id=1, source_target_pairs={{4,0},{5,1},{8,4},{9,5},{12,8},{13,9},{14,12},{15,13},{10,14},{11,... | collective-permute-start | bytes 786440 | tf_op jit(solution)/shard_map/ppermute | solution.py:429
  12.6 11.2 %collective-permute-start.8 = (bf16[512,256]{1,0:T(8,128)(2,1)S(1)}, bf16[512,256]{1,0:T(8,128)(2,1)S(1)}, u32[]{:S(2)}, u32[]{:S(2)}) collective-permute-start(bf16[512,256]{1,0:T(8,128)(2,1)S(1)} %collective-permute-done.4.refs_0_.refs_7_), channel_id=1, source_target_pairs={{4,0},{5,1},{8,4},{9,5},{12,8},{13,9},{14,12},{15,13},{10,14},{11,... | collective-permute-start | bytes 786440 | tf_op jit(solution)/shard_map/ppermute | solution.py:429
  13.8 11.2 %collective-permute-start.9 = (bf16[512,256]{1,0:T(8,128)(2,1)S(1)}, bf16[512,256]{1,0:T(8,128)(2,1)S(1)}, u32[]{:S(2)}, u32[]{:S(2)}) collective-permute-start(bf16[512,256]{1,0:T(8,128)(2,1)S(1)} %collective-permute-done.5.refs_2_.refs_6_), channel_id=1, source_target_pairs={{0,4},{1,5},{4,8},{5,9},{8,12},{9,13},{12,14},{13,15},{14,10},{15,... | collective-permute-start | bytes 786440 | tf_op jit(solution)/shard_map/ppermute | solution.py:429
  23.8 11.8 %collective-permute-start.12 = (bf16[512,256]{1,0:T(8,128)(2,1)S(1)}, bf16[512,256]{1,0:T(8,128)(2,1)S(1)}, u32[]{:S(2)}, u32[]{:S(2)}) collective-permute-start(bf16[512,256]{1,0:T(8,128)(2,1)S(1)} %collective-permute-done.8.refs_0_.refs_12_), channel_id=1, source_target_pairs={{4,0},{5,1},{8,4},{9,5},{12,8},{13,9},{14,12},{15,13},{10,14},{11,... | collective-permute-start | bytes 786440 | tf_op jit(solution)/shard_map/ppermute | solution.py:429
  25.1 10.5 %collective-permute-start.13 = (bf16[512,256]{1,0:T(8,128)(2,1)S(1)}, bf16[512,256]{1,0:T(8,128)(2,1)S(1)}, u32[]{:S(2)}, u32[]{:S(2)}) collective-permute-start(bf16[512,256]{1,0:T(8,128)(2,1)S(1)} %collective-permute-done.9.refs_2_.refs_11_), channel_id=1, source_target_pairs={{0,4},{1,5},{4,8},{5,9},{8,12},{9,13},{12,14},{13,15},{14,10},{15,... | collective-permute-start | bytes 786440 | tf_op jit(solution)/shard_map/ppermute | solution.py:429
  29.9 11.2 %collective-permute-start.10 = (bf16[512,256]{1,0:T(8,128)(2,1)S(1)}, bf16[512,256]{1,0:T(8,128)(2,1)S(1)}, u32[]{:S(2)}, u32[]{:S(2)}) collective-permute-start(bf16[512,256]{1,0:T(8,128)(2,1)S(1)} %collective-permute-done.6.refs_3_.refs_17_), channel_id=1, source_target_pairs={{0,4},{1,5},{4,8},{5,9},{8,12},{9,13},{12,14},{13,15},{14,10},{15,... | collective-permute-start | bytes 786440 | tf_op jit(solution)/shard_map/ppermute | solution.py:429
  29.9 11.2 %collective-permute-start.11 = (bf16[512,256]{1,0:T(8,128)(2,1)S(1)}, bf16[512,256]{1,0:T(8,128)(2,1)S(1)}, u32[]{:S(2)}, u32[]{:S(2)}) collective-permute-start(bf16[512,256]{1,0:T(8,128)(2,1)S(1)} %collective-permute-done.7.refs_1_.refs_18_), channel_id=1, source_target_pairs={{4,0},{5,1},{8,4},{9,5},{12,8},{13,9},{14,12},{15,13},{10,14},{11,... | collective-permute-start | bytes 786440 | tf_op jit(solution)/shard_map/ppermute | solution.py:429
  35.6 9.0 %collective-permute-start.14 = (bf16[256,256]{1,0:T(8,128)(2,1)S(1)}, bf16[256,256]{1,0:T(8,128)(2,1)S(1)}, u32[]{:S(2)}, u32[]{:S(2)}) collective-permute-start(bf16[256,256]{1,0:T(8,128)(2,1)S(1)} %slice.124), channel_id=1, source_target_pairs={{0,4},{1,5},{4,8},{5,9},{8,12},{9,13},{12,14},{13,15},{14,10},{15,... | collective-permute-start | bytes 393224 | tf_op jit(solution)/shard_map/ppermute | solution.py:429
  35.7 8.9 %collective-permute-start.15 = (bf16[256,256]{1,0:T(8,128)(2,1)S(1)}, bf16[256,256]{1,0:T(8,128)(2,1)S(1)}, u32[]{:S(2)}, u32[]{:S(2)}) collective-permute-start(bf16[256,256]{1,0:T(8,128)(2,1)S(1)} %slice.125), channel_id=1, source_target_pairs={{4,0},{5,1},{8,4},{9,5},{12,8},{13,9},{14,12},{15,13},{10,14},{11,... | collective-permute-start | bytes 393224 | tf_op jit(solution)/shard_map/ppermute | solution.py:429
  57.1 21.4 %collective-permute-start.19 = (bf16[256,256]{1,0:T(8,128)(2,1)S(1)}, bf16[256,256]{1,0:T(8,128)(2,1)S(1)}, u32[]{:S(2)}, u32[]{:S(2)}) collective-permute-start(bf16[256,256]{1,0:T(8,128)(2,1)S(1)} %get-tuple-element.92), channel_id=1, source_target_pairs={{0,4},{1,5},{4,8},{5,9},{8,12},{9,13},{12,14},{13,15},{14,10},{15,... | collective-permute-start | bytes 393224 | tf_op jit(solution)/shard_map/ppermute | solution.py:429
  57.2 21.4 %collective-permute-start.21 = (bf16[256,256]{1,0:T(8,128)(2,1)S(1)}, bf16[256,256]{1,0:T(8,128)(2,1)S(1)}, u32[]{:S(2)}, u32[]{:S(2)}) collective-permute-start(bf16[256,256]{1,0:T(8,128)(2,1)S(1)} %get-tuple-element.95), channel_id=1, source_target_pairs={{4,0},{5,1},{8,4},{9,5},{12,8},{13,9},{14,12},{15,13},{10,14},{11,... | collective-permute-start | bytes 393224 | tf_op jit(solution)/shard_map/ppermute | solution.py:429
  81.0 10.6 %collective-permute-start.23 = (bf16[512,256]{1,0:T(8,128)(2,1)S(1)}, bf16[512,256]{1,0:T(8,128)(2,1)S(1)}, u32[]{:S(2)}, u32[]{:S(2)}) collective-permute-start(bf16[512,256]{1,0:T(8,128)(2,1)S(1)} %get-tuple-element.100), channel_id=1, source_target_pairs={{0,4},{1,5},{4,8},{5,9},{8,12},{9,13},{12,14},{13,15},{14,10},{15,... | collective-permute-start | bytes 786440 | tf_op jit(solution)/shard_map/ppermute | solution.py:429
  81.0 10.6 %collective-permute-start.25 = (bf16[512,256]{1,0:T(8,128)(2,1)S(1)}, bf16[512,256]{1,0:T(8,128)(2,1)S(1)}, u32[]{:S(2)}, u32[]{:S(2)}) collective-permute-start(bf16[512,256]{1,0:T(8,128)(2,1)S(1)} %get-tuple-element.102), channel_id=1, source_target_pairs={{4,0},{5,1},{8,4},{9,5},{12,8},{13,9},{14,12},{15,13},{10,14},{11,... | collective-permute-start | bytes 786440 | tf_op jit(solution)/shard_map/ppermute | solution.py:429
  82.8 8.9 %collective-permute-start.22 = (bf16[512,256]{1,0:T(8,128)(2,1)S(1)}, bf16[512,256]{1,0:T(8,128)(2,1)S(1)}, u32[]{:S(2)}, u32[]{:S(2)}) collective-permute-start(bf16[512,256]{1,0:T(8,128)(2,1)S(1)} %get-tuple-element.99), channel_id=1, source_target_pairs={{0,4},{1,5},{4,8},{5,9},{8,12},{9,13},{12,14},{13,15},{14,10},{15,... | collective-permute-start | bytes 786440 | tf_op jit(solution)/shard_map/ppermute | solution.py:429
  91.9 19.1 %collective-permute-start.27 = (bf16[512,256]{1,0:T(8,128)(2,1)S(1)}, bf16[512,256]{1,0:T(8,128)(2,1)S(1)}, u32[]{:S(2)}, u32[]{:S(2)}) collective-permute-start(bf16[512,256]{1,0:T(8,128)(2,1)S(1)} %get-tuple-element.108), channel_id=1, source_target_pairs={{0,4},{1,5},{4,8},{5,9},{8,12},{9,13},{12,14},{13,15},{14,10},{15,... | collective-permute-start | bytes 786440 | tf_op jit(solution)/shard_map/ppermute | solution.py:429
  92.9 18.1 %collective-permute-start.29 = (bf16[512,256]{1,0:T(8,128)(2,1)S(1)}, bf16[512,256]{1,0:T(8,128)(2,1)S(1)}, u32[]{:S(2)}, u32[]{:S(2)}) collective-permute-start(bf16[512,256]{1,0:T(8,128)(2,1)S(1)} %get-tuple-element.110), channel_id=1, source_target_pairs={{4,0},{5,1},{8,4},{9,5},{12,8},{13,9},{14,12},{15,13},{10,14},{11,... | collective-permute-start | bytes 786440 | tf_op jit(solution)/shard_map/ppermute | solution.py:429
  93.4 21.1 %collective-permute-start.32 = (bf16[512,256]{1,0:T(8,128)(2,1)S(1)}, bf16[512,256]{1,0:T(8,128)(2,1)S(1)}, u32[]{:S(2)}, u32[]{:S(2)}) collective-permute-start(bf16[512,256]{1,0:T(8,128)(2,1)S(1)} %get-tuple-element.112), channel_id=1, source_target_pairs={{0,4},{1,5},{4,8},{5,9},{8,12},{9,13},{12,14},{13,15},{14,10},{15,... | collective-permute-start | bytes 786440 | tf_op jit(solution)/shard_map/ppermute | solution.py:429
  94.4 20.1 %collective-permute-start.34 = (bf16[512,256]{1,0:T(8,128)(2,1)S(1)}, bf16[512,256]{1,0:T(8,128)(2,1)S(1)}, u32[]{:S(2)}, u32[]{:S(2)}) collective-permute-start(bf16[512,256]{1,0:T(8,128)(2,1)S(1)} %get-tuple-element.114), channel_id=1, source_target_pairs={{4,0},{5,1},{8,4},{9,5},{12,8},{13,9},{14,12},{15,13},{10,14},{11,... | collective-permute-start | bytes 786440 | tf_op jit(solution)/shard_map/ppermute | solution.py:429
  103.8 26.7 %collective-permute-start.26 = (bf16[256,1280]{1,0:T(8,128)(2,1)S(1)}, bf16[256,1280]{1,0:T(8,128)(2,1)S(1)}, u32[]{:S(2)}, u32[]{:S(2)}) collective-permute-start(bf16[256,1280]{1,0:T(8,128)(2,1)S(1)} %get-tuple-element.106), channel_id=1, source_target_pairs={{0,1},{1,0},{2,3},{3,2},{4,5},{5,4},{6,7},{7,6},{8,9},{9,8},{10,11... | collective-permute-start | bytes 1966088 | tf_op jit(solution)/shard_map/ppermute | solution.py:476
  111.2 9.0 %collective-permute-start.28 = (bf16[512,256]{1,0:T(8,128)(2,1)S(1)}, bf16[512,256]{1,0:T(8,128)(2,1)S(1)}, u32[]{:S(2)}, u32[]{:S(2)}) collective-permute-start(bf16[512,256]{1,0:T(8,128)(2,1)S(1)} %get-tuple-element.125), channel_id=1, source_target_pairs={{0,4},{1,5},{4,8},{5,9},{8,12},{9,13},{12,14},{13,15},{14,10},{15,... | collective-permute-start | bytes 786440 | tf_op jit(solution)/shard_map/ppermute | solution.py:429
  115.4 10.5 %collective-permute-start.33 = (bf16[512,256]{1,0:T(8,128)(2,1)}, bf16[512,256]{1,0:T(8,128)(2,1)}, u32[]{:S(2)}, u32[]{:S(2)}) collective-permute-start(bf16[512,256]{1,0:T(8,128)(2,1)} %get-tuple-element.127), channel_id=1, source_target_pairs={{0,4},{1,5},{4,8},{5,9},{8,12},{9,13},{12,14},{13,15},{14,10},{15,... | collective-permute-start | bytes 786440 | tf_op jit(solution)/shard_map/ppermute | solution.py:429
  117.2 11.2 %collective-permute-start.35 = (bf16[512,256]{1,0:T(8,128)(2,1)}, bf16[512,256]{1,0:T(8,128)(2,1)}, u32[]{:S(2)}, u32[]{:S(2)}) collective-permute-start(bf16[512,256]{1,0:T(8,128)(2,1)} %get-tuple-element.128), channel_id=1, source_target_pairs={{4,0},{5,1},{8,4},{9,5},{12,8},{13,9},{14,12},{15,13},{10,14},{11,... | collective-permute-start | bytes 786440 | tf_op jit(solution)/shard_map/ppermute | solution.py:429
  (20 other events, 135.3 us)
